TPU v7x, 32 devices: a whole 2x2x4 slice. The times are simulated.
32 devices in a mesh: row: 8 (over z, x), col: 4 (over y, core).
Axes of the slice: x: 2, y: 2, z: 4, core: 2. Of those that a mesh axis runs over, the one named last changes fastest.
Arguments:
- iterate: float32 [8, 163840], P(None, ('row', 'col')), may hold values from -6 to 6
- residual: float32 [8, 163840], P(None, ('row', 'col')), may hold values from -6 to 6
- stored_tiles: float32 [8, 4, 640, 64, 64], P('row', 'col'), may hold values from -0.3125 to 0.3125
- block_rows: int32 [8, 4, 640], P('row', 'col'), may hold values from 0 to 319
- block_cols: int32 [8, 4, 640], P('row', 'col'), may hold values from 0 to 639
- live_counts: int32 [8, 4], P('row', 'col'), may hold values from 1 to 640, as said below
Outputs:
- h_iterate: float32 [8, 163840], P(None, ('row', 'col'))
- h_residual: float32 [8, 163840], P(None, ('row', 'col'))
Inputs may be any that keep to these rules, and one draw needn't show every extreme that they name: Only the first live_counts slots of a device hold stored tiles; the others are not part of the matrix. Some device fills all 640 slots.
All inputs are finite; a program needn't handle non-finite values.
Results may differ from a plain program's by a relative error of at most 0.0003.
Values sent between devices are 32-bit elements; how exact they have to be, the bound alone decides.
No kernel may reach another device: no remote copies, remote signals or barrier semaphores. Data moves between devices by JAX's collectives and lax.ppermute only.
A program may use at most 192 MiB of HBM per device.

v0:
```python
import jax
import jax.numpy as jnp
from jax import lax
from jax.sharding import PartitionSpec as P

BLK = 64


def tile_products(
    tile_set, rows_idx, cols_idx, live_mask, near_rows, near_cols, row_total, col_total
):
    cols_taken = jnp.take(near_cols, cols_idx, axis=1)
    forward = jnp.einsum("sab,vsb->vsa", tile_set, cols_taken, precision=lax.Precision.HIGHEST)
    forward = forward * live_mask[None, :, None]
    row_total = row_total.at[:, rows_idx, :].add(forward)
    rows_taken = jnp.take(near_rows, rows_idx, axis=1)
    mirrored = jnp.einsum("sab,vsa->vsb", tile_set, rows_taken, precision=lax.Precision.HIGHEST)
    mirrored = mirrored * live_mask[None, :, None]
    col_total = col_total.at[:, cols_idx, :].add(mirrored)
    return (row_total, col_total)


def local_terms(tile_set, rows_idx, cols_idx, live_count, near_rows, near_cols):
    slot_count = tile_set.shape[0]
    row_zero = jnp.zeros(near_rows.shape, jnp.float32)
    col_zero = jnp.zeros(near_cols.shape, jnp.float32)
    live_mask = (jnp.arange(slot_count, dtype=jnp.int32) < live_count).astype(jnp.float32)
    return tile_products(
        tile_set, rows_idx, cols_idx, live_mask, near_rows, near_cols, row_zero, col_zero
    )


def apply_blocks(vectors, tile_set, rows_idx, cols_idx, live_count):
    vec_count = vectors.shape[0]
    near_rows = lax.all_gather(vectors, "col", axis=1, tiled=True)
    near_cols = lax.all_gather(vectors, "row", axis=1, tiled=True)
    near_rows = near_rows.reshape(vec_count, -1, BLK)
    near_cols = near_cols.reshape(vec_count, -1, BLK)
    row_part, col_part = local_terms(tile_set, rows_idx, cols_idx, live_count, near_rows, near_cols)
    row_part = row_part.reshape(vec_count, -1)
    col_part = col_part.reshape(vec_count, -1)
    row_result = lax.psum_scatter(row_part, "col", scatter_dimension=1, tiled=True)
    col_result = lax.psum_scatter(col_part, "row", scatter_dimension=1, tiled=True)
    return row_result + col_result


def body(iterate, residual, stored_tiles, block_rows, block_cols, live_counts):
    tile_set = stored_tiles[0, 0]
    rows_idx = block_rows[0, 0]
    cols_idx = block_cols[0, 0]
    live_count = live_counts[0, 0]
    stacked = jnp.concatenate([iterate, residual], axis=0)
    combined = apply_blocks(stacked, tile_set, rows_idx, cols_idx, live_count)
    vec_count = iterate.shape[0]
    h_iterate = combined[:vec_count]
    h_residual = combined[vec_count:]
    return (h_iterate, h_residual)


def solution(mesh):
    in_specs = (
        P(None, ("row", "col")),
        P(None, ("row", "col")),
        P("row", "col", None, None, None),
        P("row", "col", None),
        P("row", "col", None),
        P("row", "col"),
    )
    out_specs = (P(None, ("row", "col")), P(None, ("row", "col")))
    return jax.shard_map(body, mesh=mesh, in_specs=in_specs, out_specs=out_specs, check_vma=False)
```

profile of v0, /device:TPU:0, one launch (start us, length us, event | category | flops | bytes accessed | tf_op | source)
XLA Modules:
  0.0 384.7 jit_solution(3841185723743917656)
XLA Ops:
  7.2 0.9 constant_dynamic-update-slice_fusion.1
  8.1 0.9 constant_dynamic-update-slice_fusion
  9.1 0.7 copy-done
  9.9 0.7 all-gather.5.cloned.1.call-update
  11.3 19.8 %copy.11 = f32[640,64,64]{2,1,0:T(8,128)} copy(f32[640,64,64]{0,2,1:T(8,128)} %bitcast.19) | data formatting | bytes 20971520 | tf_op jit(solution)/shard_map/squeeze | solution.py:48
  31.3 36.3 %all-gather.3.cloned.1.call-done = f32[16,40960]{1,0:T(8,128)} async-done(((f32[16,5120]{1,0:T(8,128)}), f32[16,40960]{1,0:T(8,128)}) %all-gather.3.cloned.1.call-update) | async-done | bytes 2621456 | tf_op jit(solution)/shard_map/all_gather | solution.py:36
  67.6 5.0 %reshape.89 = f32[16,640,64]{2,1,0:T(8,128)} reshape(f32[16,40960]{1,0:T(8,128)} %all-gather.3.cloned.1.call-done) | data formatting | bytes 5242880 | tf_op jit(solution)/shard_map/reshape | solution.py:38
  72.5 8.1 %copy.10 = f32[16,640,64]{2,0,1:T(8,128)} copy(f32[16,640,64]{2,1,0:T(8,128)} %reshape.89) | data formatting | bytes 5242880 | tf_op jit(solution)/shard_map/reshape | solution.py:38
  80.7 5.9 %gather_fusion = f32[640,16,64]{2,1,0:T(8,128)} fusion(f32[16,640,64]{2,0,1:T(8,128)} %copy.10, s32[1024]{0:T(1024)S(1)} %pad_clamp_fusion.1), kind=kCustom, calls=%fused_computation | custom fusion | bytes 5245440 | tf_op jit(solution)/shard_map/jit(_take)/gather | solution.py:12
  86.6 37.1 %broadcast_multiply_fusion.1 = f32[640,16,64]{2,1,0:T(8,128)} fusion(f32[640]{0:T(1024)S(1)} %get-tuple-element.4, f32[640,64,64]{2,1,0:T(8,128)} %copy.11, f32[640,16,64]{2,1,0:T(8,128)} %gather_fusion, pred[640]{0:T(1024)(128)(4,1)S(1)} %get-tuple-element.5), kind=kOutput, calls=%fused_computation.13 | convolution fusion | flops 504627200 | bytes 15731840 | tf_op jit(solution)/shard_map/sab,vsb->vsa/dot_general | solution.py:13
  123.9 50.5 %scatter_fusion = f32[16,320,64]{2,0,1:T(8,128)S(1)} fusion(f32[16,320,64]{2,0,1:T(8,128)S(1)} %broadcast_in_dim.28, s32[640]{0:T(1024)S(1)} %fusion.15, f32[640,16,64]{2,1,0:T(8,128)} %broadcast_multiply_fusion.1), kind=kCustom, calls=%fused_computation.2 | custom fusion | flops 655360 | bytes 7866880 | tf_op jit(solution)/shard_map/scatter-add | solution.py:15
  174.4 2.3 copy.12
  176.7 3.6 reshape.90
  180.5 3.9 %reshape.91 = f32[16,320,64]{2,1,0:T(8,128)} reshape(f32[16,20480]{1,0:T(8,128)} %all-gather.5.cloned.1.call-done) | data formatting | bytes 2621440 | tf_op jit(solution)/shard_map/reshape | solution.py:37
  184.4 3.3 copy.13
  187.7 3.8 gather_fusion.1
  191.5 23.4 %broadcast_multiply_fusion = f32[640,16,64]{2,1,0:T(8,128)} fusion(f32[640]{0:T(1024)S(1)} %get-tuple-element.4, f32[640,64,64]{2,1,0:T(8,128)} %copy.11, f32[640,16,64]{2,1,0:T(8,128)} %gather_fusion.1, pred[640]{0:T(1024)(128)(4,1)S(1)} %compare_and_fusion), kind=kOutput, calls=%fused_computation.12 | convolution fusion | flops 504627200 | bytes 15731840 | tf_op jit(solution)/shard_map/sab,vsa->vsb/dot_general | solution.py:17
  214.9 2.7 broadcast_in_dim.31
  217.5 78.6 %scatter_fusion.1 = f32[16,640,64]{2,0,1:T(8,128)} fusion(f32[16,640,64]{2,0,1:T(8,128)} %broadcast_in_dim.31, s32[640]{0:T(1024)S(1)} %fusion.16, f32[640,16,64]{2,1,0:T(8,128)} %broadcast_multiply_fusion), kind=kCustom, calls=%fused_computation.3 | custom fusion | flops 655360 | bytes 7866880 | tf_op jit(solution)/shard_map/scatter-add | solution.py:19
  296.1 6.5 %copy.15 = f32[16,640,64]{2,1,0:T(8,128)} copy(f32[16,640,64]{2,0,1:T(8,128)} %scatter_fusion.1) | data formatting | bytes 5242880 | tf_op jit(solution)/shard_map/scatter-add | solution.py:19
  302.7 4.4 %reshape.92 = f32[16,40960]{1,0:T(8,128)} reshape(f32[16,640,64]{2,1,0:T(8,128)} %copy.15) | data formatting | bytes 5242880 | tf_op jit(solution)/shard_map/reshape | solution.py:41
  307.1 69.2 %reduce-scatter.5.cloned.1.call-done = f32[16,5120]{1,0:T(8,128)} async-done(((f32[16,40960]{1,0:T(8,128)}), f32[16,5120]{1,0:T(8,128)}) %reduce-scatter.5.cloned.1.call-update) | async-done | bytes 327696 | tf_op jit(solution)/shard_map/reduce_scatter | solution.py:43
  376.3 1.1 add.65
  377.4 0.7 fusion.19
  (23 shorter events, 0.5 us)
Async XLA Ops:
  7.2 60.4 %all-gather.3.cloned.1.call-start = ((), (), s32[]{:S(2)}) async-start(), calls=%async_computation.2 | async-start | bytes 2949120 | tf_op jit(solution)/shard_map/all_gather | solution.py:36
  9.1 0.7 copy-start
  9.8 170.6 %all-gather.5.cloned.1.call-start = ((), (), s32[]{:S(2)}) async-start(), calls=%async_computation.4 | async-start | bytes 1638400 | tf_op jit(solution)/shard_map/all_gather | solution.py:35
  10.6 296.6 %reduce-scatter.3.cloned.1.call-start = ((), (), s32[]{:S(2)}) async-start(), calls=%async_computation.3 | async-start | bytes 1638400 | tf_op jit(solution)/shard_map/reduce_scatter | solution.py:42
  11.3 19.9 %copy-start.1 = (s32[1,1,640]{2,1,0:T(1,128)S(1)}, s32[1,1,640]{2,1,0:T(1,128)}, u32[]{:S(2)}) copy-start(s32[1,1,640]{2,1,0:T(1,128)} %param.10) | copy-start | bytes 7684
  11.3 19.9 %copy-start.2 = (s32[1,1,640]{2,1,0:T(1,128)S(1)}, s32[1,1,640]{2,1,0:T(1,128)}, u32[]{:S(2)}) copy-start(s32[1,1,640]{2,1,0:T(1,128)} %param.9) | copy-start | bytes 7684
  180.3 196.0 %reduce-scatter.5.cloned.1.call-start = ((), (), s32[]{:S(2)}) async-start(), calls=%async_computation.5 | async-start | bytes 2949120 | tf_op jit(solution)/shard_map/reduce_scatter | solution.py:43
Sparse Core Ops, SparseCore 0:
  10.2 57.3 all-gather.2
  69.1 16.7 all-gather.4
  180.5 24.9 reduce-scatter.2
  307.2 69.0 reduce-scatter.4
where the time goes:
time: 387 us; the launch traced here: 385 us
  other arithmetic  130 us (34%)
  waiting for transfers between devices  106 us (27%)
  local copies, waits for them, and re-layouts  72.9 us (19%)
  matrix products  60.5 us (16%)
  between operations  14.5 us (4%)
    scatter-add x1, other arithmetic, tile_products(): col_total = col_total.at[:, cols_idx, :].add(mirrored)  78.6 us
    reduce_scatter x1, waiting for transfers between devices, apply_blocks(): lax.psum_scatter(col_part, 'row', scatter_dimension=1, tiled=True)  69.2 us
    scatter-add x1, other arithmetic, tile_products(): row_total = row_total.at[:, rows_idx, :].add(forward)  50.5 us
    dot_general x1, matrix products, tile_products(): jnp.einsum('sab,vsb->vsa', tile_set, cols_taken, precision=lax.Precision....  37.1 us
    all_gather x1, waiting for transfers between devices, apply_blocks(): near_cols = lax.all_gather(vectors, 'row', axis=1, tiled=True)  36.3 us
    dot_general x1, matrix products, tile_products(): jnp.einsum('sab,vsa->vsb', tile_set, rows_taken, precision=lax.Precision....  23.4 us
    squeeze x1, local copies, waits for them, and re-layouts, body(): tile_set = stored_tiles[0, 0]  19.8 us
    reshape x2, local copies, waits for them, and re-layouts, apply_blocks(): near_cols = near_cols.reshape(vec_count, -1, BLK)  13.1 us
  transfers between devices with their start and end apart: 4, of which 2 were waited for; matrix products, arithmetic and copies ran while one was open for 67% of the time, Pallas kernels for 0%

commit v1 on v0

v1 whole, which is shorter than its diff:
```python
import functools

import jax
import jax.numpy as jnp
from jax import lax
from jax.experimental import pallas as pl
from jax.experimental.pallas import tpu as pltpu
from jax.sharding import PartitionSpec as P

BLK = 64
SUB = 8
LANES = 128
VMEM = pl.BlockSpec(memory_space=pltpu.VMEM)
SMEM = pl.BlockSpec(memory_space=pltpu.SMEM)


def ring_order(count):
    half = count // 2
    return [2 * k for k in range(half)] + [2 * k + 1 for k in reversed(range(half))]


def prep_kernel(nrow, ncol, blocks, place, live, it, res, rows, cols, xb, grows, gcols, srows, scols):
    lane = lax.broadcasted_iota(jnp.int32, (SUB, LANES), 1)
    for k in range(blocks // 2):
        a = it[:, k * LANES:(k + 1) * LANES]
        b = res[:, k * LANES:(k + 1) * LANES]
        xb[2 * k * SUB:(2 * k + 1) * SUB, :] = jnp.where(lane < BLK, a, pltpu.roll(b, BLK, 1))
        xb[(2 * k + 1) * SUB:(2 * k + 2) * SUB, :] = jnp.where(lane < BLK, pltpu.roll(a, BLK, 1), b)
    slots = rows.shape[-1]
    alive = lax.broadcasted_iota(jnp.int32, (1, slots), 1) < live[0, 0]

    def split(idx, count):
        chunk = jnp.zeros_like(idx)
        for j in range(1, count):
            chunk += (idx >= j * blocks).astype(jnp.int32)
        return chunk, idx - chunk * blocks

    me = place[0]
    chunk, rest = split(cols[...], nrow)
    pos = jnp.where(chunk % 2 == 0, chunk // 2, nrow - 1 - chunk // 2)
    gap = pos - me
    rel = jnp.where(gap < 0, gap + nrow, gap)
    idx = rel * blocks + rest
    gcols[...] = jnp.where(alive, idx, 0)
    scols[...] = jnp.where(alive, idx, -1)
    major = ncol // 2
    chunk, rest = split(rows[...], ncol)
    gap = chunk // 2 - place[1]
    rel = jnp.where(gap < 0, gap + major, gap) + major * jnp.where(chunk % 2 == place[2], 0, 1)
    idx = rel * blocks + rest
    grows[...] = jnp.where(alive, idx, 0)
    srows[...] = jnp.where(alive, idx, -1)


def tile_kernel(forward, nsrc, slots, gidx, sidx, tiles, *refs):
    srcs, outs = refs[:nsrc], refs[nsrc:-5]
    xall, xg, xt, yhl, hot = refs[-5:]
    step = pl.program_id(0)
    rows_each = srcs[0].shape[0]
    width = sum(o.shape[0] for o in outs) // SUB

    @pl.when(step == 0)
    def _():
        at = 0
        for src in srcs:
            xall[at:at + src.shape[0], :] = src[...]
            at += src.shape[0]

    def take(j, carry):
        for u in range(8):
            s = j * 8 + u
            c = gidx[0, step * LANES + s]
            xg[pl.ds(pl.multiple_of(s * SUB, SUB), SUB), :] = xall[pl.ds(pl.multiple_of(c * SUB, SUB), SUB), :]
        return carry

    lax.fori_loop(0, LANES // 8, take, 0)
    for i in range(SUB):
        xt[i] = xg[pl.ds(i, LANES, stride=SUB), :].T

    lanes_at = pl.multiple_of(step * 2 * LANES, 2 * LANES)
    ids = lax.broadcasted_iota(jnp.int32, (width, LANES), 0)
    match = (ids == sidx[...]).astype(jnp.float32).astype(jnp.bfloat16)
    hot[:, pl.ds(lanes_at, LANES)] = match
    hot[:, pl.ds(pl.multiple_of(lanes_at + LANES, LANES), LANES)] = match

    group = 4 * SUB

    def products(g, carry):
        h, og = g // 2, g % 2

        def term(k, accs):
            if forward:
                parts = [tiles[pl.ds((og * group + o * SUB) * BLK + k, SUB, stride=BLK), :] for o in range(4)]
                t = jnp.concatenate(parts, axis=0)
            else:
                t = tiles[pl.ds(pl.multiple_of(k * BLK + og * group, group), group), :]
            return tuple(acc + t * xt[i, pl.ds(h * BLK + k, 1), :] for i, acc in enumerate(accs))

        zero = jnp.zeros((group, LANES), jnp.float32)
        accs = lax.fori_loop(0, BLK, term, (zero,) * SUB, unroll=8)
        for i, acc in enumerate(accs):
            hi = acc.astype(jnp.bfloat16)
            lo = (acc - hi.astype(jnp.float32)).astype(jnp.bfloat16)
            at = pl.ds(pl.multiple_of(i * LANES + h * BLK + og * group, group), group)
            yhl[at, pl.ds(lanes_at, LANES)] = hi
            yhl[at, pl.ds(pl.multiple_of(lanes_at + LANES, LANES), LANES)] = lo
        return carry

    lax.fori_loop(0, 4, products, 0)

    @pl.when(step == pl.num_programs(0) - 1)
    def _():
        for i in range(0, SUB, 2):
            y = lax.dot_general(
                hot[...], yhl[i * LANES:(i + 2) * LANES, :], (((1,), (1,)), ((), ())), preferred_element_type=jnp.float32
            )
            at = 0
            for out in outs:
                n = out.shape[0] // SUB
                for u in range(2):
                    out[pl.ds(i + u, n, stride=SUB), :] = y[at:at + n, u * LANES:(u + 1) * LANES]
                at += n


def tile_products(forward, gidx, sidx, tiles, srcs, out_blocks):
    slots = tiles.shape[1]
    nsrc = len(srcs)
    width = sum(out_blocks)
    rows = sum(s.shape[0] for s in srcs)
    return pl.pallas_call(
        functools.partial(tile_kernel, forward, nsrc, slots),
        out_shape=tuple(jax.ShapeDtypeStruct((n * SUB, LANES), jnp.float32) for n in out_blocks),
        grid=(slots // LANES,),
        in_specs=[
            SMEM,
            pl.BlockSpec((1, LANES), lambda s: (0, s)),
            pl.BlockSpec((BLK * BLK, LANES), lambda s: (0, s)),
        ]
        + [VMEM] * nsrc,
        out_specs=tuple([VMEM] * len(out_blocks)),
        scratch_shapes=[
            pltpu.VMEM((rows, LANES), jnp.float32),
            pltpu.VMEM((LANES * SUB, LANES), jnp.float32),
            pltpu.VMEM((SUB, LANES, LANES), jnp.float32),
            pltpu.VMEM((SUB * LANES, 2 * slots), jnp.bfloat16),
            pltpu.VMEM((width, 2 * slots), jnp.bfloat16),
        ],
        compiler_params=pltpu.CompilerParams(vmem_limit_bytes=40 << 20),
        cost_estimate=pl.CostEstimate(flops=2 * slots * BLK * BLK * 16, bytes_accessed=tiles.size * 4, transcendentals=0),
        name="forward_products" if forward else "mirrored_products",
    )(gidx, sidx, tiles, *srcs)


def finish_kernel(blocks, nterm, *refs):
    terms, h_it, h_res = refs[:nterm], refs[nterm], refs[nterm + 1]
    lane = lax.broadcasted_iota(jnp.int32, (SUB, LANES), 1)

    def total(k):
        at = slice(k * SUB, (k + 1) * SUB)
        out = terms[0][at, :]
        for term in terms[1:]:
            out = out + term[at, :]
        return out

    for k in range(blocks // 2):
        a, b = total(2 * k), total(2 * k + 1)
        h_it[:, k * LANES:(k + 1) * LANES] = jnp.where(lane < BLK, a, pltpu.roll(b, BLK, 1))
        h_res[:, k * LANES:(k + 1) * LANES] = jnp.where(lane < BLK, pltpu.roll(a, BLK, 1), b)


def body(nrow, ncol, iterate, residual, stored_tiles, block_rows, block_cols, live_counts):
    slots, blk = stored_tiles.shape[2], stored_tiles.shape[3]
    dev = iterate.shape[1]
    blocks = dev // blk
    rows_each = blocks * SUB
    order = ring_order(nrow)
    major = ncol // 2
    tiles = stored_tiles[0, 0].transpose(1, 2, 0).reshape(blk * blk, slots)

    r, c = lax.axis_index("row"), lax.axis_index("col")
    pos = jnp.where(r % 2 == 0, r // 2, nrow - 1 - r // 2)
    place = jnp.stack([pos, c // 2, c % 2]).astype(jnp.int32)
    idx_shape = jax.ShapeDtypeStruct((1, slots), jnp.int32)
    xb, grows, gcols, srows, scols = pl.pallas_call(
        functools.partial(prep_kernel, nrow, ncol, blocks),
        out_shape=(jax.ShapeDtypeStruct((rows_each, LANES), jnp.float32),) + (idx_shape,) * 4,
        in_specs=[SMEM, SMEM, VMEM, VMEM, VMEM, VMEM],
        out_specs=(VMEM,) * 5,
        name="pack",
    )(place, live_counts, iterate, residual, block_rows[0], block_cols[0])

    cw = [(order[p], order[(p + 1) % nrow]) for p in range(nrow)]
    ccw = [(b, a) for a, b in cw]
    core = [(k, k ^ 1) for k in range(ncol)]
    up = [(2 * m + k, 2 * ((m + 1) % major) + k) for m in range(major) for k in range(2)]

    held = [xb]
    for _ in range(major - 1):
        held.append(lax.ppermute(held[-1], "col", up))
    held = [held[0]] + held[:0:-1]
    near_rows = held + [lax.ppermute(h, "col", core) for h in held]

    near_cols = [None] * nrow
    near_cols[0] = xb
    left = right = xb
    for k in range(1, nrow // 2):
        left = lax.ppermute(left, "row", cw)
        right = lax.ppermute(right, "row", ccw)
        near_cols[nrow - k], near_cols[k] = left, right
    mid = rows_each // 2
    left = lax.ppermute(left[:mid], "row", cw)
    right = lax.ppermute(right[mid:], "row", ccw)
    near_cols[nrow // 2:nrow // 2 + 1] = [left, right]

    col_parts = tile_products(
        False, grows, scols, tiles, near_rows, [blocks] * (nrow // 2) + [blocks // 2] * 2 + [blocks] * (nrow // 2 - 1)
    )
    first, last = col_parts[nrow // 2], col_parts[nrow // 2 + 1]
    col_parts = list(col_parts[:nrow // 2]) + [None] + list(col_parts[nrow // 2 + 2:])
    left = lax.ppermute(first, "row", cw)
    right = lax.ppermute(last, "row", ccw)
    for k in range(nrow // 2 - 1, 0, -1):
        a, b = col_parts[k], col_parts[nrow - k]
        if k == nrow // 2 - 1:
            a = jnp.concatenate([a[:mid] + left, a[mid:]], axis=0)
            b = jnp.concatenate([b[:mid], b[mid:] + right], axis=0)
        else:
            a, b = a + left, b + right
        left = lax.ppermute(a, "row", cw)
        right = lax.ppermute(b, "row", ccw)

    own, other = tile_products(True, gcols, srows, tiles, near_cols, [major * blocks] * 2)
    own = own + lax.ppermute(other, "col", core)
    part = own[(major - 1) * rows_each:] if major > 1 else None
    terms = [col_parts[0], left, right, own[:rows_each]]
    for k in range(major - 1, 0, -1):
        got = lax.ppermute(part, "col", up)
        part = got if k == 1 else own[(k - 1) * rows_each:k * rows_each] + got
    if major > 1:
        terms.append(part)

    out_shape = jax.ShapeDtypeStruct(iterate.shape, jnp.float32)
    return pl.pallas_call(
        functools.partial(finish_kernel, blocks, len(terms)),
        out_shape=(out_shape, out_shape),
        in_specs=[VMEM] * len(terms),
        out_specs=(VMEM, VMEM),
        name="unpack",
    )(*terms)


def solution(mesh):
    in_specs = (
        P(None, ("row", "col")),
        P(None, ("row", "col")),
        P("row", "col", None, None, None),
        P("row", "col", None),
        P("row", "col", None),
        P("row", "col"),
    )
    out_specs = (P(None, ("row", "col")), P(None, ("row", "col")))
    run = functools.partial(body, mesh.shape["row"], mesh.shape["col"])
    return jax.shard_map(run, mesh=mesh, in_specs=in_specs, out_specs=out_specs, check_vma=False)
```

time: 387 us -> 120 us (0.31)
  other arithmetic: 130 us -> 0.94 us
  waiting for transfers between devices: 106 us -> 37.1 us
  local copies, waits for them, and re-layouts: 72.9 us -> 7.83 us
  matrix products: 60.5 us -> 0 us
  Pallas kernels: 0 us -> 51.3 us
  starting transfers between devices: 0.16 us -> 21.2 us
  between operations: 14.5 us -> 1.44 us
    scatter-add x2 -> x0, other arithmetic: 129 us -> none  [the longest x1 78.6 us: tile_products(): col_total = col_total.at[:, cols_idx, :].add(mirrored)]
    reduce_scatter x2 -> x0, waiting for transfers between devices: 69.2 us -> none  [the longest x1 69.2 us: apply_blocks(): lax.psum_scatter(col_part, 'row', scatter_dimension=1, tiled=True)]
    dot_general x2 -> x0, matrix products: 60.5 us -> none  [the longest x1 37.1 us: tile_products(): jnp.einsum('sab,vsb->vsa', tile_set, cols_taken, precision=lax.Precision....]
    pallas_call x0 -> x4, Pallas kernels: none -> 51.3 us  [the longest x2 47.2 us: tile_products(): pl.pallas_call(functools.partial(tile_kernel, forward, nsrc, slots), out_...]
    ppermute x0 -> x21, waiting for transfers between devices: none -> 37.1 us  [the longest x3 13.3 us: body(): right = lax.ppermute(b, 'row', ccw)]
    all_gather x2 -> x0, waiting for transfers between devices: 36.4 us -> none  [the longest x1 36.3 us: apply_blocks(): near_cols = lax.all_gather(vectors, 'row', axis=1, tiled=True)]
    reshape x6 -> x0, local copies, waits for them, and re-layouts: 28.3 us -> none  [the longest x2 13.1 us: apply_blocks(): near_cols = near_cols.reshape(vec_count, -1, BLK)]
    ppermute x0 -> x21, starting transfers between devices: none -> 21.2 us  [the longest x3 4.73 us: body(): left = lax.ppermute(left, 'row', cw)]
  transfers between devices with their start and end apart: 4 -> 21, of which waited for: 2 -> 11; matrix products, arithmetic and copies ran while one was open for 67% -> 1% of each run, Pallas kernels for 0% -> 39%
where the time goes in v1:
time: 120 us
  Pallas kernels  51.3 us (43%)
  waiting for transfers between devices  37.1 us (31%)
  starting transfers between devices  21.2 us (18%)
  local copies, waits for them, and re-layouts  7.83 us (7%)
  between operations  1.44 us (1%)
    pallas_call x2, Pallas kernels, tile_products(): pl.pallas_call(functools.partial(tile_kernel, forward, nsrc, slots), out_...  47.2 us
    ppermute x3, waiting for transfers between devices, body(): right = lax.ppermute(b, 'row', ccw)  13.3 us
    unnamed x20, local copies, waits for them, and re-layouts  7.04 us
    ppermute x1, waiting for transfers between devices, body(): held.append(lax.ppermute(held[-1], 'col', up))  5.89 us
    ppermute x3, waiting for transfers between devices, body(): left = lax.ppermute(left, 'row', cw)  5.77 us
    ppermute x3, starting transfers between devices, body(): left = lax.ppermute(left, 'row', cw)  4.73 us
    ppermute x3, starting transfers between devices, body(): right = lax.ppermute(b, 'row', ccw)  4.14 us
    ppermute x1, waiting for transfers between devices, body(): left = lax.ppermute(left[:mid], 'row', cw)  3.77 us
  transfers between devices with their start and end apart: 21, of which 11 were waited for; matrix products, arithmetic and copies ran while one was open for 1% of the time, Pallas kernels for 39%

profile of v1, /device:TPU:0, one launch (start us, length us, event | category | flops | bytes accessed | tf_op | source)
XLA Modules:
  0.0 119.8 jit_solution(10981006820563183705)
XLA Ops:
  1.9 1.9 %pack.1 = (f32[640,128]{1,0:T(8,128)}, s32[1,640]{1,0:T(1,128)}, s32[1,640]{1,0:T(1,128)}, s32[1,640]{1,0:T(1,128)}, s32[1,640]{1,0:T(1,128)}) custom-call(s32[3]{0:T(128)} %pad_add_fusion.place, s32[1,1]{1,0:T(1,128)S(6)} %copy.8.live, f32[8,5120]{1,0:T(8,128)} %it.1, f32[8,5120]{1,0:T(8,128)} %res.1, s32[1,640]{1,0:T(1,128)} %bitcast.12, s32[1,640]{1,0:T(1,128)} %bitcast.13), custom_call_target="tpu_custom_call" | custom-call | tf_op jit(solution)/shard_map/pack/pallas_call | solution.py:184
  3.8 3.0 %collective-permute-start = (f32[640,128]{1,0:T(8,128)}, f32[640,128]{1,0:T(8,128)S(1)}, u32[]{:S(2)}, u32[]{:S(2)}) collective-permute-start(f32[640,128]{1,0:T(8,128)} %get-tuple-element.20.refs_0_), channel_id=1, source_target_pairs={{0,2},{1,3},{2,0},{3,1},{4,6},{5,7},{6,4},{7,5},{8,10},{9,11},{10,... | collective-permute-start | bytes 983048 | tf_op jit(solution)/shard_map/ppermute | solution.py:199
  6.9 1.6 %collective-permute-start.14 = (f32[640,128]{1,0:T(8,128)}, f32[640,128]{1,0:T(8,128)S(1)}, u32[]{:S(2)}, u32[]{:S(2)}) collective-permute-start(f32[640,128]{1,0:T(8,128)} %get-tuple-element.20.refs_0_), channel_id=1, source_target_pairs={{0,8},{8,16},{16,24},{24,28},{28,20},{20,12},{12,4},{4,0},{1,9},{9... | collective-permute-start | bytes 983048 | tf_op jit(solution)/shard_map/ppermute | solution.py:207
  8.9 5.9 %collective-permute-done.refs_1_ = f32[640,128]{1,0:T(8,128)S(1)} collective-permute-done((f32[640,128]{1,0:T(8,128)}, f32[640,128]{1,0:T(8,128)S(1)}, u32[]{:S(2)}, u32[]{:S(2)}) %collective-permute-start) | collective-permute-done | bytes 327712 | tf_op jit(solution)/shard_map/ppermute | solution.py:199
  14.8 1.5 %collective-permute-done.14.refs_8_ = f32[640,128]{1,0:T(8,128)S(1)} collective-permute-done((f32[640,128]{1,0:T(8,128)}, f32[640,128]{1,0:T(8,128)S(1)}, u32[]{:S(2)}, u32[]{:S(2)}) %collective-permute-start.14) | collective-permute-done | bytes 327712 | tf_op jit(solution)/shard_map/ppermute | solution.py:207
  16.2 1.6 %collective-permute-start.15 = (f32[640,128]{1,0:T(8,128)S(1)}, f32[640,128]{1,0:T(8,128)S(1)}, u32[]{:S(2)}, u32[]{:S(2)}) collective-permute-start(f32[640,128]{1,0:T(8,128)S(1)} %collective-permute-done.14.refs_8_), channel_id=1, source_target_pairs={{0,8},{8,16},{16,24},{24,28},{28,20},{20,12},{12,4},{4,0},{1,9},{9... | collective-permute-start | bytes 983048 | tf_op jit(solution)/shard_map/ppermute | solution.py:207
  18.3 4.0 %copy-done = f32[1,1,640,64,64]{2,4,3,1,0:T(8,128)S(1)} copy-done((f32[1,1,640,64,64]{2,4,3,1,0:T(8,128)S(1)}, f32[1,1,640,64,64]{2,4,3,1,0:T(8,128)}, u32[]{:S(2)}) %copy-start) | copy-done | bytes 10485784
  24.6 19.0 %mirrored_products.1 = (f32[640,128]{1,0:T(8,128)S(1)}, f32[640,128]{1,0:T(8,128)S(1)}, f32[640,128]{1,0:T(8,128)S(1)}, f32[640,128]{1,0:T(8,128)S(1)}, f32[320,...) custom-call(s32[1,640]{1,0:T(1,128)S(1)} %copy-done.5, ...), custom_call_target="tpu_custom_call" | custom-call | flops 83886080 | bytes 10485760 | tf_op jit(solution)/shard_map/mirrored_products/pallas_call | solution.py:130
  43.6 1.5 %collective-permute-start.7 = (f32[320,128]{1,0:T(8,128)S(1)}, f32[320,128]{1,0:T(8,128)S(1)}, u32[]{:S(2)}, u32[]{:S(2)}) collective-permute-start(f32[320,128]{1,0:T(8,128)S(1)} %get-tuple-element.29), channel_id=1, source_target_pairs={{8,0},{16,8},{24,16},{28,24},{20,28},{12,20},{4,12},{0,4},{9,1},{1... | collective-permute-start | bytes 491528 | tf_op jit(solution)/shard_map/ppermute | solution.py:221
  45.7 1.6 %collective-permute-start.16 = (f32[640,128]{1,0:T(8,128)S(1)}, f32[640,128]{1,0:T(8,128)S(1)}, u32[]{:S(2)}, u32[]{:S(2)}) collective-permute-start(f32[640,128]{1,0:T(8,128)S(1)} %collective-permute-done.15.refs_7_), channel_id=1, source_target_pairs={{0,8},{8,16},{16,24},{24,28},{28,20},{20,12},{12,4},{4,0},{1,9},{9... | collective-permute-start | bytes 983048 | tf_op jit(solution)/shard_map/ppermute | solution.py:207
  47.7 2.6 %collective-permute-done.7 = f32[320,128]{1,0:T(8,128)S(1)} collective-permute-done((f32[320,128]{1,0:T(8,128)S(1)}, f32[320,128]{1,0:T(8,128)S(1)}, u32[]{:S(2)}, u32[]{:S(2)}) %collective-permute-start.7) | collective-permute-done | bytes 163872 | tf_op jit(solution)/shard_map/ppermute | solution.py:221
  50.3 2.1 %collective-permute-start.8 = (f32[640,128]{1,0:T(8,128)S(1)}, f32[640,128]{1,0:T(8,128)S(1)}, u32[]{:S(2)}, u32[]{:S(2)}) collective-permute-start(f32[640,128]{1,0:T(8,128)S(1)} %pad_maximum_fusion.1), channel_id=1, source_target_pairs={{8,0},{16,8},{24,16},{28,24},{20,28},{12,20},{4,12},{0,4},{9,1},{1... | collective-permute-start | bytes 983048 | tf_op jit(solution)/shard_map/ppermute | solution.py:230
  52.4 4.3 %collective-permute-done.16.refs_6_ = f32[640,128]{1,0:T(8,128)S(1)} collective-permute-done((f32[640,128]{1,0:T(8,128)S(1)}, f32[640,128]{1,0:T(8,128)S(1)}, u32[]{:S(2)}, u32[]{:S(2)}) %collective-permute-start.16) | collective-permute-done | bytes 327712 | tf_op jit(solution)/shard_map/ppermute | solution.py:207
  57.9 1.4 %collective-permute-start.18 = (f32[320,128]{1,0:T(8,128)S(1)}, f32[320,128]{1,0:T(8,128)S(1)}, u32[]{:S(2)}, u32[]{:S(2)}) collective-permute-start(f32[320,128]{1,0:T(8,128)S(1)} %slice.33), channel_id=1, source_target_pairs={{8,0},{16,8},{24,16},{28,24},{20,28},{12,20},{4,12},{0,4},{9,1},{1... | collective-permute-start | bytes 491528 | tf_op jit(solution)/shard_map/ppermute | solution.py:212
  60.1 3.8 %collective-permute-done.17.refs_4_ = f32[320,128]{1,0:T(8,128)S(1)} collective-permute-done((f32[320,128]{1,0:T(8,128)S(1)}, f32[320,128]{1,0:T(8,128)S(1)}, u32[]{:S(2)}, u32[]{:S(2)}) %collective-permute-start.17) | collective-permute-done | bytes 163872 | tf_op jit(solution)/shard_map/ppermute | solution.py:211
  63.9 2.6 %collective-permute-done.18.refs_5_ = f32[320,128]{1,0:T(8,128)S(1)} collective-permute-done((f32[320,128]{1,0:T(8,128)S(1)}, f32[320,128]{1,0:T(8,128)S(1)}, u32[]{:S(2)}, u32[]{:S(2)}) %collective-permute-start.18) | collective-permute-done | bytes 163872 | tf_op jit(solution)/shard_map/ppermute | solution.py:212
  66.5 28.2 %forward_products.1 = (f32[1280,128]{1,0:T(8,128)S(1)}, f32[1280,128]{1,0:T(8,128)S(1)}) custom-call(s32[1,640]{1,0:T(1,128)S(1)} %copy-done.3, s32[1,640]{1,0:T(1,128)S(1)} %copy-done.4, f32[4096,640]{1,0:T(8,128)S(1)} %bitcast.11, f32[640,128]{1,0:T(8,128)S(1)} %copy-done.1, f32[640,128]{1,0:T(8,128)S(1)} %collective-permute-done.11.refs_1_, ...), custom_call_target="tpu_custom_call" | custom-call | flops 83886080 | bytes 10485760 | tf_op jit(solution)/shard_map/forward_products/pallas_call | solution.py:130
  94.8 1.0 collective-permute-start.9
  95.9 1.1 collective-permute-start.5
  97.0 8.0 %collective-permute-done.9 = f32[640,128]{1,0:T(8,128)S(1)} collective-permute-done((f32[640,128]{1,0:T(8,128)S(1)}, f32[640,128]{1,0:T(8,128)S(1)}, u32[]{:S(2)}, u32[]{:S(2)}) %collective-permute-start.9) | collective-permute-done | bytes 327712 | tf_op jit(solution)/shard_map/ppermute | solution.py:230
  106.1 1.1 collective-permute-start.6
  109.1 5.3 %collective-permute-done.10.refs_2_ = f32[640,128]{1,0:T(8,128)S(1)} collective-permute-done((f32[640,128]{1,0:T(8,128)S(1)}, f32[640,128]{1,0:T(8,128)S(1)}, u32[]{:S(2)}, u32[]{:S(2)}) %collective-permute-start.10) | collective-permute-done | bytes 327712 | tf_op jit(solution)/shard_map/ppermute | solution.py:230
  115.2 1.6 %collective-permute-done.20.refs_4_ = f32[640,128]{1,0:T(8,128)S(1)} collective-permute-done((f32[640,128]{1,0:T(8,128)S(1)}, f32[640,128]{1,0:T(8,128)S(1)}, u32[]{:S(2)}, u32[]{:S(2)}) %collective-permute-start.20) | collective-permute-done | bytes 327712 | tf_op jit(solution)/shard_map/ppermute | solution.py:237
  117.5 2.2 %unpack.1 = (f32[8,5120]{1,0:T(8,128)}, f32[8,5120]{1,0:T(8,128)}) custom-call(f32[640,128]{1,0:T(8,128)} %copy-done.2, f32[640,128]{1,0:T(8,128)} %copy-done.8, f32[640,128]{1,0:T(8,128)} %copy-done.7, f32[640,128]{1,0:T(8,128)} %get-tuple-element.35.refs_3_, f32[640,128]{1,0:T(8,128)} %copy-done.9), custom_call_target="tpu_custom_call" | custom-call | tf_op jit(solution)/shard_map/unpack/pallas_call | solution.py:243
  (55 shorter events, 11.5 us)
Async XLA Ops:
  3.8 62.7 %copy-start.3 = (s32[1,640]{1,0:T(1,128)S(1)}, s32[1,640]{1,0:T(1,128)}, u32[]{:S(2)}) copy-start(s32[1,640]{1,0:T(1,128)} %get-tuple-element.30.gidx) | copy-start | bytes 7684
  3.8 62.7 %copy-start.4 = (s32[1,640]{1,0:T(1,128)S(1)}, s32[1,640]{1,0:T(1,128)}, u32[]{:S(2)}) copy-start(s32[1,640]{1,0:T(1,128)} %get-tuple-element.31.sidx) | copy-start | bytes 7684
  3.8 11.0 %collective-permute-start = (f32[640,128]{1,0:T(8,128)}, f32[640,128]{1,0:T(8,128)S(1)}, u32[]{:S(2)}, u32[]{:S(2)}) collective-permute-start(f32[640,128]{1,0:T(8,128)} %get-tuple-element.20.refs_0_), channel_id=1, source_target_pairs={{0,2},{1,3},{2,0},{3,1},{4,6},{5,7},{6,4},{7,5},{8,10},{9,11},{10,... | collective-permute-start | bytes 983048 | tf_op jit(solution)/shard_map/ppermute | solution.py:199
  6.9 9.4 %collective-permute-start.14 = (f32[640,128]{1,0:T(8,128)}, f32[640,128]{1,0:T(8,128)S(1)}, u32[]{:S(2)}, u32[]{:S(2)}) collective-permute-start(f32[640,128]{1,0:T(8,128)} %get-tuple-element.20.refs_0_), channel_id=1, source_target_pairs={{0,8},{8,16},{16,24},{24,28},{28,20},{20,12},{12,4},{4,0},{1,9},{9... | collective-permute-start | bytes 983048 | tf_op jit(solution)/shard_map/ppermute | solution.py:207
  8.4 9.4 %collective-permute-start.11 = (f32[640,128]{1,0:T(8,128)}, f32[640,128]{1,0:T(8,128)S(1)}, u32[]{:S(2)}, u32[]{:S(2)}) collective-permute-start(f32[640,128]{1,0:T(8,128)} %get-tuple-element.20.refs_0_), channel_id=1, source_target_pairs={{8,0},{16,8},{24,16},{28,24},{20,28},{12,20},{4,12},{0,4},{9,1},{1... | collective-permute-start | bytes 983048 | tf_op jit(solution)/shard_map/ppermute | solution.py:208
  8.9 9.4 %collective-permute-start.1 = (f32[640,128]{1,0:T(8,128)}, f32[640,128]{1,0:T(8,128)S(1)}, u32[]{:S(2)}, u32[]{:S(2)}) collective-permute-start(f32[640,128]{1,0:T(8,128)} %get-tuple-element.20.refs_0_), channel_id=1, source_target_pairs={{0,1},{1,0},{2,3},{3,2},{4,5},{5,4},{6,7},{7,6},{8,9},{9,8},{10,11... | collective-permute-start | bytes 983048 | tf_op jit(solution)/shard_map/ppermute | solution.py:201
  14.8 3.5 %collective-permute-start.2 = (f32[640,128]{1,0:T(8,128)S(1)}, f32[640,128]{1,0:T(8,128)S(1)}, u32[]{:S(2)}, u32[]{:S(2)}) collective-permute-start(f32[640,128]{1,0:T(8,128)S(1)} %collective-permute-done.refs_1_), channel_id=1, source_target_pairs={{0,1},{1,0},{2,3},{3,2},{4,5},{5,4},{6,7},{7,6},{8,9},{9,8},{10,11... | collective-permute-start | bytes 983048 | tf_op jit(solution)/shard_map/ppermute | solution.py:201
  16.2 29.4 %collective-permute-start.15 = (f32[640,128]{1,0:T(8,128)S(1)}, f32[640,128]{1,0:T(8,128)S(1)}, u32[]{:S(2)}, u32[]{:S(2)}) collective-permute-start(f32[640,128]{1,0:T(8,128)S(1)} %collective-permute-done.14.refs_8_), channel_id=1, source_target_pairs={{0,8},{8,16},{16,24},{24,28},{28,20},{20,12},{12,4},{4,0},{1,9},{9... | collective-permute-start | bytes 983048 | tf_op jit(solution)/shard_map/ppermute | solution.py:207
  17.8 29.4 %collective-permute-start.12 = (f32[640,128]{1,0:T(8,128)S(1)}, f32[640,128]{1,0:T(8,128)S(1)}, u32[]{:S(2)}, u32[]{:S(2)}) collective-permute-start(f32[640,128]{1,0:T(8,128)S(1)} %collective-permute-done.11.refs_1_), channel_id=1, source_target_pairs={{8,0},{16,8},{24,16},{28,24},{20,28},{12,20},{4,12},{0,4},{9,1},{1... | collective-permute-start | bytes 983048 | tf_op jit(solution)/shard_map/ppermute | solution.py:208
  43.6 22.9 %copy-start.2 = (f32[640,128]{1,0:T(8,128)}, f32[640,128]{1,0:T(8,128)S(1)}, u32[]{:S(2)}) copy-start(f32[640,128]{1,0:T(8,128)S(1)} %get-tuple-element.21.refs_0_) | copy-start | bytes 983044
  43.6 6.7 %collective-permute-start.7 = (f32[320,128]{1,0:T(8,128)S(1)}, f32[320,128]{1,0:T(8,128)S(1)}, u32[]{:S(2)}, u32[]{:S(2)}) collective-permute-start(f32[320,128]{1,0:T(8,128)S(1)} %get-tuple-element.29), channel_id=1, source_target_pairs={{8,0},{16,8},{24,16},{28,24},{20,28},{12,20},{4,12},{0,4},{9,1},{1... | collective-permute-start | bytes 491528 | tf_op jit(solution)/shard_map/ppermute | solution.py:221
  45.1 14.2 %collective-permute-start.3 = (f32[320,128]{1,0:T(8,128)S(1)}, f32[320,128]{1,0:T(8,128)S(1)}, u32[]{:S(2)}, u32[]{:S(2)}) collective-permute-start(f32[320,128]{1,0:T(8,128)S(1)} %get-tuple-element.25), channel_id=1, source_target_pairs={{0,8},{8,16},{16,24},{24,28},{28,20},{20,12},{12,4},{4,0},{1,9},{9... | collective-permute-start | bytes 491528 | tf_op jit(solution)/shard_map/ppermute | solution.py:220
  45.7 11.0 %collective-permute-start.16 = (f32[640,128]{1,0:T(8,128)S(1)}, f32[640,128]{1,0:T(8,128)S(1)}, u32[]{:S(2)}, u32[]{:S(2)}) collective-permute-start(f32[640,128]{1,0:T(8,128)S(1)} %collective-permute-done.15.refs_7_), channel_id=1, source_target_pairs={{0,8},{8,16},{16,24},{24,28},{28,20},{20,12},{12,4},{4,0},{1,9},{9... | collective-permute-start | bytes 983048 | tf_op jit(solution)/shard_map/ppermute | solution.py:207
  47.2 10.6 %collective-permute-start.13 = (f32[640,128]{1,0:T(8,128)S(1)}, f32[640,128]{1,0:T(8,128)S(1)}, u32[]{:S(2)}, u32[]{:S(2)}) collective-permute-start(f32[640,128]{1,0:T(8,128)S(1)} %collective-permute-done.12.refs_2_), channel_id=1, source_target_pairs={{8,0},{16,8},{24,16},{28,24},{20,28},{12,20},{4,12},{0,4},{9,1},{1... | collective-permute-start | bytes 983048 | tf_op jit(solution)/shard_map/ppermute | solution.py:208
  50.3 44.5 %collective-permute-start.8 = (f32[640,128]{1,0:T(8,128)S(1)}, f32[640,128]{1,0:T(8,128)S(1)}, u32[]{:S(2)}, u32[]{:S(2)}) collective-permute-start(f32[640,128]{1,0:T(8,128)S(1)} %pad_maximum_fusion.1), channel_id=1, source_target_pairs={{8,0},{16,8},{24,16},{28,24},{20,28},{12,20},{4,12},{0,4},{9,1},{1... | collective-permute-start | bytes 983048 | tf_op jit(solution)/shard_map/ppermute | solution.py:230
  56.7 7.2 %collective-permute-start.17 = (f32[320,128]{1,0:T(8,128)S(1)}, f32[320,128]{1,0:T(8,128)S(1)}, u32[]{:S(2)}, u32[]{:S(2)}) collective-permute-start(f32[320,128]{1,0:T(8,128)S(1)} %slice.32), channel_id=1, source_target_pairs={{0,8},{8,16},{16,24},{24,28},{28,20},{20,12},{12,4},{4,0},{1,9},{9... | collective-permute-start | bytes 491528 | tf_op jit(solution)/shard_map/ppermute | solution.py:211
  57.9 8.6 %collective-permute-start.18 = (f32[320,128]{1,0:T(8,128)S(1)}, f32[320,128]{1,0:T(8,128)S(1)}, u32[]{:S(2)}, u32[]{:S(2)}) collective-permute-start(f32[320,128]{1,0:T(8,128)S(1)} %slice.33), channel_id=1, source_target_pairs={{8,0},{16,8},{24,16},{28,24},{20,28},{12,20},{4,12},{0,4},{9,1},{1... | collective-permute-start | bytes 491528 | tf_op jit(solution)/shard_map/ppermute | solution.py:212
  59.4 36.5 %collective-permute-start.4 = (f32[640,128]{1,0:T(8,128)S(1)}, f32[640,128]{1,0:T(8,128)S(1)}, u32[]{:S(2)}, u32[]{:S(2)}) collective-permute-start(f32[640,128]{1,0:T(8,128)S(1)} %pad_maximum_fusion), channel_id=1, source_target_pairs={{0,8},{8,16},{16,24},{24,28},{28,20},{20,12},{12,4},{4,0},{1,9},{9... | collective-permute-start | bytes 983048 | tf_op jit(solution)/shard_map/ppermute | solution.py:229
  94.7 12.5 %collective-permute-start.19 = (f32[1280,128]{1,0:T(8,128)S(1)}, f32[1280,128]{1,0:T(8,128)S(1)}, u32[]{:S(2)}, u32[]{:S(2)}) collective-permute-start(f32[1280,128]{1,0:T(8,128)S(1)} %get-tuple-element.33), channel_id=1, source_target_pairs={{0,1},{1,0},{2,3},{3,2},{4,5},{5,4},{6,7},{7,6},{8,9},{9,8},{10,11... | collective-permute-start | bytes 1966088 | tf_op jit(solution)/shard_map/ppermute | solution.py:233
  94.8 10.2 %collective-permute-start.9 = (f32[640,128]{1,0:T(8,128)S(1)}, f32[640,128]{1,0:T(8,128)S(1)}, u32[]{:S(2)}, u32[]{:S(2)}) collective-permute-start(f32[640,128]{1,0:T(8,128)S(1)} %add.36), channel_id=1, source_target_pairs={{8,0},{16,8},{24,16},{28,24},{20,28},{12,20},{4,12},{0,4},{9,1},{1... | collective-permute-start | bytes 983048 | tf_op jit(solution)/shard_map/ppermute | solution.py:230
  95.9 10.2 %collective-permute-start.5 = (f32[640,128]{1,0:T(8,128)S(1)}, f32[640,128]{1,0:T(8,128)S(1)}, u32[]{:S(2)}, u32[]{:S(2)}) collective-permute-start(f32[640,128]{1,0:T(8,128)S(1)} %add.33), channel_id=1, source_target_pairs={{0,8},{8,16},{16,24},{24,28},{28,20},{20,12},{12,4},{4,0},{1,9},{9... | collective-permute-start | bytes 983048 | tf_op jit(solution)/shard_map/ppermute | solution.py:229
  105.0 9.4 %collective-permute-start.10 = (f32[640,128]{1,0:T(8,128)S(1)}, f32[640,128]{1,0:T(8,128)S(1)}, u32[]{:S(2)}, u32[]{:S(2)}) collective-permute-start(f32[640,128]{1,0:T(8,128)S(1)} %add.37), channel_id=1, source_target_pairs={{8,0},{16,8},{24,16},{28,24},{20,28},{12,20},{4,12},{0,4},{9,1},{1... | collective-permute-start | bytes 983048 | tf_op jit(solution)/shard_map/ppermute | solution.py:230
  106.1 9.1 %collective-permute-start.6 = (f32[640,128]{1,0:T(8,128)S(1)}, f32[640,128]{1,0:T(8,128)S(1)}, u32[]{:S(2)}, u32[]{:S(2)}) collective-permute-start(f32[640,128]{1,0:T(8,128)S(1)} %add.34), channel_id=1, source_target_pairs={{0,8},{8,16},{16,24},{24,28},{28,20},{20,12},{12,4},{4,0},{1,9},{9... | collective-permute-start | bytes 983048 | tf_op jit(solution)/shard_map/ppermute | solution.py:229
  108.0 8.8 %collective-permute-start.20 = (f32[640,128]{1,0:T(8,128)S(1)}, f32[640,128]{1,0:T(8,128)S(1)}, u32[]{:S(2)}, u32[]{:S(2)}) collective-permute-start(f32[640,128]{1,0:T(8,128)S(1)} %get-tuple-element.34), channel_id=1, source_target_pairs={{0,2},{1,3},{2,0},{3,1},{4,6},{5,7},{6,4},{7,5},{8,10},{9,11},{10,... | collective-permute-start | bytes 983048 | tf_op jit(solution)/shard_map/ppermute | solution.py:237
  (7 other events, 11.0 us)

commit v2 on v1

--- a/solution.py
+++ b/solution.py
@@ -10,6 +10,8 @@
 BLK = 64
 SUB = 8
 LANES = 128
+PITCH = 40
+PAIR = 32
 VMEM = pl.BlockSpec(memory_space=pltpu.VMEM)
 SMEM = pl.BlockSpec(memory_space=pltpu.SMEM)
 
@@ -42,113 +44,135 @@
     rel = jnp.where(gap < 0, gap + nrow, gap)
     idx = rel * blocks + rest
     gcols[...] = jnp.where(alive, idx, 0)
-    scols[...] = jnp.where(alive, idx, -1)
+    scols[...] = jnp.where(alive, idx, nrow * blocks)
     major = ncol // 2
     chunk, rest = split(rows[...], ncol)
     gap = chunk // 2 - place[1]
     rel = jnp.where(gap < 0, gap + major, gap) + major * jnp.where(chunk % 2 == place[2], 0, 1)
     idx = rel * blocks + rest
     grows[...] = jnp.where(alive, idx, 0)
-    srows[...] = jnp.where(alive, idx, -1)
-
-
-def tile_kernel(forward, nsrc, slots, gidx, sidx, tiles, *refs):
-    srcs, outs = refs[:nsrc], refs[nsrc:-5]
-    xall, xg, xt, yhl, hot = refs[-5:]
-    step = pl.program_id(0)
-    rows_each = srcs[0].shape[0]
-    width = sum(o.shape[0] for o in outs) // SUB
-
-    @pl.when(step == 0)
-    def _():
-        at = 0
-        for src in srcs:
-            xall[at:at + src.shape[0], :] = src[...]
-            at += src.shape[0]
-
-    def take(j, carry):
-        for u in range(8):
-            s = j * 8 + u
-            c = gidx[0, step * LANES + s]
-            xg[pl.ds(pl.multiple_of(s * SUB, SUB), SUB), :] = xall[pl.ds(pl.multiple_of(c * SUB, SUB), SUB), :]
+    srows[...] = jnp.where(alive, idx, ncol * blocks)
+
+
+def first_half(rows):
+    return lax.broadcasted_iota(jnp.int32, (rows, LANES), 1) < BLK
+
+
+def split_kernel(tiles, parts, turned):
+    half = BLK // 2
+
+    def turn(j, carry):
+        a = tiles[pl.ds(pl.multiple_of(j * BLK, BLK), BLK), :]
+        b = tiles[pl.ds(pl.multiple_of((j + half) * BLK, BLK), BLK), :]
+        turned[pl.ds(j, LANES, stride=PITCH), :] = jnp.concatenate([a, b], axis=0).T
         return carry
 
-    lax.fori_loop(0, LANES // 8, take, 0)
-    for i in range(SUB):
-        xt[i] = xg[pl.ds(i, LANES, stride=SUB), :].T
-
-    lanes_at = pl.multiple_of(step * 2 * LANES, 2 * LANES)
-    ids = lax.broadcasted_iota(jnp.int32, (width, LANES), 0)
-    match = (ids == sidx[...]).astype(jnp.float32).astype(jnp.bfloat16)
-    hot[:, pl.ds(lanes_at, LANES)] = match
-    hot[:, pl.ds(pl.multiple_of(lanes_at + LANES, LANES), LANES)] = match
-
-    group = 4 * SUB
-
-    def products(g, carry):
-        h, og = g // 2, g % 2
-
-        def term(k, accs):
+    lax.fori_loop(0, half, turn, 0, unroll=32)
+    first = first_half(half)
+
+    def split(s, carry):
+        x = turned[pl.ds(pl.multiple_of(s * PITCH, SUB), half), :]
+        hi = x.astype(jnp.bfloat16).astype(jnp.float32)
+        lo = x - hi
+        top = jnp.where(first, hi, pltpu.roll(lo, BLK, 1))
+        bottom = jnp.where(first, pltpu.roll(hi, BLK, 1), lo)
+        both = jnp.concatenate([top, bottom], axis=0).astype(jnp.bfloat16)
+        parts[pl.ds(pl.multiple_of(s * BLK, BLK), BLK), :] = both
+        return carry
+
+    lax.fori_loop(0, LANES, split, 0, unroll=32)
+
+
+def split_tiles(tiles):
+    slots = tiles.shape[1]
+    return pl.pallas_call(
+        split_kernel,
+        out_shape=jax.ShapeDtypeStruct((slots * BLK, LANES), jnp.bfloat16),
+        grid=(slots // LANES,),
+        in_specs=[pl.BlockSpec((BLK * BLK, LANES), lambda s: (0, s))],
+        out_specs=pl.BlockSpec((LANES * BLK, LANES), lambda s: (s, 0)),
+        scratch_shapes=[pltpu.VMEM((LANES * PITCH, LANES), jnp.float32)],
+        compiler_params=pltpu.CompilerParams(vmem_limit_bytes=16 << 20),
+        cost_estimate=pl.CostEstimate(flops=0, bytes_accessed=30 << 20, transcendentals=0),
+        name="split_tiles",
+    )(tiles)
+
+
+def tile_kernel(forward, nsrc, group, live, gidx, sidx, parts, *refs):
+    srcs, outs, pairs, acc = refs[:nsrc], refs[nsrc:-2], refs[-2], refs[-1]
+    first8 = first_half(SUB)
+    at = 0
+    some = 4
+    first = first_half(some * SUB)
+    for src in srcs:
+        n = src.shape[0] // SUB
+
+        def pack(k, carry, src=src, at=at):
+            x = src[pl.ds(pl.multiple_of(k * some * SUB, some * SUB), some * SUB), :]
+            swapped = pltpu.roll(x, BLK, 1)
+            his, los = [], []
+            for v in (jnp.where(first, x, swapped), jnp.where(first, swapped, x)):
+                hi = v.astype(jnp.bfloat16).astype(jnp.float32)
+                his.append(hi.reshape(some, SUB, LANES))
+                los.append(jnp.where(first, v - hi, 0.0).reshape(some, SUB, LANES))
+            rows = jnp.concatenate(his + los, axis=1).reshape(some * PAIR, LANES)
+            to = pl.ds(pl.multiple_of((at + k * some) * PAIR, some * PAIR), some * PAIR)
+            pairs[to, :] = rows.astype(jnp.bfloat16)
+            return carry
+
+        lax.fori_loop(0, n // some, pack, 0, unroll=n // some)
+        at += n
+    acc[...] = jnp.zeros_like(acc)
+
+    def step(k, carry):
+        for u in range(LANES // group):
+            s = k * LANES + u * group
+            x = jnp.concatenate(
+                [pairs[pl.ds(pl.multiple_of(gidx[0, s + t] * PAIR, PAIR), PAIR), :] for t in range(group)], axis=0
+            )
+            w = parts[pl.ds(pl.multiple_of(s * BLK, BLK), BLK * group), :]
             if forward:
-                parts = [tiles[pl.ds((og * group + o * SUB) * BLK + k, SUB, stride=BLK), :] for o in range(4)]
-                t = jnp.concatenate(parts, axis=0)
+                y = lax.dot_general(x, w, (((1,), (1,)), ((), ())), preferred_element_type=jnp.float32)
             else:
-                t = tiles[pl.ds(pl.multiple_of(k * BLK + og * group, group), group), :]
-            return tuple(acc + t * xt[i, pl.ds(h * BLK + k, 1), :] for i, acc in enumerate(accs))
-
-        zero = jnp.zeros((group, LANES), jnp.float32)
-        accs = lax.fori_loop(0, BLK, term, (zero,) * SUB, unroll=8)
-        for i, acc in enumerate(accs):
-            hi = acc.astype(jnp.bfloat16)
-            lo = (acc - hi.astype(jnp.float32)).astype(jnp.bfloat16)
-            at = pl.ds(pl.multiple_of(i * LANES + h * BLK + og * group, group), group)
-            yhl[at, pl.ds(lanes_at, LANES)] = hi
-            yhl[at, pl.ds(pl.multiple_of(lanes_at + LANES, LANES), LANES)] = lo
+                y = jnp.dot(x[:, :BLK], w, preferred_element_type=jnp.float32)
+            for t in range(group):
+                at = slice(t * PAIR, t * PAIR + PAIR)
+                z = y[at, t // 2 * LANES:(t // 2 + 1) * LANES] if forward else y[at]
+                z = z[:2 * SUB] + z[2 * SUB:]
+                if not forward:
+                    z = z + pltpu.roll(z, BLK, 1)
+                    z = jnp.where(first8, z[:SUB], z[SUB:])
+                elif t % 2 == 0:
+                    z = jnp.where(first8, z[:SUB], pltpu.roll(z[SUB:], BLK, 1))
+                else:
+                    z = jnp.where(first8, pltpu.roll(z[:SUB], BLK, 1), z[SUB:])
+                to = pl.ds(pl.multiple_of(sidx[0, s + t] * SUB, SUB), SUB)
+                acc[to, :] += z
         return carry
 
-    lax.fori_loop(0, 4, products, 0)
-
-    @pl.when(step == pl.num_programs(0) - 1)
-    def _():
-        for i in range(0, SUB, 2):
-            y = lax.dot_general(
-                hot[...], yhl[i * LANES:(i + 2) * LANES, :], (((1,), (1,)), ((), ())), preferred_element_type=jnp.float32
-            )
-            at = 0
-            for out in outs:
-                n = out.shape[0] // SUB
-                for u in range(2):
-                    out[pl.ds(i + u, n, stride=SUB), :] = y[at:at + n, u * LANES:(u + 1) * LANES]
-                at += n
-
-
-def tile_products(forward, gidx, sidx, tiles, srcs, out_blocks):
-    slots = tiles.shape[1]
-    nsrc = len(srcs)
-    width = sum(out_blocks)
-    rows = sum(s.shape[0] for s in srcs)
+    lax.fori_loop(0, (live[0, 0] + LANES - 1) // LANES, step, 0)
+    at = 0
+    for out in outs:
+        n = out.shape[0]
+        out[...] = acc[at:at + n, :]
+        at += n
+
+
+def tile_products(forward, live, gidx, sidx, parts, srcs, out_blocks):
+    slots = gidx.shape[1]
     return pl.pallas_call(
-        functools.partial(tile_kernel, forward, nsrc, slots),
+        functools.partial(tile_kernel, forward, len(srcs), 4 if forward else 1),
         out_shape=tuple(jax.ShapeDtypeStruct((n * SUB, LANES), jnp.float32) for n in out_blocks),
-        grid=(slots // LANES,),
-        in_specs=[
-            SMEM,
-            pl.BlockSpec((1, LANES), lambda s: (0, s)),
-            pl.BlockSpec((BLK * BLK, LANES), lambda s: (0, s)),
-        ]
-        + [VMEM] * nsrc,
+        in_specs=[SMEM] * 3 + [VMEM] * (1 + len(srcs)),
         out_specs=tuple([VMEM] * len(out_blocks)),
         scratch_shapes=[
-            pltpu.VMEM((rows, LANES), jnp.float32),
-            pltpu.VMEM((LANES * SUB, LANES), jnp.float32),
-            pltpu.VMEM((SUB, LANES, LANES), jnp.float32),
-            pltpu.VMEM((SUB * LANES, 2 * slots), jnp.bfloat16),
-            pltpu.VMEM((width, 2 * slots), jnp.bfloat16),
+            pltpu.VMEM((sum(s.shape[0] for s in srcs) * PAIR // SUB, LANES), jnp.bfloat16),
+            pltpu.VMEM(((sum(out_blocks) + 1) * SUB, LANES), jnp.float32),
         ],
-        compiler_params=pltpu.CompilerParams(vmem_limit_bytes=40 << 20),
-        cost_estimate=pl.CostEstimate(flops=2 * slots * BLK * BLK * 16, bytes_accessed=tiles.size * 4, transcendentals=0),
+        compiler_params=pltpu.CompilerParams(vmem_limit_bytes=20 << 20),
+        cost_estimate=pl.CostEstimate(flops=0, bytes_accessed=25 << 20, transcendentals=0),
         name="forward_products" if forward else "mirrored_products",
-    )(gidx, sidx, tiles, *srcs)
+    )(live, gidx, sidx, parts, *srcs)
 
 
 def finish_kernel(blocks, nterm, *refs):
@@ -212,8 +236,9 @@
     right = lax.ppermute(right[mid:], "row", ccw)
     near_cols[nrow // 2:nrow // 2 + 1] = [left, right]
 
+    parts = split_tiles(tiles)
     col_parts = tile_products(
-        False, grows, scols, tiles, near_rows, [blocks] * (nrow // 2) + [blocks // 2] * 2 + [blocks] * (nrow // 2 - 1)
+        False, live_counts, grows, scols, parts, near_rows, [blocks] * (nrow // 2) + [blocks // 2] * 2 + [blocks] * (nrow // 2 - 1)
     )
     first, last = col_parts[nrow // 2], col_parts[nrow // 2 + 1]
     col_parts = list(col_parts[:nrow // 2]) + [None] + list(col_parts[nrow // 2 + 2:])
@@ -229,7 +254,7 @@
         left = lax.ppermute(a, "row", cw)
         right = lax.ppermute(b, "row", ccw)
 
-    own, other = tile_products(True, gcols, srows, tiles, near_cols, [major * blocks] * 2)
+    own, other = tile_products(True, live_counts, gcols, srows, parts, near_cols, [major * blocks] * 2)
     own = own + lax.ppermute(other, "col", core)
     part = own[(major - 1) * rows_each:] if major > 1 else None
     terms = [col_parts[0], left, right, own[:rows_each]]

time: 120 us -> 90.3 us (0.75)
  Pallas kernels: 51.3 us -> 17.5 us
  starting transfers between devices: 21.2 us -> 27.6 us
  local copies, waits for them, and re-layouts: 7.83 us -> 6.24 us
    pallas_call x2 -> x3, Pallas kernels: 47.2 us -> 13.3 us  [the longest x1 8.02 us: split_tiles(): pl.pallas_call(split_kernel, out_shape=jax.ShapeDtypeStruct((slots * BLK,...]
    ppermute x3, starting transfers between devices: 4.14 us -> 10.1 us  [body(): right = lax.ppermute(b, 'row', ccw)]
    ppermute x1, starting transfers between devices: 1.55 us -> 4.03 us  [body(): right = lax.ppermute(last, 'row', ccw)]
    ppermute x3, starting transfers between devices: 2.86 us -> 0.91 us  [body(): left = lax.ppermute(a, 'row', cw)]
    unnamed x20, local copies, waits for them, and re-layouts: 7.04 us -> 5.45 us
    ppermute x1, starting transfers between devices: 0.49 us -> 1.99 us  [body(): left = lax.ppermute(left[:mid], 'row', cw)]
    ppermute x1, waiting for transfers between devices: 3.77 us -> 2.32 us  [body(): left = lax.ppermute(left[:mid], 'row', cw)]
  transfers between devices with their start and end apart: 21 -> 21, of which waited for: 11 -> 10; matrix products, arithmetic and copies ran while one was open for 1% -> 1% of each run, Pallas kernels for 39% -> 15%
where the time goes in v2:
time: 90.3 us; the launch traced here: 89.8 us
  waiting for transfers between devices  36 us (40%)
  starting transfers between devices  27.6 us (31%)
  Pallas kernels  17.5 us (19%)
  local copies, waits for them, and re-layouts  6.24 us (7%)
  between operations  1.51 us (2%)
  other arithmetic  0.96 us (1%)
    ppermute x3, waiting for transfers between devices, body(): right = lax.ppermute(b, 'row', ccw)  14.2 us
    ppermute x3, starting transfers between devices, body(): right = lax.ppermute(b, 'row', ccw)  10.1 us
    pallas_call x1, Pallas kernels, split_tiles(): pl.pallas_call(split_kernel, out_shape=jax.ShapeDtypeStruct((slots * BLK,...  8.02 us
    ppermute x1, waiting for transfers between devices, body(): held.append(lax.ppermute(held[-1], 'col', up))  5.89 us
    unnamed x20, local copies, waits for them, and re-layouts  5.45 us
    pallas_call x2, Pallas kernels, tile_products(): pl.pallas_call(functools.partial(tile_kernel, forward, len(srcs), 4 if fo...  5.32 us
    ppermute x3, waiting for transfers between devices, body(): left = lax.ppermute(left, 'row', cw)  5.08 us
    ppermute x3, starting transfers between devices, body(): left = lax.ppermute(left, 'row', cw)  4.81 us
  transfers between devices with their start and end apart: 21, of which 10 were waited for; matrix products, arithmetic and copies ran while one was open for 1% of the time, Pallas kernels for 15%

profile of v2, /device:TPU:0, one launch (start us, length us, event | category | flops | bytes accessed | tf_op | source)
XLA Modules:
  0.0 89.8 jit_solution(4348512746748256112)
XLA Ops:
  1.9 1.9 %pack.1 = (f32[640,128]{1,0:T(8,128)}, s32[1,640]{1,0:T(1,128)}, s32[1,640]{1,0:T(1,128)}, s32[1,640]{1,0:T(1,128)}, s32[1,640]{1,0:T(1,128)}) custom-call(s32[3]{0:T(128)} %pad_add_fusion.place, s32[1,1]{1,0:T(1,128)S(6)} %copy.8.live, f32[8,5120]{1,0:T(8,128)} %it.1, f32[8,5120]{1,0:T(8,128)} %res.1, s32[1,640]{1,0:T(1,128)} %bitcast.11, s32[1,640]{1,0:T(1,128)} %bitcast.12), custom_call_target="tpu_custom_call" | custom-call | tf_op jit(solution)/shard_map/pack/pallas_call | solution.py:208
  3.8 3.0 %collective-permute-start = (f32[640,128]{1,0:T(8,128)}, f32[640,128]{1,0:T(8,128)S(1)}, u32[]{:S(2)}, u32[]{:S(2)}) collective-permute-start(f32[640,128]{1,0:T(8,128)} %get-tuple-element.20.refs_0_), channel_id=1, source_target_pairs={{0,2},{1,3},{2,0},{3,1},{4,6},{5,7},{6,4},{7,5},{8,10},{9,11},{10,... | collective-permute-start | bytes 983048 | tf_op jit(solution)/shard_map/ppermute | solution.py:223
  6.8 1.6 %collective-permute-start.14 = (f32[640,128]{1,0:T(8,128)}, f32[640,128]{1,0:T(8,128)S(1)}, u32[]{:S(2)}, u32[]{:S(2)}) collective-permute-start(f32[640,128]{1,0:T(8,128)} %get-tuple-element.20.refs_0_), channel_id=1, source_target_pairs={{0,8},{8,16},{16,24},{24,28},{28,20},{20,12},{12,4},{4,0},{1,9},{9... | collective-permute-start | bytes 983048 | tf_op jit(solution)/shard_map/ppermute | solution.py:231
  8.8 5.9 %collective-permute-done.refs_1_ = f32[640,128]{1,0:T(8,128)S(1)} collective-permute-done((f32[640,128]{1,0:T(8,128)}, f32[640,128]{1,0:T(8,128)S(1)}, u32[]{:S(2)}, u32[]{:S(2)}) %collective-permute-start) | collective-permute-done | bytes 327712 | tf_op jit(solution)/shard_map/ppermute | solution.py:223
  14.7 1.5 %collective-permute-done.14.refs_8_ = f32[640,128]{1,0:T(8,128)S(1)} collective-permute-done((f32[640,128]{1,0:T(8,128)}, f32[640,128]{1,0:T(8,128)S(1)}, u32[]{:S(2)}, u32[]{:S(2)}) %collective-permute-start.14) | collective-permute-done | bytes 327712 | tf_op jit(solution)/shard_map/ppermute | solution.py:231
  16.2 1.6 %collective-permute-start.15 = (f32[640,128]{1,0:T(8,128)S(1)}, f32[640,128]{1,0:T(8,128)S(1)}, u32[]{:S(2)}, u32[]{:S(2)}) collective-permute-start(f32[640,128]{1,0:T(8,128)S(1)} %collective-permute-done.14.refs_8_), channel_id=1, source_target_pairs={{0,8},{8,16},{16,24},{24,28},{28,20},{20,12},{12,4},{4,0},{1,9},{9... | collective-permute-start | bytes 983048 | tf_op jit(solution)/shard_map/ppermute | solution.py:231
  18.2 4.0 %copy-done = f32[1,1,640,64,64]{2,4,3,1,0:T(8,128)S(1)} copy-done((f32[1,1,640,64,64]{2,4,3,1,0:T(8,128)S(1)}, f32[1,1,640,64,64]{2,4,3,1,0:T(8,128)}, u32[]{:S(2)}) %copy-start) | copy-done | bytes 10485784
  22.2 8.0 %split_tiles.1.parts = bf16[40960,128]{1,0:T(8,128)(2,1)S(1)} custom-call(f32[4096,640]{1,0:T(8,128)S(1)} %bitcast.10), custom_call_target="tpu_custom_call" | custom-call | bytes 31457280 | tf_op jit(solution)/shard_map/split_tiles/pallas_call | solution.py:88
  30.3 2.4 %mirrored_products.1 = (f32[640,128]{1,0:T(8,128)S(1)}, f32[640,128]{1,0:T(8,128)S(1)}, f32[640,128]{1,0:T(8,128)S(1)}, f32[640,128]{1,0:T(8,128)S(1)}, f32[320,...) custom-call(s32[1,1]{1,0:T(1,128)S(6)} %copy.8.live, ...), custom_call_target="tpu_custom_call" | custom-call | bytes 26214400 | tf_op jit(solution)/shard_map/mirrored_products/pallas_call | solution.py:163
  33.5 4.0 %collective-permute-start.7 = (f32[320,128]{1,0:T(8,128)S(1)}, f32[320,128]{1,0:T(8,128)S(1)}, u32[]{:S(2)}, u32[]{:S(2)}) collective-permute-start(f32[320,128]{1,0:T(8,128)S(1)} %get-tuple-element.29), channel_id=1, source_target_pairs={{8,0},{16,8},{24,16},{28,24},{20,28},{12,20},{4,12},{0,4},{9,1},{1... | collective-permute-start | bytes 491528 | tf_op jit(solution)/shard_map/ppermute | solution.py:246
  37.5 1.7 %collective-permute-start.16 = (f32[640,128]{1,0:T(8,128)S(1)}, f32[640,128]{1,0:T(8,128)S(1)}, u32[]{:S(2)}, u32[]{:S(2)}) collective-permute-start(f32[640,128]{1,0:T(8,128)S(1)} %collective-permute-done.15.refs_7_), channel_id=1, source_target_pairs={{0,8},{8,16},{16,24},{24,28},{28,20},{20,12},{12,4},{4,0},{1,9},{9... | collective-permute-start | bytes 983048 | tf_op jit(solution)/shard_map/ppermute | solution.py:231
  39.6 2.5 %collective-permute-done.7 = f32[320,128]{1,0:T(8,128)S(1)} collective-permute-done((f32[320,128]{1,0:T(8,128)S(1)}, f32[320,128]{1,0:T(8,128)S(1)}, u32[]{:S(2)}, u32[]{:S(2)}) %collective-permute-start.7) | collective-permute-done | bytes 163872 | tf_op jit(solution)/shard_map/ppermute | solution.py:246
  42.1 2.5 %collective-permute-start.8 = (f32[640,128]{1,0:T(8,128)S(1)}, f32[640,128]{1,0:T(8,128)S(1)}, u32[]{:S(2)}, u32[]{:S(2)}) collective-permute-start(f32[640,128]{1,0:T(8,128)S(1)} %pad_maximum_fusion.1), channel_id=1, source_target_pairs={{8,0},{16,8},{24,16},{28,24},{20,28},{12,20},{4,12},{0,4},{9,1},{1... | collective-permute-start | bytes 983048 | tf_op jit(solution)/shard_map/ppermute | solution.py:255
  44.6 3.6 %collective-permute-done.16.refs_6_ = f32[640,128]{1,0:T(8,128)S(1)} collective-permute-done((f32[640,128]{1,0:T(8,128)S(1)}, f32[640,128]{1,0:T(8,128)S(1)}, u32[]{:S(2)}, u32[]{:S(2)}) %collective-permute-start.16) | collective-permute-done | bytes 327712 | tf_op jit(solution)/shard_map/ppermute | solution.py:231
  48.3 2.0 %collective-permute-start.17 = (f32[320,128]{1,0:T(8,128)S(1)}, f32[320,128]{1,0:T(8,128)S(1)}, u32[]{:S(2)}, u32[]{:S(2)}) collective-permute-start(f32[320,128]{1,0:T(8,128)S(1)} %slice.32), channel_id=1, source_target_pairs={{0,8},{8,16},{16,24},{24,28},{28,20},{20,12},{12,4},{4,0},{1,9},{9... | collective-permute-start | bytes 491528 | tf_op jit(solution)/shard_map/ppermute | solution.py:235
  52.5 2.3 %collective-permute-done.17.refs_4_ = f32[320,128]{1,0:T(8,128)S(1)} collective-permute-done((f32[320,128]{1,0:T(8,128)S(1)}, f32[320,128]{1,0:T(8,128)S(1)}, u32[]{:S(2)}, u32[]{:S(2)}) %collective-permute-start.17) | collective-permute-done | bytes 163872 | tf_op jit(solution)/shard_map/ppermute | solution.py:235
  54.8 3.6 %collective-permute-done.18.refs_5_ = f32[320,128]{1,0:T(8,128)S(1)} collective-permute-done((f32[320,128]{1,0:T(8,128)S(1)}, f32[320,128]{1,0:T(8,128)S(1)}, u32[]{:S(2)}, u32[]{:S(2)}) %collective-permute-start.18) | collective-permute-done | bytes 163872 | tf_op jit(solution)/shard_map/ppermute | solution.py:236
  58.4 2.9 %forward_products.1 = (f32[1280,128]{1,0:T(8,128)S(1)}, f32[1280,128]{1,0:T(8,128)S(1)}) custom-call(s32[1,1]{1,0:T(1,128)S(6)} %copy.8.live, s32[1,640]{1,0:T(1,128)S(1)} %copy-done.3, s32[1,640]{1,0:T(1,128)S(1)} %copy-done.4, bf16[40960,128]{1,0:T(8,128)(2,1)S(1)} %split_tiles.1.parts, f32[640,128]{1,0:T(8,128)S(1)} %copy-done.1, ...), custom_call_target="tpu_custom_call" | custom-call | bytes 26214400 | tf_op jit(solution)/shard_map/forward_products/pallas_call | solution.py:163
  61.4 5.1 %collective-permute-start.9 = (f32[640,128]{1,0:T(8,128)S(1)}, f32[640,128]{1,0:T(8,128)S(1)}, u32[]{:S(2)}, u32[]{:S(2)}) collective-permute-start(f32[640,128]{1,0:T(8,128)S(1)} %add.36), channel_id=1, source_target_pairs={{8,0},{16,8},{24,16},{28,24},{20,28},{12,20},{4,12},{0,4},{9,1},{1... | collective-permute-start | bytes 983048 | tf_op jit(solution)/shard_map/ppermute | solution.py:255
  66.6 7.5 %collective-permute-done.9 = f32[640,128]{1,0:T(8,128)S(1)} collective-permute-done((f32[640,128]{1,0:T(8,128)S(1)}, f32[640,128]{1,0:T(8,128)S(1)}, u32[]{:S(2)}, u32[]{:S(2)}) %collective-permute-start.9) | collective-permute-done | bytes 327712 | tf_op jit(solution)/shard_map/ppermute | solution.py:255
  74.1 2.5 %collective-permute-start.10 = (f32[640,128]{1,0:T(8,128)S(1)}, f32[640,128]{1,0:T(8,128)S(1)}, u32[]{:S(2)}, u32[]{:S(2)}) collective-permute-start(f32[640,128]{1,0:T(8,128)S(1)} %add.37), channel_id=1, source_target_pairs={{8,0},{16,8},{24,16},{28,24},{20,28},{12,20},{4,12},{0,4},{9,1},{1... | collective-permute-start | bytes 983048 | tf_op jit(solution)/shard_map/ppermute | solution.py:255
  77.6 6.7 %collective-permute-done.10.refs_2_ = f32[640,128]{1,0:T(8,128)S(1)} collective-permute-done((f32[640,128]{1,0:T(8,128)S(1)}, f32[640,128]{1,0:T(8,128)S(1)}, u32[]{:S(2)}, u32[]{:S(2)}) %collective-permute-start.10) | collective-permute-done | bytes 327712 | tf_op jit(solution)/shard_map/ppermute | solution.py:255
  84.4 1.5 %collective-permute-done.6.refs_1_ = f32[640,128]{1,0:T(8,128)S(1)} collective-permute-done((f32[640,128]{1,0:T(8,128)S(1)}, f32[640,128]{1,0:T(8,128)S(1)}, u32[]{:S(2)}, u32[]{:S(2)}) %collective-permute-start.6) | collective-permute-done | bytes 327712 | tf_op jit(solution)/shard_map/ppermute | solution.py:254
  87.5 2.2 %unpack.1 = (f32[8,5120]{1,0:T(8,128)}, f32[8,5120]{1,0:T(8,128)}) custom-call(f32[640,128]{1,0:T(8,128)} %copy-done.2, f32[640,128]{1,0:T(8,128)} %copy-done.8, f32[640,128]{1,0:T(8,128)} %copy-done.7, f32[640,128]{1,0:T(8,128)} %get-tuple-element.35.refs_3_, f32[640,128]{1,0:T(8,128)} %copy-done.9), custom_call_target="tpu_custom_call" | custom-call | tf_op jit(solution)/shard_map/unpack/pallas_call | solution.py:268
  (56 shorter events, 7.9 us)
Async XLA Ops:
  3.8 10.9 %collective-permute-start = (f32[640,128]{1,0:T(8,128)}, f32[640,128]{1,0:T(8,128)S(1)}, u32[]{:S(2)}, u32[]{:S(2)}) collective-permute-start(f32[640,128]{1,0:T(8,128)} %get-tuple-element.20.refs_0_), channel_id=1, source_target_pairs={{0,2},{1,3},{2,0},{3,1},{4,6},{5,7},{6,4},{7,5},{8,10},{9,11},{10,... | collective-permute-start | bytes 983048 | tf_op jit(solution)/shard_map/ppermute | solution.py:223
  6.8 9.4 %collective-permute-start.14 = (f32[640,128]{1,0:T(8,128)}, f32[640,128]{1,0:T(8,128)S(1)}, u32[]{:S(2)}, u32[]{:S(2)}) collective-permute-start(f32[640,128]{1,0:T(8,128)} %get-tuple-element.20.refs_0_), channel_id=1, source_target_pairs={{0,8},{8,16},{16,24},{24,28},{28,20},{20,12},{12,4},{4,0},{1,9},{9... | collective-permute-start | bytes 983048 | tf_op jit(solution)/shard_map/ppermute | solution.py:231
  8.4 9.4 %collective-permute-start.11 = (f32[640,128]{1,0:T(8,128)}, f32[640,128]{1,0:T(8,128)S(1)}, u32[]{:S(2)}, u32[]{:S(2)}) collective-permute-start(f32[640,128]{1,0:T(8,128)} %get-tuple-element.20.refs_0_), channel_id=1, source_target_pairs={{8,0},{16,8},{24,16},{28,24},{20,28},{12,20},{4,12},{0,4},{9,1},{1... | collective-permute-start | bytes 983048 | tf_op jit(solution)/shard_map/ppermute | solution.py:232
  8.8 21.4 %collective-permute-start.1 = (f32[640,128]{1,0:T(8,128)}, f32[640,128]{1,0:T(8,128)S(1)}, u32[]{:S(2)}, u32[]{:S(2)}) collective-permute-start(f32[640,128]{1,0:T(8,128)} %get-tuple-element.20.refs_0_), channel_id=1, source_target_pairs={{0,1},{1,0},{2,3},{3,2},{4,5},{5,4},{6,7},{7,6},{8,9},{9,8},{10,11... | collective-permute-start | bytes 983048 | tf_op jit(solution)/shard_map/ppermute | solution.py:225
  14.7 15.5 %collective-permute-start.2 = (f32[640,128]{1,0:T(8,128)S(1)}, f32[640,128]{1,0:T(8,128)S(1)}, u32[]{:S(2)}, u32[]{:S(2)}) collective-permute-start(f32[640,128]{1,0:T(8,128)S(1)} %collective-permute-done.refs_1_), channel_id=1, source_target_pairs={{0,1},{1,0},{2,3},{3,2},{4,5},{5,4},{6,7},{7,6},{8,9},{9,8},{10,11... | collective-permute-start | bytes 983048 | tf_op jit(solution)/shard_map/ppermute | solution.py:225
  16.2 21.3 %collective-permute-start.15 = (f32[640,128]{1,0:T(8,128)S(1)}, f32[640,128]{1,0:T(8,128)S(1)}, u32[]{:S(2)}, u32[]{:S(2)}) collective-permute-start(f32[640,128]{1,0:T(8,128)S(1)} %collective-permute-done.14.refs_8_), channel_id=1, source_target_pairs={{0,8},{8,16},{16,24},{24,28},{28,20},{20,12},{12,4},{4,0},{1,9},{9... | collective-permute-start | bytes 983048 | tf_op jit(solution)/shard_map/ppermute | solution.py:231
  17.7 21.4 %collective-permute-start.12 = (f32[640,128]{1,0:T(8,128)S(1)}, f32[640,128]{1,0:T(8,128)S(1)}, u32[]{:S(2)}, u32[]{:S(2)}) collective-permute-start(f32[640,128]{1,0:T(8,128)S(1)} %collective-permute-done.11.refs_1_), channel_id=1, source_target_pairs={{8,0},{16,8},{24,16},{28,24},{20,28},{12,20},{4,12},{0,4},{9,1},{1... | collective-permute-start | bytes 983048 | tf_op jit(solution)/shard_map/ppermute | solution.py:232
  22.2 8.1 %copy-start.6 = (s32[1,640]{1,0:T(1,128)S(1)}, s32[1,640]{1,0:T(1,128)}, u32[]{:S(2)}) copy-start(s32[1,640]{1,0:T(1,128)} %get-tuple-element.19.sidx) | copy-start | bytes 7684
  30.2 28.2 %copy-start.3 = (s32[1,640]{1,0:T(1,128)S(1)}, s32[1,640]{1,0:T(1,128)}, u32[]{:S(2)}) copy-start(s32[1,640]{1,0:T(1,128)} %get-tuple-element.30.gidx) | copy-start | bytes 7684
  30.2 28.1 %copy-start.4 = (s32[1,640]{1,0:T(1,128)S(1)}, s32[1,640]{1,0:T(1,128)}, u32[]{:S(2)}) copy-start(s32[1,640]{1,0:T(1,128)} %get-tuple-element.31.sidx) | copy-start | bytes 7684
  33.5 8.6 %collective-permute-start.7 = (f32[320,128]{1,0:T(8,128)S(1)}, f32[320,128]{1,0:T(8,128)S(1)}, u32[]{:S(2)}, u32[]{:S(2)}) collective-permute-start(f32[320,128]{1,0:T(8,128)S(1)} %get-tuple-element.29), channel_id=1, source_target_pairs={{8,0},{16,8},{24,16},{28,24},{20,28},{12,20},{4,12},{0,4},{9,1},{1... | collective-permute-start | bytes 491528 | tf_op jit(solution)/shard_map/ppermute | solution.py:246
  37.5 14.1 %collective-permute-start.3 = (f32[320,128]{1,0:T(8,128)S(1)}, f32[320,128]{1,0:T(8,128)S(1)}, u32[]{:S(2)}, u32[]{:S(2)}) collective-permute-start(f32[320,128]{1,0:T(8,128)S(1)} %get-tuple-element.25), channel_id=1, source_target_pairs={{0,8},{8,16},{16,24},{24,28},{28,20},{20,12},{12,4},{4,0},{1,9},{9... | collective-permute-start | bytes 491528 | tf_op jit(solution)/shard_map/ppermute | solution.py:245
  37.5 10.8 %collective-permute-start.16 = (f32[640,128]{1,0:T(8,128)S(1)}, f32[640,128]{1,0:T(8,128)S(1)}, u32[]{:S(2)}, u32[]{:S(2)}) collective-permute-start(f32[640,128]{1,0:T(8,128)S(1)} %collective-permute-done.15.refs_7_), channel_id=1, source_target_pairs={{0,8},{8,16},{16,24},{24,28},{28,20},{20,12},{12,4},{4,0},{1,9},{9... | collective-permute-start | bytes 983048 | tf_op jit(solution)/shard_map/ppermute | solution.py:231
  39.2 11.1 %collective-permute-start.13 = (f32[640,128]{1,0:T(8,128)S(1)}, f32[640,128]{1,0:T(8,128)S(1)}, u32[]{:S(2)}, u32[]{:S(2)}) collective-permute-start(f32[640,128]{1,0:T(8,128)S(1)} %collective-permute-done.12.refs_2_), channel_id=1, source_target_pairs={{8,0},{16,8},{24,16},{28,24},{20,28},{12,20},{4,12},{0,4},{9,1},{1... | collective-permute-start | bytes 983048 | tf_op jit(solution)/shard_map/ppermute | solution.py:232
  42.1 19.2 %collective-permute-start.8 = (f32[640,128]{1,0:T(8,128)S(1)}, f32[640,128]{1,0:T(8,128)S(1)}, u32[]{:S(2)}, u32[]{:S(2)}) collective-permute-start(f32[640,128]{1,0:T(8,128)S(1)} %pad_maximum_fusion.1), channel_id=1, source_target_pairs={{8,0},{16,8},{24,16},{28,24},{20,28},{12,20},{4,12},{0,4},{9,1},{1... | collective-permute-start | bytes 983048 | tf_op jit(solution)/shard_map/ppermute | solution.py:255
  48.3 6.5 %collective-permute-start.17 = (f32[320,128]{1,0:T(8,128)S(1)}, f32[320,128]{1,0:T(8,128)S(1)}, u32[]{:S(2)}, u32[]{:S(2)}) collective-permute-start(f32[320,128]{1,0:T(8,128)S(1)} %slice.32), channel_id=1, source_target_pairs={{0,8},{8,16},{16,24},{24,28},{28,20},{20,12},{12,4},{4,0},{1,9},{9... | collective-permute-start | bytes 491528 | tf_op jit(solution)/shard_map/ppermute | solution.py:235
  50.3 8.1 %collective-permute-start.18 = (f32[320,128]{1,0:T(8,128)S(1)}, f32[320,128]{1,0:T(8,128)S(1)}, u32[]{:S(2)}, u32[]{:S(2)}) collective-permute-start(f32[320,128]{1,0:T(8,128)S(1)} %slice.33), channel_id=1, source_target_pairs={{8,0},{16,8},{24,16},{28,24},{20,28},{12,20},{4,12},{0,4},{9,1},{1... | collective-permute-start | bytes 491528 | tf_op jit(solution)/shard_map/ppermute | solution.py:236
  51.7 14.8 %collective-permute-start.4 = (f32[640,128]{1,0:T(8,128)S(1)}, f32[640,128]{1,0:T(8,128)S(1)}, u32[]{:S(2)}, u32[]{:S(2)}) collective-permute-start(f32[640,128]{1,0:T(8,128)S(1)} %pad_maximum_fusion), channel_id=1, source_target_pairs={{0,8},{8,16},{16,24},{24,28},{28,20},{20,12},{12,4},{4,0},{1,9},{9... | collective-permute-start | bytes 983048 | tf_op jit(solution)/shard_map/ppermute | solution.py:254
  61.3 15.5 %collective-permute-start.19 = (f32[1280,128]{1,0:T(8,128)S(1)}, f32[1280,128]{1,0:T(8,128)S(1)}, u32[]{:S(2)}, u32[]{:S(2)}) collective-permute-start(f32[1280,128]{1,0:T(8,128)S(1)} %get-tuple-element.33), channel_id=1, source_target_pairs={{0,1},{1,0},{2,3},{3,2},{4,5},{5,4},{6,7},{7,6},{8,9},{9,8},{10,11... | collective-permute-start | bytes 1966088 | tf_op jit(solution)/shard_map/ppermute | solution.py:258
  61.4 12.7 %collective-permute-start.9 = (f32[640,128]{1,0:T(8,128)S(1)}, f32[640,128]{1,0:T(8,128)S(1)}, u32[]{:S(2)}, u32[]{:S(2)}) collective-permute-start(f32[640,128]{1,0:T(8,128)S(1)} %add.36), channel_id=1, source_target_pairs={{8,0},{16,8},{24,16},{28,24},{20,28},{12,20},{4,12},{0,4},{9,1},{1... | collective-permute-start | bytes 983048 | tf_op jit(solution)/shard_map/ppermute | solution.py:255
  66.5 10.1 %collective-permute-start.5 = (f32[640,128]{1,0:T(8,128)S(1)}, f32[640,128]{1,0:T(8,128)S(1)}, u32[]{:S(2)}, u32[]{:S(2)}) collective-permute-start(f32[640,128]{1,0:T(8,128)S(1)} %add.33), channel_id=1, source_target_pairs={{0,8},{8,16},{16,24},{24,28},{28,20},{20,12},{12,4},{4,0},{1,9},{9... | collective-permute-start | bytes 983048 | tf_op jit(solution)/shard_map/ppermute | solution.py:254
  74.1 10.2 %collective-permute-start.10 = (f32[640,128]{1,0:T(8,128)S(1)}, f32[640,128]{1,0:T(8,128)S(1)}, u32[]{:S(2)}, u32[]{:S(2)}) collective-permute-start(f32[640,128]{1,0:T(8,128)S(1)} %add.37), channel_id=1, source_target_pairs={{8,0},{16,8},{24,16},{28,24},{20,28},{12,20},{4,12},{0,4},{9,1},{1... | collective-permute-start | bytes 983048 | tf_op jit(solution)/shard_map/ppermute | solution.py:255
  76.7 9.1 %collective-permute-start.6 = (f32[640,128]{1,0:T(8,128)S(1)}, f32[640,128]{1,0:T(8,128)S(1)}, u32[]{:S(2)}, u32[]{:S(2)}) collective-permute-start(f32[640,128]{1,0:T(8,128)S(1)} %add.34), channel_id=1, source_target_pairs={{0,8},{8,16},{16,24},{24,28},{28,20},{20,12},{12,4},{4,0},{1,9},{9... | collective-permute-start | bytes 983048 | tf_op jit(solution)/shard_map/ppermute | solution.py:254
  77.6 9.1 %collective-permute-start.20 = (f32[640,128]{1,0:T(8,128)S(1)}, f32[640,128]{1,0:T(8,128)S(1)}, u32[]{:S(2)}, u32[]{:S(2)}) collective-permute-start(f32[640,128]{1,0:T(8,128)S(1)} %get-tuple-element.34), channel_id=1, source_target_pairs={{0,2},{1,3},{2,0},{3,1},{4,6},{5,7},{6,4},{7,5},{8,10},{9,11},{10,... | collective-permute-start | bytes 983048 | tf_op jit(solution)/shard_map/ppermute | solution.py:262
  (7 other events, 25.0 us)

commit v3 on v2

--- a/solution.py
+++ b/solution.py
@@ -12,6 +12,7 @@
 LANES = 128
 PITCH = 40
 PAIR = 32
+PIECES = 16
 VMEM = pl.BlockSpec(memory_space=pltpu.VMEM)
 SMEM = pl.BlockSpec(memory_space=pltpu.SMEM)
 
@@ -58,16 +59,46 @@
     return lax.broadcasted_iota(jnp.int32, (rows, LANES), 1) < BLK
 
 
-def split_kernel(tiles, parts, turned):
+def turn_kernel(tiles, turned, room, sems):
     half = BLK // 2
-
-    def turn(j, carry):
-        a = tiles[pl.ds(pl.multiple_of(j * BLK, BLK), BLK), :]
-        b = tiles[pl.ds(pl.multiple_of((j + half) * BLK, BLK), BLK), :]
-        turned[pl.ds(j, LANES, stride=PITCH), :] = jnp.concatenate([a, b], axis=0).T
-        return carry
-
-    lax.fori_loop(0, half, turn, 0, unroll=32)
+    slots = tiles.shape[1]
+    piece = BLK * BLK // PIECES
+    mine = PIECES // 2
+
+    def load(p):
+        at = pl.ds(p * piece, piece)
+        return pltpu.make_async_copy(tiles.at[at], room.at[at], sems.at[p])
+
+    for p in range(mine):
+        load(p).start()
+        load(p + mine).start()
+    for p in range(mine):
+        load(p).wait()
+        load(p + mine).wait()
+        for j in range(p * half // mine, (p + 1) * half // mine):
+            for k in range(slots // LANES):
+                lanes = slice(k * LANES, (k + 1) * LANES)
+                a = room[j * BLK:(j + 1) * BLK, lanes]
+                b = room[(j + half) * BLK:(j + half + 1) * BLK, lanes]
+                turned[pl.ds(k * LANES * PITCH + j, LANES, stride=PITCH), :] = jnp.concatenate([a, b], axis=0).T
+
+
+def turn_tiles(tiles):
+    slots = tiles.shape[1]
+    return pl.pallas_call(
+        turn_kernel,
+        out_shape=pltpu.VMEM((slots * PITCH, LANES), jnp.float32),
+        in_specs=[pl.BlockSpec(memory_space=pltpu.HBM)],
+        out_specs=VMEM,
+        scratch_shapes=[pltpu.VMEM(tiles.shape, jnp.float32), pltpu.SemaphoreType.DMA((PIECES,))],
+        compiler_params=pltpu.CompilerParams(vmem_limit_bytes=14 << 20),
+        cost_estimate=pl.CostEstimate(flops=0, bytes_accessed=1 << 20, transcendentals=0),
+        name="turn_tiles",
+    )(pltpu.with_memory_space_constraint(tiles, pltpu.HBM))
+
+
+def split_kernel(turned, parts):
+    half = BLK // 2
     first = first_half(half)
 
     def split(s, carry):
@@ -80,25 +111,24 @@
         parts[pl.ds(pl.multiple_of(s * BLK, BLK), BLK), :] = both
         return carry
 
-    lax.fori_loop(0, LANES, split, 0, unroll=32)
-
-
-def split_tiles(tiles):
-    slots = tiles.shape[1]
+    lax.fori_loop(0, turned.shape[0] // PITCH, split, 0, unroll=32)
+
+
+def split_tiles(turned):
+    slots = turned.shape[0] // PITCH
     return pl.pallas_call(
         split_kernel,
         out_shape=jax.ShapeDtypeStruct((slots * BLK, LANES), jnp.bfloat16),
-        grid=(slots // LANES,),
-        in_specs=[pl.BlockSpec((BLK * BLK, LANES), lambda s: (0, s))],
-        out_specs=pl.BlockSpec((LANES * BLK, LANES), lambda s: (s, 0)),
-        scratch_shapes=[pltpu.VMEM((LANES * PITCH, LANES), jnp.float32)],
-        compiler_params=pltpu.CompilerParams(vmem_limit_bytes=16 << 20),
-        cost_estimate=pl.CostEstimate(flops=0, bytes_accessed=30 << 20, transcendentals=0),
+        in_specs=[VMEM],
+        out_specs=VMEM,
+        compiler_params=pltpu.CompilerParams(vmem_limit_bytes=4 << 20),
+        cost_estimate=pl.CostEstimate(flops=0, bytes_accessed=1 << 20, transcendentals=0),
         name="split_tiles",
-    )(tiles)
-
-
-def tile_kernel(forward, nsrc, group, live, gidx, sidx, parts, *refs):
+    )(turned)
+
+
+def tile_kernel(forward, nsrc, group, live, gidx, sidx, *refs):
+    parts, refs = refs[0], refs[1:]
     srcs, outs, pairs, acc = refs[:nsrc], refs[nsrc:-2], refs[-2], refs[-1]
     first8 = first_half(SUB)
     at = 0
@@ -170,7 +200,7 @@
             pltpu.VMEM(((sum(out_blocks) + 1) * SUB, LANES), jnp.float32),
         ],
         compiler_params=pltpu.CompilerParams(vmem_limit_bytes=20 << 20),
-        cost_estimate=pl.CostEstimate(flops=0, bytes_accessed=25 << 20, transcendentals=0),
+        cost_estimate=pl.CostEstimate(flops=0, bytes_accessed=1 << 20, transcendentals=0),
         name="forward_products" if forward else "mirrored_products",
     )(live, gidx, sidx, parts, *srcs)
 
@@ -218,43 +248,62 @@
     core = [(k, k ^ 1) for k in range(ncol)]
     up = [(2 * m + k, 2 * ((m + 1) % major) + k) for m in range(major) for k in range(2)]
 
+    half = nrow // 2
+    mid = rows_each // 2
+    hold = lax.optimization_barrier
+
     held = [xb]
-    for _ in range(major - 1):
-        held.append(lax.ppermute(held[-1], "col", up))
-    held = [held[0]] + held[:0:-1]
-    near_rows = held + [lax.ppermute(h, "col", core) for h in held]
-
+    near_core = [lax.ppermute(xb, "col", core)]
     near_cols = [None] * nrow
     near_cols[0] = xb
     left = right = xb
-    for k in range(1, nrow // 2):
+    turned = turn_tiles(tiles)
+    parts = None
+    col_parts = None
+    for k in range(1, half):
         left = lax.ppermute(left, "row", cw)
         right = lax.ppermute(right, "row", ccw)
+        if k < major:
+            held.append(lax.ppermute(held[-1], "col", up))
+        if k == 1:
+            left, right, turned = hold((left, right, turned))
+        if k < major:
+            near_core.append(lax.ppermute(held[-1], "col", core))
         near_cols[nrow - k], near_cols[k] = left, right
-    mid = rows_each // 2
-    left = lax.ppermute(left[:mid], "row", cw)
-    right = lax.ppermute(right[mid:], "row", ccw)
-    near_cols[nrow // 2:nrow // 2 + 1] = [left, right]
-
-    parts = split_tiles(tiles)
+        if k == 2:
+            parts = split_tiles(turned)
+            left, right, parts = hold((left, right, parts))
+            near_cols[nrow - k], near_cols[k] = left, right
+    for k in range(half, major):
+        held.append(lax.ppermute(held[-1], "col", up))
+        near_core.append(lax.ppermute(held[-1], "col", core))
+    near_rows = [held[0]] + held[:0:-1] + [near_core[0]] + near_core[:0:-1]
     col_parts = tile_products(
-        False, live_counts, grows, scols, parts, near_rows, [blocks] * (nrow // 2) + [blocks // 2] * 2 + [blocks] * (nrow // 2 - 1)
+        False, live_counts, grows, scols, parts, near_rows,
+        [blocks] * half + [blocks // 2] * 2 + [blocks] * (half - 1),
     )
-    first, last = col_parts[nrow // 2], col_parts[nrow // 2 + 1]
-    col_parts = list(col_parts[:nrow // 2]) + [None] + list(col_parts[nrow // 2 + 2:])
+    left, right, col_parts = hold((left, right, col_parts))
+    near_cols[half + 1], near_cols[half - 1] = left, right
+    near_cols[half:half + 1] = [lax.ppermute(left[:mid], "row", cw), lax.ppermute(right[mid:], "row", ccw)]
+    first, last = col_parts[half], col_parts[half + 1]
+    col_parts = list(col_parts[:half]) + [None] + list(col_parts[half + 2:])
+
     left = lax.ppermute(first, "row", cw)
     right = lax.ppermute(last, "row", ccw)
-    for k in range(nrow // 2 - 1, 0, -1):
+    left, right, near_cols = hold((left, right, near_cols))
+    own, other = tile_products(True, live_counts, gcols, srows, parts, near_cols, [major * blocks] * 2)
+    for k in range(half - 1, 0, -1):
         a, b = col_parts[k], col_parts[nrow - k]
-        if k == nrow // 2 - 1:
+        if k == half - 1:
             a = jnp.concatenate([a[:mid] + left, a[mid:]], axis=0)
             b = jnp.concatenate([b[:mid], b[mid:] + right], axis=0)
         else:
             a, b = a + left, b + right
         left = lax.ppermute(a, "row", cw)
         right = lax.ppermute(b, "row", ccw)
-
-    own, other = tile_products(True, live_counts, gcols, srows, parts, near_cols, [major * blocks] * 2)
+        if k == half - 1:
+            left, right, own, other = hold((left, right, own, other))
+
     own = own + lax.ppermute(other, "col", core)
     part = own[(major - 1) * rows_each:] if major > 1 else None
     terms = [col_parts[0], left, right, own[:rows_each]]
@@ -270,6 +319,7 @@
         out_shape=(out_shape, out_shape),
         in_specs=[VMEM] * len(terms),
         out_specs=(VMEM, VMEM),
+        compiler_params=pltpu.CompilerParams(vmem_limit_bytes=4 << 20),
         name="unpack",
     )(*terms)
 

time: 90.3 us -> 76 us (0.84)
  local copies, waits for them, and re-layouts: 6.24 us -> 0.09 us
  starting transfers between devices: 27.6 us -> 21.8 us
  waiting for transfers between devices: 36 us -> 33.7 us
    ppermute x3, starting transfers between devices: 10.1 us -> 1.24 us  [body(): right = lax.ppermute(b, 'row', ccw)]
    ppermute x1, waiting for transfers between devices: 5.89 us -> 0.01 us  [body(): held.append(lax.ppermute(held[-1], 'col', up))]
    unnamed x20 -> x10, local copies, waits for them, and re-layouts: 5.45 us -> 0.02 us
    pallas_call x0 -> x1, Pallas kernels: none -> 4.86 us  [turn_tiles(): pl.pallas_call(turn_kernel, out_shape=pltpu.VMEM((slots * PITCH, LANES),...]
    ppermute x3, waiting for transfers between devices: 0.01 us -> 4.42 us  [body(): right = lax.ppermute(right, 'row', ccw)]
    ppermute x3, starting transfers between devices: 0.91 us -> 5.15 us  [body(): left = lax.ppermute(a, 'row', cw)]
    pallas_call x1, Pallas kernels: 8.02 us -> 4.25 us  [split_tiles(): pl.pallas_call(split_kernel, out_shape=jax.ShapeDtypeStruct((slots * BLK,...]
    ppermute x1, starting transfers between devices: 4.03 us -> 0.45 us  [body(): right = lax.ppermute(last, 'row', ccw)]
  transfers between devices with their start and end apart: 21 -> 21, of which waited for: 10 -> 15; matrix products, arithmetic and copies ran while one was open for 1% -> 0% of each run, Pallas kernels for 15% -> 19%
where the time goes in v3:
time: 76 us; the launch traced here: 75.2 us
  waiting for transfers between devices  33.7 us (44%)
  starting transfers between devices  21.8 us (29%)
  Pallas kernels  17.3 us (23%)
  between operations  1.46 us (2%)
  other arithmetic  0.99 us (1%)
    ppermute x3, waiting for transfers between devices, body(): right = lax.ppermute(b, 'row', ccw)  15.6 us
    ppermute x3, starting transfers between devices, body(): left = lax.ppermute(left, 'row', cw)  6.18 us
    pallas_call x2, Pallas kernels, tile_products(): pl.pallas_call(functools.partial(tile_kernel, forward, len(srcs), 4 if fo...  5.34 us
    ppermute x3, starting transfers between devices, body(): left = lax.ppermute(a, 'row', cw)  5.15 us
    ppermute x3, waiting for transfers between devices, body(): left = lax.ppermute(left, 'row', cw)  4.91 us
    pallas_call x1, Pallas kernels, turn_tiles(): pl.pallas_call(turn_kernel, out_shape=pltpu.VMEM((slots * PITCH, LANES),...  4.86 us
    ppermute x3, waiting for transfers between devices, body(): right = lax.ppermute(right, 'row', ccw)  4.42 us
    pallas_call x1, Pallas kernels, split_tiles(): pl.pallas_call(split_kernel, out_shape=jax.ShapeDtypeStruct((slots * BLK,...  4.25 us
  transfers between devices with their start and end apart: 21, of which 15 were waited for; matrix products, arithmetic and copies ran while one was open for 0% of the time, Pallas kernels for 19%

profile of v3, /device:TPU:0, one launch (start us, length us, event | category | flops | bytes accessed | tf_op | source)
XLA Modules:
  0.0 75.2 jit_solution(5021623124375596925)
XLA Ops:
  2.0 1.9 %pack.1 = (f32[640,128]{1,0:T(8,128)}, s32[1,640]{1,0:T(1,128)}, s32[1,640]{1,0:T(1,128)}, s32[1,640]{1,0:T(1,128)}, s32[1,640]{1,0:T(1,128)}) custom-call(s32[3]{0:T(128)} %pad_add_fusion.place, s32[1,1]{1,0:T(1,128)S(6)} %copy.8.live, f32[8,5120]{1,0:T(8,128)} %it.1, f32[8,5120]{1,0:T(8,128)} %res.1, s32[1,640]{1,0:T(1,128)} %bitcast.11, s32[1,640]{1,0:T(1,128)} %bitcast.12), custom_call_target="tpu_custom_call" | custom-call | tf_op jit(solution)/shard_map/pack/pallas_call | solution.py:238
  3.8 3.0 %collective-permute-start = (f32[640,128]{1,0:T(8,128)}, f32[640,128]{1,0:T(8,128)S(1)}, u32[]{:S(2)}, u32[]{:S(2)}) collective-permute-start(f32[640,128]{1,0:T(8,128)} %get-tuple-element.81.refs_1_), channel_id=1, source_target_pairs={{0,8},{8,16},{16,24},{24,28},{28,20},{20,12},{12,4},{4,0},{1,9},{9... | collective-permute-start | bytes 983048 | tf_op jit(solution)/shard_map/ppermute | solution.py:264
  6.9 2.0 %collective-permute-start.6 = (f32[640,128]{1,0:T(8,128)}, f32[640,128]{1,0:T(8,128)S(1)}, u32[]{:S(2)}, u32[]{:S(2)}) collective-permute-start(f32[640,128]{1,0:T(8,128)} %get-tuple-element.81.refs_1_), channel_id=1, source_target_pairs={{0,2},{1,3},{2,0},{3,1},{4,6},{5,7},{6,4},{7,5},{8,10},{9,11},{10,... | collective-permute-start | bytes 983048 | tf_op jit(solution)/shard_map/ppermute | solution.py:267
  8.8 4.9 %turn_tiles.1.turned = f32[25600,128]{1,0:T(8,128)S(1)} custom-call(f32[4096,640]{1,0:T(8,128)} %bitcast.10), custom_call_target="tpu_custom_call" | custom-call | bytes 1048576 | tf_op jit(solution)/shard_map/turn_tiles/pallas_call | solution.py:88
  14.7 1.5 %collective-permute-done.1.refs_2_ = f32[640,128]{1,0:T(8,128)S(1)} collective-permute-done((f32[640,128]{1,0:T(8,128)}, f32[640,128]{1,0:T(8,128)S(1)}, u32[]{:S(2)}, u32[]{:S(2)}) %collective-permute-start.1) | collective-permute-done | bytes 327712 | tf_op jit(solution)/shard_map/ppermute | solution.py:265
  16.2 1.6 %collective-permute-start.2 = (f32[640,128]{1,0:T(8,128)S(1)}, f32[640,128]{1,0:T(8,128)S(1)}, u32[]{:S(2)}, u32[]{:S(2)}) collective-permute-start(f32[640,128]{1,0:T(8,128)S(1)} %collective-permute-done.refs_9_), channel_id=1, source_target_pairs={{0,8},{8,16},{16,24},{24,28},{28,20},{20,12},{12,4},{4,0},{1,9},{9... | collective-permute-start | bytes 983048 | tf_op jit(solution)/shard_map/ppermute | solution.py:264
  18.3 4.2 %split_tiles.1.refs_0_ = bf16[40960,128]{1,0:T(8,128)(2,1)S(1)} custom-call(f32[25600,128]{1,0:T(8,128)S(1)} %turn_tiles.1.turned), custom_call_target="tpu_custom_call" | custom-call | bytes 1048576 | tf_op jit(solution)/shard_map/split_tiles/pallas_call | solution.py:119
  23.1 1.4 %collective-permute-done.2.refs_8_ = f32[640,128]{1,0:T(8,128)S(1)} collective-permute-done((f32[640,128]{1,0:T(8,128)S(1)}, f32[640,128]{1,0:T(8,128)S(1)}, u32[]{:S(2)}, u32[]{:S(2)}) %collective-permute-start.2) | collective-permute-done | bytes 327712 | tf_op jit(solution)/shard_map/ppermute | solution.py:264
  25.8 1.6 %collective-permute-start.4 = (f32[640,128]{1,0:T(8,128)S(1)}, f32[640,128]{1,0:T(8,128)S(1)}, u32[]{:S(2)}, u32[]{:S(2)}) collective-permute-start(f32[640,128]{1,0:T(8,128)S(1)} %collective-permute-done.2.refs_8_), channel_id=1, source_target_pairs={{0,8},{8,16},{16,24},{24,28},{28,20},{20,12},{12,4},{4,0},{1,9},{9... | collective-permute-start | bytes 983048 | tf_op jit(solution)/shard_map/ppermute | solution.py:264
  27.9 2.4 %mirrored_products.1 = (f32[640,128]{1,0:T(8,128)S(1)}, f32[640,128]{1,0:T(8,128)S(1)}, f32[640,128]{1,0:T(8,128)S(1)}, f32[640,128]{1,0:T(8,128)S(1)}, f32[320,...) custom-call(s32[1,1]{1,0:T(1,128)S(6)} %copy.8.live, ...), custom_call_target="tpu_custom_call" | custom-call | bytes 1048576 | tf_op jit(solution)/shard_map/mirrored_products/pallas_call | solution.py:193
  30.3 2.6 %collective-permute-done.4.refs_7_ = f32[640,128]{1,0:T(8,128)S(1)} collective-permute-done((f32[640,128]{1,0:T(8,128)S(1)}, f32[640,128]{1,0:T(8,128)S(1)}, u32[]{:S(2)}, u32[]{:S(2)}) %collective-permute-start.4) | collective-permute-done | bytes 327712 | tf_op jit(solution)/shard_map/ppermute | solution.py:264
  32.9 1.6 %collective-permute-done.5.refs_4_ = f32[640,128]{1,0:T(8,128)S(1)} collective-permute-done((f32[640,128]{1,0:T(8,128)S(1)}, f32[640,128]{1,0:T(8,128)S(1)}, u32[]{:S(2)}, u32[]{:S(2)}) %collective-permute-start.5) | collective-permute-done | bytes 327712 | tf_op jit(solution)/shard_map/ppermute | solution.py:265
  34.5 1.5 %collective-permute-start.11 = (f32[320,128]{1,0:T(8,128)S(1)}, f32[320,128]{1,0:T(8,128)S(1)}, u32[]{:S(2)}, u32[]{:S(2)}) collective-permute-start(f32[320,128]{1,0:T(8,128)S(1)} %slice.25), channel_id=1, source_target_pairs={{0,8},{8,16},{16,24},{24,28},{28,20},{20,12},{12,4},{4,0},{1,9},{9... | collective-permute-start | bytes 491528 | tf_op jit(solution)/shard_map/ppermute | solution.py:287
  37.1 1.6 %collective-permute-start.9 = (f32[320,128]{1,0:T(8,128)S(1)}, f32[320,128]{1,0:T(8,128)S(1)}, u32[]{:S(2)}, u32[]{:S(2)}) collective-permute-start(f32[320,128]{1,0:T(8,128)S(1)} %get-tuple-element.72), channel_id=1, source_target_pairs={{0,8},{8,16},{16,24},{24,28},{28,20},{20,12},{12,4},{4,0},{1,9},{9... | collective-permute-start | bytes 491528 | tf_op jit(solution)/shard_map/ppermute | solution.py:291
  39.8 1.6 %collective-permute-done.12.refs_6_ = f32[320,128]{1,0:T(8,128)S(1)} collective-permute-done((f32[320,128]{1,0:T(8,128)S(1)}, f32[320,128]{1,0:T(8,128)S(1)}, u32[]{:S(2)}, u32[]{:S(2)}) %collective-permute-start.12) | collective-permute-done | bytes 163872 | tf_op jit(solution)/shard_map/ppermute | solution.py:287
  41.4 3.4 %collective-permute-done.10 = f32[320,128]{1,0:T(8,128)S(1)} collective-permute-done((f32[320,128]{1,0:T(8,128)S(1)}, f32[320,128]{1,0:T(8,128)S(1)}, u32[]{:S(2)}, u32[]{:S(2)}) %collective-permute-start.10) | collective-permute-done | bytes 163872 | tf_op jit(solution)/shard_map/ppermute | solution.py:292
  47.0 2.9 %forward_products.1 = (f32[1280,128]{1,0:T(8,128)S(1)}, f32[1280,128]{1,0:T(8,128)S(1)}) custom-call(s32[1,1]{1,0:T(1,128)S(6)} %copy.8.live, s32[1,640]{1,0:T(1,128)S(1)} %copy-done.1, s32[1,640]{1,0:T(1,128)S(1)} %copy-done.2, bf16[40960,128]{1,0:T(8,128)(2,1)S(1)} %split_tiles.1.refs_0_, f32[640,128]{1,0:T(8,128)S(1)} %copy-done, ...), custom_call_target="tpu_custom_call" | custom-call | bytes 1048576 | tf_op jit(solution)/shard_map/forward_products/pallas_call | solution.py:193
  49.9 2.1 %collective-permute-done.14 = f32[640,128]{1,0:T(8,128)S(1)} collective-permute-done((f32[640,128]{1,0:T(8,128)S(1)}, f32[640,128]{1,0:T(8,128)S(1)}, u32[]{:S(2)}, u32[]{:S(2)}) %collective-permute-start.14) | collective-permute-done | bytes 327712 | tf_op jit(solution)/shard_map/ppermute | solution.py:303
  53.0 2.1 %collective-permute-start.15 = (f32[640,128]{1,0:T(8,128)S(1)}, f32[640,128]{1,0:T(8,128)S(1)}, u32[]{:S(2)}, u32[]{:S(2)}) collective-permute-start(f32[640,128]{1,0:T(8,128)S(1)} %add.34), channel_id=1, source_target_pairs={{0,8},{8,16},{16,24},{24,28},{28,20},{20,12},{12,4},{4,0},{1,9},{9... | collective-permute-start | bytes 983048 | tf_op jit(solution)/shard_map/ppermute | solution.py:302
  55.1 8.0 %collective-permute-done.17 = f32[640,128]{1,0:T(8,128)S(1)} collective-permute-done((f32[640,128]{1,0:T(8,128)S(1)}, f32[640,128]{1,0:T(8,128)S(1)}, u32[]{:S(2)}, u32[]{:S(2)}) %collective-permute-start.17) | collective-permute-done | bytes 327712 | tf_op jit(solution)/shard_map/ppermute | solution.py:303
  63.5 1.8 %collective-permute-start.16 = (f32[640,128]{1,0:T(8,128)S(1)}, f32[640,128]{1,0:T(8,128)S(1)}, u32[]{:S(2)}, u32[]{:S(2)}) collective-permute-start(f32[640,128]{1,0:T(8,128)S(1)} %add.35), channel_id=1, source_target_pairs={{0,8},{8,16},{16,24},{24,28},{28,20},{20,12},{12,4},{4,0},{1,9},{9... | collective-permute-start | bytes 983048 | tf_op jit(solution)/shard_map/ppermute | solution.py:302
  65.4 1.6 %collective-permute-start.20 = (f32[640,128]{1,0:T(8,128)S(1)}, f32[640,128]{1,0:T(8,128)S(1)}, u32[]{:S(2)}, u32[]{:S(2)}) collective-permute-start(f32[640,128]{1,0:T(8,128)S(1)} %get-tuple-element.98), channel_id=1, source_target_pairs={{0,2},{1,3},{2,0},{3,1},{4,6},{5,7},{6,4},{7,5},{8,10},{9,11},{10,... | collective-permute-start | bytes 983048 | tf_op jit(solution)/shard_map/ppermute | solution.py:311
  67.0 5.5 %collective-permute-done.18.refs_2_ = f32[640,128]{1,0:T(8,128)S(1)} collective-permute-done((f32[640,128]{1,0:T(8,128)S(1)}, f32[640,128]{1,0:T(8,128)S(1)}, u32[]{:S(2)}, u32[]{:S(2)}) %collective-permute-start.18) | collective-permute-done | bytes 327712 | tf_op jit(solution)/shard_map/ppermute | solution.py:303
  72.8 1.5 %collective-permute-done.20.refs_4_ = f32[640,128]{1,0:T(8,128)S(1)} collective-permute-done((f32[640,128]{1,0:T(8,128)S(1)}, f32[640,128]{1,0:T(8,128)S(1)}, u32[]{:S(2)}, u32[]{:S(2)}) %collective-permute-start.20) | collective-permute-done | bytes 327712 | tf_op jit(solution)/shard_map/ppermute | solution.py:311
  (46 shorter events, 11.7 us)
Async XLA Ops:
  3.8 10.9 %collective-permute-start = (f32[640,128]{1,0:T(8,128)}, f32[640,128]{1,0:T(8,128)S(1)}, u32[]{:S(2)}, u32[]{:S(2)}) collective-permute-start(f32[640,128]{1,0:T(8,128)} %get-tuple-element.81.refs_1_), channel_id=1, source_target_pairs={{0,8},{8,16},{16,24},{24,28},{28,20},{20,12},{12,4},{4,0},{1,9},{9... | collective-permute-start | bytes 983048 | tf_op jit(solution)/shard_map/ppermute | solution.py:264
  6.9 9.4 %collective-permute-start.1 = (f32[640,128]{1,0:T(8,128)}, f32[640,128]{1,0:T(8,128)S(1)}, u32[]{:S(2)}, u32[]{:S(2)}) collective-permute-start(f32[640,128]{1,0:T(8,128)} %get-tuple-element.81.refs_1_), channel_id=1, source_target_pairs={{8,0},{16,8},{24,16},{28,24},{20,28},{12,20},{4,12},{0,4},{9,1},{1... | collective-permute-start | bytes 983048 | tf_op jit(solution)/shard_map/ppermute | solution.py:265
  6.9 15.7 %collective-permute-start.6 = (f32[640,128]{1,0:T(8,128)}, f32[640,128]{1,0:T(8,128)S(1)}, u32[]{:S(2)}, u32[]{:S(2)}) collective-permute-start(f32[640,128]{1,0:T(8,128)} %get-tuple-element.81.refs_1_), channel_id=1, source_target_pairs={{0,2},{1,3},{2,0},{3,1},{4,6},{5,7},{6,4},{7,5},{8,10},{9,11},{10,... | collective-permute-start | bytes 983048 | tf_op jit(solution)/shard_map/ppermute | solution.py:267
  13.7 14.1 %copy-start.3 = (s32[1,640]{1,0:T(1,128)S(1)}, s32[1,640]{1,0:T(1,128)}, u32[]{:S(2)}) copy-start(s32[1,640]{1,0:T(1,128)} %get-tuple-element.56.gidx) | copy-start | bytes 7684
  16.2 8.3 %collective-permute-start.2 = (f32[640,128]{1,0:T(8,128)S(1)}, f32[640,128]{1,0:T(8,128)S(1)}, u32[]{:S(2)}, u32[]{:S(2)}) collective-permute-start(f32[640,128]{1,0:T(8,128)S(1)} %collective-permute-done.refs_9_), channel_id=1, source_target_pairs={{0,8},{8,16},{16,24},{24,28},{28,20},{20,12},{12,4},{4,0},{1,9},{9... | collective-permute-start | bytes 983048 | tf_op jit(solution)/shard_map/ppermute | solution.py:264
  17.8 8.0 %collective-permute-start.3 = (f32[640,128]{1,0:T(8,128)S(1)}, f32[640,128]{1,0:T(8,128)S(1)}, u32[]{:S(2)}, u32[]{:S(2)}) collective-permute-start(f32[640,128]{1,0:T(8,128)S(1)} %collective-permute-done.1.refs_2_), channel_id=1, source_target_pairs={{8,0},{16,8},{24,16},{28,24},{20,28},{12,20},{4,12},{0,4},{9,1},{1... | collective-permute-start | bytes 983048 | tf_op jit(solution)/shard_map/ppermute | solution.py:265
  18.3 9.6 %collective-permute-start.7 = (f32[640,128]{1,0:T(8,128)S(1)}, f32[640,128]{1,0:T(8,128)S(1)}, u32[]{:S(2)}, u32[]{:S(2)}) collective-permute-start(f32[640,128]{1,0:T(8,128)S(1)} %copy-done), channel_id=1, source_target_pairs={{0,1},{1,0},{2,3},{3,2},{4,5},{5,4},{6,7},{7,6},{8,9},{9,8},{10,11... | collective-permute-start | bytes 983048 | tf_op jit(solution)/shard_map/ppermute | solution.py:256
  22.5 24.5 %copy-start.1 = (s32[1,640]{1,0:T(1,128)S(1)}, s32[1,640]{1,0:T(1,128)}, u32[]{:S(2)}) copy-start(s32[1,640]{1,0:T(1,128)} %get-tuple-element.79.gidx) | copy-start | bytes 7684
  22.5 24.5 %copy-start.2 = (s32[1,640]{1,0:T(1,128)S(1)}, s32[1,640]{1,0:T(1,128)}, u32[]{:S(2)}) copy-start(s32[1,640]{1,0:T(1,128)} %get-tuple-element.80.sidx) | copy-start | bytes 7684
  22.6 5.3 %collective-permute-start.8 = (f32[640,128]{1,0:T(8,128)S(1)}, f32[640,128]{1,0:T(8,128)S(1)}, u32[]{:S(2)}, u32[]{:S(2)}) collective-permute-start(f32[640,128]{1,0:T(8,128)S(1)} %collective-permute-done.6.refs_2_), channel_id=1, source_target_pairs={{0,1},{1,0},{2,3},{3,2},{4,5},{5,4},{6,7},{7,6},{8,9},{9,8},{10,11... | collective-permute-start | bytes 983048 | tf_op jit(solution)/shard_map/ppermute | solution.py:271
  25.8 7.1 %collective-permute-start.4 = (f32[640,128]{1,0:T(8,128)S(1)}, f32[640,128]{1,0:T(8,128)S(1)}, u32[]{:S(2)}, u32[]{:S(2)}) collective-permute-start(f32[640,128]{1,0:T(8,128)S(1)} %collective-permute-done.2.refs_8_), channel_id=1, source_target_pairs={{0,8},{8,16},{16,24},{24,28},{28,20},{20,12},{12,4},{4,0},{1,9},{9... | collective-permute-start | bytes 983048 | tf_op jit(solution)/shard_map/ppermute | solution.py:264
  27.4 7.1 %collective-permute-start.5 = (f32[640,128]{1,0:T(8,128)S(1)}, f32[640,128]{1,0:T(8,128)S(1)}, u32[]{:S(2)}, u32[]{:S(2)}) collective-permute-start(f32[640,128]{1,0:T(8,128)S(1)} %collective-permute-done.3.refs_3_), channel_id=1, source_target_pairs={{8,0},{16,8},{24,16},{28,24},{20,28},{12,20},{4,12},{0,4},{9,1},{1... | collective-permute-start | bytes 983048 | tf_op jit(solution)/shard_map/ppermute | solution.py:265
  34.5 5.4 %collective-permute-start.11 = (f32[320,128]{1,0:T(8,128)S(1)}, f32[320,128]{1,0:T(8,128)S(1)}, u32[]{:S(2)}, u32[]{:S(2)}) collective-permute-start(f32[320,128]{1,0:T(8,128)S(1)} %slice.25), channel_id=1, source_target_pairs={{0,8},{8,16},{16,24},{24,28},{28,20},{20,12},{12,4},{4,0},{1,9},{9... | collective-permute-start | bytes 491528 | tf_op jit(solution)/shard_map/ppermute | solution.py:287
  36.0 5.4 %collective-permute-start.12 = (f32[320,128]{1,0:T(8,128)S(1)}, f32[320,128]{1,0:T(8,128)S(1)}, u32[]{:S(2)}, u32[]{:S(2)}) collective-permute-start(f32[320,128]{1,0:T(8,128)S(1)} %slice.26), channel_id=1, source_target_pairs={{8,0},{16,8},{24,16},{28,24},{20,28},{12,20},{4,12},{0,4},{9,1},{1... | collective-permute-start | bytes 491528 | tf_op jit(solution)/shard_map/ppermute | solution.py:287
  36.6 8.2 %collective-permute-start.10 = (f32[320,128]{1,0:T(8,128)S(1)}, f32[320,128]{1,0:T(8,128)S(1)}, u32[]{:S(2)}, u32[]{:S(2)}) collective-permute-start(f32[320,128]{1,0:T(8,128)S(1)} %get-tuple-element.73), channel_id=1, source_target_pairs={{8,0},{16,8},{24,16},{28,24},{20,28},{12,20},{4,12},{0,4},{9,1},{1... | collective-permute-start | bytes 491528 | tf_op jit(solution)/shard_map/ppermute | solution.py:292
  37.1 7.7 %collective-permute-start.9 = (f32[320,128]{1,0:T(8,128)S(1)}, f32[320,128]{1,0:T(8,128)S(1)}, u32[]{:S(2)}, u32[]{:S(2)}) collective-permute-start(f32[320,128]{1,0:T(8,128)S(1)} %get-tuple-element.72), channel_id=1, source_target_pairs={{0,8},{8,16},{16,24},{24,28},{28,20},{20,12},{12,4},{4,0},{1,9},{9... | collective-permute-start | bytes 491528 | tf_op jit(solution)/shard_map/ppermute | solution.py:291
  44.9 7.1 %collective-permute-start.14 = (f32[640,128]{1,0:T(8,128)S(1)}, f32[640,128]{1,0:T(8,128)S(1)}, u32[]{:S(2)}, u32[]{:S(2)}) collective-permute-start(f32[640,128]{1,0:T(8,128)S(1)} %pad_maximum_fusion.1), channel_id=1, source_target_pairs={{8,0},{16,8},{24,16},{28,24},{20,28},{12,20},{4,12},{0,4},{9,1},{1... | collective-permute-start | bytes 983048 | tf_op jit(solution)/shard_map/ppermute | solution.py:303
  45.7 7.1 %collective-permute-start.13 = (f32[640,128]{1,0:T(8,128)S(1)}, f32[640,128]{1,0:T(8,128)S(1)}, u32[]{:S(2)}, u32[]{:S(2)}) collective-permute-start(f32[640,128]{1,0:T(8,128)S(1)} %pad_maximum_fusion), channel_id=1, source_target_pairs={{0,8},{8,16},{16,24},{24,28},{28,20},{20,12},{12,4},{4,0},{1,9},{9... | collective-permute-start | bytes 983048 | tf_op jit(solution)/shard_map/ppermute | solution.py:302
  52.9 12.4 %collective-permute-start.19 = (f32[1280,128]{1,0:T(8,128)S(1)}, f32[1280,128]{1,0:T(8,128)S(1)}, u32[]{:S(2)}, u32[]{:S(2)}) collective-permute-start(f32[1280,128]{1,0:T(8,128)S(1)} %get-tuple-element.97), channel_id=1, source_target_pairs={{0,1},{1,0},{2,3},{3,2},{4,5},{5,4},{6,7},{7,6},{8,9},{9,8},{10,11... | collective-permute-start | bytes 1966088 | tf_op jit(solution)/shard_map/ppermute | solution.py:307
  52.9 10.2 %collective-permute-start.17 = (f32[640,128]{1,0:T(8,128)S(1)}, f32[640,128]{1,0:T(8,128)S(1)}, u32[]{:S(2)}, u32[]{:S(2)}) collective-permute-start(f32[640,128]{1,0:T(8,128)S(1)} %add.36), channel_id=1, source_target_pairs={{8,0},{16,8},{24,16},{28,24},{20,28},{12,20},{4,12},{0,4},{9,1},{1... | collective-permute-start | bytes 983048 | tf_op jit(solution)/shard_map/ppermute | solution.py:303
  53.0 10.4 %collective-permute-start.15 = (f32[640,128]{1,0:T(8,128)S(1)}, f32[640,128]{1,0:T(8,128)S(1)}, u32[]{:S(2)}, u32[]{:S(2)}) collective-permute-start(f32[640,128]{1,0:T(8,128)S(1)} %add.34), channel_id=1, source_target_pairs={{0,8},{8,16},{16,24},{24,28},{28,20},{20,12},{12,4},{4,0},{1,9},{9... | collective-permute-start | bytes 983048 | tf_op jit(solution)/shard_map/ppermute | solution.py:302
  63.1 9.4 %collective-permute-start.18 = (f32[640,128]{1,0:T(8,128)S(1)}, f32[640,128]{1,0:T(8,128)S(1)}, u32[]{:S(2)}, u32[]{:S(2)}) collective-permute-start(f32[640,128]{1,0:T(8,128)S(1)} %add.37), channel_id=1, source_target_pairs={{8,0},{16,8},{24,16},{28,24},{20,28},{12,20},{4,12},{0,4},{9,1},{1... | collective-permute-start | bytes 983048 | tf_op jit(solution)/shard_map/ppermute | solution.py:303
  63.5 9.3 %collective-permute-start.16 = (f32[640,128]{1,0:T(8,128)S(1)}, f32[640,128]{1,0:T(8,128)S(1)}, u32[]{:S(2)}, u32[]{:S(2)}) collective-permute-start(f32[640,128]{1,0:T(8,128)S(1)} %add.35), channel_id=1, source_target_pairs={{0,8},{8,16},{16,24},{24,28},{28,20},{20,12},{12,4},{4,0},{1,9},{9... | collective-permute-start | bytes 983048 | tf_op jit(solution)/shard_map/ppermute | solution.py:302
  65.4 8.8 %collective-permute-start.20 = (f32[640,128]{1,0:T(8,128)S(1)}, f32[640,128]{1,0:T(8,128)S(1)}, u32[]{:S(2)}, u32[]{:S(2)}) collective-permute-start(f32[640,128]{1,0:T(8,128)S(1)} %get-tuple-element.98), channel_id=1, source_target_pairs={{0,2},{1,3},{2,0},{3,1},{4,6},{5,7},{6,4},{7,5},{8,10},{9,11},{10,... | collective-permute-start | bytes 983048 | tf_op jit(solution)/shard_map/ppermute | solution.py:311
  (2 other events, 23.6 us)

commit v4 on v3

--- a/solution.py
+++ b/solution.py
@@ -22,13 +22,16 @@
     return [2 * k for k in range(half)] + [2 * k + 1 for k in reversed(range(half))]
 
 
-def prep_kernel(nrow, ncol, blocks, place, live, it, res, rows, cols, xb, grows, gcols, srows, scols):
+def pack_kernel(blocks, it, res, xb):
     lane = lax.broadcasted_iota(jnp.int32, (SUB, LANES), 1)
     for k in range(blocks // 2):
         a = it[:, k * LANES:(k + 1) * LANES]
         b = res[:, k * LANES:(k + 1) * LANES]
         xb[2 * k * SUB:(2 * k + 1) * SUB, :] = jnp.where(lane < BLK, a, pltpu.roll(b, BLK, 1))
         xb[(2 * k + 1) * SUB:(2 * k + 2) * SUB, :] = jnp.where(lane < BLK, pltpu.roll(a, BLK, 1), b)
+
+
+def index_kernel(nrow, ncol, blocks, live, rows, cols, grows, gcols, srows, scols):
     slots = rows.shape[-1]
     alive = lax.broadcasted_iota(jnp.int32, (1, slots), 1) < live[0, 0]
 
@@ -38,7 +41,8 @@
             chunk += (idx >= j * blocks).astype(jnp.int32)
         return chunk, idx - chunk * blocks
 
-    me = place[0]
+    r, c = lax.axis_index("row"), lax.axis_index("col")
+    me = jnp.where(r % 2 == 0, r // 2, nrow - 1 - r // 2)
     chunk, rest = split(cols[...], nrow)
     pos = jnp.where(chunk % 2 == 0, chunk // 2, nrow - 1 - chunk // 2)
     gap = pos - me
@@ -48,8 +52,8 @@
     scols[...] = jnp.where(alive, idx, nrow * blocks)
     major = ncol // 2
     chunk, rest = split(rows[...], ncol)
-    gap = chunk // 2 - place[1]
-    rel = jnp.where(gap < 0, gap + major, gap) + major * jnp.where(chunk % 2 == place[2], 0, 1)
+    gap = chunk // 2 - c // 2
+    rel = jnp.where(gap < 0, gap + major, gap) + major * jnp.where(chunk % 2 == c % 2, 0, 1)
     idx = rel * blocks + rest
     grows[...] = jnp.where(alive, idx, 0)
     srows[...] = jnp.where(alive, idx, ncol * blocks)
@@ -118,13 +122,13 @@
     slots = turned.shape[0] // PITCH
     return pl.pallas_call(
         split_kernel,
-        out_shape=jax.ShapeDtypeStruct((slots * BLK, LANES), jnp.bfloat16),
+        out_shape=pltpu.VMEM((slots * BLK, LANES), jnp.bfloat16),
         in_specs=[VMEM],
         out_specs=VMEM,
         compiler_params=pltpu.CompilerParams(vmem_limit_bytes=4 << 20),
         cost_estimate=pl.CostEstimate(flops=0, bytes_accessed=1 << 20, transcendentals=0),
         name="split_tiles",
-    )(turned)
+    )(pltpu.with_memory_space_constraint(turned, pltpu.VMEM))
 
 
 def tile_kernel(forward, nsrc, group, live, gidx, sidx, *refs):
@@ -202,17 +206,21 @@
         compiler_params=pltpu.CompilerParams(vmem_limit_bytes=20 << 20),
         cost_estimate=pl.CostEstimate(flops=0, bytes_accessed=1 << 20, transcendentals=0),
         name="forward_products" if forward else "mirrored_products",
-    )(live, gidx, sidx, parts, *srcs)
+    )(live, gidx, sidx, pltpu.with_memory_space_constraint(parts, pltpu.VMEM), *srcs)
 
 
 def finish_kernel(blocks, nterm, *refs):
-    terms, h_it, h_res = refs[:nterm], refs[nterm], refs[nterm + 1]
+    halves, terms, h_it, h_res = (refs[:3], refs[3:6]), refs[6:6 + nterm], refs[6 + nterm], refs[7 + nterm]
     lane = lax.broadcasted_iota(jnp.int32, (SUB, LANES), 1)
 
     def total(k):
+        mid = blocks // 2
         at = slice(k * SUB, (k + 1) * SUB)
         out = terms[0][at, :]
         for term in terms[1:]:
+            out = out + term[at, :]
+        at = slice(k % mid * SUB, (k % mid + 1) * SUB)
+        for term in halves[k // mid]:
             out = out + term[at, :]
         return out
 
@@ -231,17 +239,24 @@
     major = ncol // 2
     tiles = stored_tiles[0, 0].transpose(1, 2, 0).reshape(blk * blk, slots)
 
-    r, c = lax.axis_index("row"), lax.axis_index("col")
-    pos = jnp.where(r % 2 == 0, r // 2, nrow - 1 - r // 2)
-    place = jnp.stack([pos, c // 2, c % 2]).astype(jnp.int32)
-    idx_shape = jax.ShapeDtypeStruct((1, slots), jnp.int32)
-    xb, grows, gcols, srows, scols = pl.pallas_call(
-        functools.partial(prep_kernel, nrow, ncol, blocks),
-        out_shape=(jax.ShapeDtypeStruct((rows_each, LANES), jnp.float32),) + (idx_shape,) * 4,
-        in_specs=[SMEM, SMEM, VMEM, VMEM, VMEM, VMEM],
-        out_specs=(VMEM,) * 5,
+    far_off = functools.partial(pltpu.with_memory_space_constraint, memory_space=pltpu.HBM)
+    xb = pl.pallas_call(
+        functools.partial(pack_kernel, blocks),
+        out_shape=pltpu.VMEM((rows_each, LANES), jnp.float32),
+        in_specs=[VMEM, VMEM],
+        out_specs=VMEM,
+        compiler_params=pltpu.CompilerParams(vmem_limit_bytes=4 << 20),
         name="pack",
-    )(place, live_counts, iterate, residual, block_rows[0], block_cols[0])
+    )(far_off(iterate), far_off(residual))
+    grows, gcols, srows, scols = pl.pallas_call(
+        functools.partial(index_kernel, nrow, ncol, blocks),
+        out_shape=(pltpu.VMEM((1, slots), jnp.int32),) * 4,
+        in_specs=[SMEM, VMEM, VMEM],
+        out_specs=(VMEM,) * 4,
+        compiler_params=pltpu.CompilerParams(vmem_limit_bytes=4 << 20),
+        cost_estimate=pl.CostEstimate(flops=0, bytes_accessed=1 << 16, transcendentals=0),
+        name="index",
+    )(live_counts, far_off(block_rows[0]), far_off(block_cols[0]))
 
     cw = [(order[p], order[(p + 1) % nrow]) for p in range(nrow)]
     ccw = [(b, a) for a, b in cw]
@@ -257,6 +272,7 @@
     near_cols = [None] * nrow
     near_cols[0] = xb
     left = right = xb
+    tiles, grows, gcols, srows, scols = hold((tiles, grows, gcols, srows, scols))
     turned = turn_tiles(tiles)
     parts = None
     col_parts = None
@@ -266,47 +282,52 @@
         if k < major:
             held.append(lax.ppermute(held[-1], "col", up))
         if k == 1:
-            left, right, turned = hold((left, right, turned))
+            left, unused = hold((left, turned))
+            right, unused = hold((right, turned))
         if k < major:
             near_core.append(lax.ppermute(held[-1], "col", core))
         near_cols[nrow - k], near_cols[k] = left, right
         if k == 2:
             parts = split_tiles(turned)
-            left, right, parts = hold((left, right, parts))
+            left, parts = hold((left, parts))
+            right, parts = hold((right, parts))
             near_cols[nrow - k], near_cols[k] = left, right
     for k in range(half, major):
         held.append(lax.ppermute(held[-1], "col", up))
         near_core.append(lax.ppermute(held[-1], "col", core))
     near_rows = [held[0]] + held[:0:-1] + [near_core[0]] + near_core[:0:-1]
-    col_parts = tile_products(
-        False, live_counts, grows, scols, parts, near_rows,
-        [blocks] * half + [blocks // 2] * 2 + [blocks] * (half - 1),
-    )
+    col_parts = tile_products(False, live_counts, grows, scols, parts, near_rows, [blocks // 2] * (2 * nrow))
     left, right, col_parts = hold((left, right, col_parts))
     near_cols[half + 1], near_cols[half - 1] = left, right
     near_cols[half:half + 1] = [lax.ppermute(left[:mid], "row", cw), lax.ppermute(right[mid:], "row", ccw)]
-    first, last = col_parts[half], col_parts[half + 1]
-    col_parts = list(col_parts[:half]) + [None] + list(col_parts[half + 2:])
-
-    left = lax.ppermute(first, "row", cw)
-    right = lax.ppermute(last, "row", ccw)
-    left, right, near_cols = hold((left, right, near_cols))
-    own, other = tile_products(True, live_counts, gcols, srows, parts, near_cols, [major * blocks] * 2)
+
+    def send(pair):
+        return lax.ppermute(pair[0], "row", cw), lax.ppermute(pair[1], "row", ccw)
+
+    def mine(k, first):
+        return col_parts[2 * k + 1 - first], col_parts[2 * ((nrow - k) % nrow) + first]
+
+    def add(pair, more):
+        return pair[0] + more[0], pair[1] + more[1]
+
+    far = send(mine(half, 1))
+    near = send(mine(half - 1, 0))
     for k in range(half - 1, 0, -1):
-        a, b = col_parts[k], col_parts[nrow - k]
+        far = hold(far)
+        more = add(far, mine(k, 1))
+        far = send(more)
+        near, unused = hold((near, more))
+        if k > 1:
+            near = send(add(near, mine(k - 1, 0)))
         if k == half - 1:
-            a = jnp.concatenate([a[:mid] + left, a[mid:]], axis=0)
-            b = jnp.concatenate([b[:mid], b[mid:] + right], axis=0)
-        else:
-            a, b = a + left, b + right
-        left = lax.ppermute(a, "row", cw)
-        right = lax.ppermute(b, "row", ccw)
-        if k == half - 1:
-            left, right, own, other = hold((left, right, own, other))
+            near_cols = hold((near_cols, more))[0]
+            own, other = tile_products(True, live_counts, gcols, srows, parts, near_cols, [major * blocks] * 2)
+            far, near, own, other = hold((far, near, own, other))
 
     own = own + lax.ppermute(other, "col", core)
     part = own[(major - 1) * rows_each:] if major > 1 else None
-    terms = [col_parts[0], left, right, own[:rows_each]]
+    halves = [(col_parts[0], far[0], near[1]), (col_parts[1], near[0], far[1])]
+    terms = [own[:rows_each]]
     for k in range(major - 1, 0, -1):
         got = lax.ppermute(part, "col", up)
         part = got if k == 1 else own[(k - 1) * rows_each:k * rows_each] + got
@@ -317,11 +338,11 @@
     return pl.pallas_call(
         functools.partial(finish_kernel, blocks, len(terms)),
         out_shape=(out_shape, out_shape),
-        in_specs=[VMEM] * len(terms),
+        in_specs=[VMEM] * (6 + len(terms)),
         out_specs=(VMEM, VMEM),
         compiler_params=pltpu.CompilerParams(vmem_limit_bytes=4 << 20),
         name="unpack",
-    )(*terms)
+    )(*halves[0], *halves[1], *terms)
 
 
 def solution(mesh):

time: 76 us -> 68.6 us (0.903)
  waiting for transfers between devices: 33.7 us -> 16.7 us
  starting transfers between devices: 21.8 us -> 29 us
  Pallas kernels: 17.3 us -> 21 us
    ppermute x8 -> x14, waiting for transfers between devices: 20.1 us -> 10.8 us  [send(): return (lax.ppermute(pair[0], 'row', cw), lax.ppermute(pair[1], 'row', ccw))]
    ppermute x8 -> x14, starting transfers between devices: 8.42 us -> 16.1 us  [send(): return (lax.ppermute(pair[0], 'row', cw), lax.ppermute(pair[1], 'row', ccw))]
    pallas_call x2, Pallas kernels: 5.34 us -> 9.13 us  [tile_products(): pl.pallas_call(functools.partial(tile_kernel, forward, len(srcs), 4 if fo...]
    ppermute x3, waiting for transfers between devices: 4.91 us -> 2.21 us  [body(): left = lax.ppermute(left, 'row', cw)]
    ppermute x3, waiting for transfers between devices: 4.42 us -> 2.49 us  [body(): right = lax.ppermute(right, 'row', ccw)]
    ppermute x1, waiting for transfers between devices: 1.56 us -> 0.01 us  [body(): lax.ppermute(right[mid:], 'row', ccw)]
    ppermute x1, starting transfers between devices: 1.58 us -> 0.07 us  [body(): got = lax.ppermute(part, 'col', up)]
    ppermute x1, waiting for transfers between devices: 1.48 us -> 0.01 us  [body(): got = lax.ppermute(part, 'col', up)]
  transfers between devices with their start and end apart: 21 -> 27, of which waited for: 15 -> 14; matrix products, arithmetic and copies ran while one was open for 0% -> 1% of each run, Pallas kernels for 19% -> 28%
where the time goes in v4:
time: 68.6 us; the launch traced here: 68.5 us
  starting transfers between devices  29 us (42%)
  Pallas kernels  21 us (31%)
  waiting for transfers between devices  16.7 us (24%)
  between operations  1.45 us (2%)
    ppermute x14, starting transfers between devices, send(): return (lax.ppermute(pair[0], 'row', cw), lax.ppermute(pair[1], 'row', ccw))  16.1 us
    ppermute x14, waiting for transfers between devices, send(): return (lax.ppermute(pair[0], 'row', cw), lax.ppermute(pair[1], 'row', ccw))  10.8 us
    pallas_call x2, Pallas kernels, tile_products(): pl.pallas_call(functools.partial(tile_kernel, forward, len(srcs), 4 if fo...  9.13 us
    ppermute x3, starting transfers between devices, body(): left = lax.ppermute(left, 'row', cw)  6.28 us
    pallas_call x1, Pallas kernels, turn_tiles(): pl.pallas_call(turn_kernel, out_shape=pltpu.VMEM((slots * PITCH, LANES),...  4.82 us
    pallas_call x1, Pallas kernels, split_tiles(): pl.pallas_call(split_kernel, out_shape=pltpu.VMEM((slots * BLK, LANES), j...  4.25 us
    ppermute x3, waiting for transfers between devices, body(): right = lax.ppermute(right, 'row', ccw)  2.49 us
    ppermute x3, waiting for transfers between devices, body(): left = lax.ppermute(left, 'row', cw)  2.21 us
  transfers between devices with their start and end apart: 27, of which 14 were waited for; matrix products, arithmetic and copies ran while one was open for 1% of the time, Pallas kernels for 28%

profile of v4, /device:TPU:0, one launch (start us, length us, event | category | flops | bytes accessed | tf_op | source)
XLA Modules:
  0.0 68.5 jit_solution(7348579994043187709)
XLA Ops:
  1.8 3.1 %collective-permute-start = (f32[640,128]{1,0:T(8,128)S(1)}, f32[640,128]{1,0:T(8,128)S(1)}, u32[]{:S(2)}, u32[]{:S(2)}) collective-permute-start(f32[640,128]{1,0:T(8,128)S(1)} %pack.1.refs_1_), channel_id=1, source_target_pairs={{0,8},{8,16},{16,24},{24,28},{28,20},{20,12},{12,4},{4,0},{1,9},{9... | collective-permute-start | bytes 983048 | tf_op jit(solution)/shard_map/ppermute | solution.py:280
  4.9 2.0 %collective-permute-start.6 = (f32[640,128]{1,0:T(8,128)S(1)}, f32[640,128]{1,0:T(8,128)S(1)}, u32[]{:S(2)}, u32[]{:S(2)}) collective-permute-start(f32[640,128]{1,0:T(8,128)S(1)} %pack.1.refs_1_), channel_id=1, source_target_pairs={{0,2},{1,3},{2,0},{3,1},{4,6},{5,7},{6,4},{7,5},{8,10},{9,11},{10,... | collective-permute-start | bytes 983048 | tf_op jit(solution)/shard_map/ppermute | solution.py:283
  8.2 4.8 %turn_tiles.1.turned = f32[25600,128]{1,0:T(8,128)S(1)} custom-call(f32[4096,640]{1,0:T(8,128)} %bitcast.7), custom_call_target="tpu_custom_call" | custom-call | bytes 1048576 | tf_op jit(solution)/shard_map/turn_tiles/pallas_call | solution.py:92
  13.1 1.6 %collective-permute-start.1 = (f32[640,128]{1,0:T(8,128)S(1)}, f32[640,128]{1,0:T(8,128)S(1)}, u32[]{:S(2)}, u32[]{:S(2)}) collective-permute-start(f32[640,128]{1,0:T(8,128)S(1)} %collective-permute-done.refs_9_), channel_id=1, source_target_pairs={{0,8},{8,16},{16,24},{24,28},{28,20},{20,12},{12,4},{4,0},{1,9},{9... | collective-permute-start | bytes 983048 | tf_op jit(solution)/shard_map/ppermute | solution.py:280
  15.1 4.2 %split_tiles.1.refs_0_ = bf16[40960,128]{1,0:T(8,128)(2,1)S(1)} custom-call(f32[25600,128]{1,0:T(8,128)S(1)} %turn_tiles.1.turned), custom_call_target="tpu_custom_call" | custom-call | bytes 1048576 | tf_op jit(solution)/shard_map/split_tiles/pallas_call | solution.py:123
  20.0 1.7 %collective-permute-done.1.refs_8_ = f32[640,128]{1,0:T(8,128)S(1)} collective-permute-done((f32[640,128]{1,0:T(8,128)S(1)}, f32[640,128]{1,0:T(8,128)S(1)}, u32[]{:S(2)}, u32[]{:S(2)}) %collective-permute-start.1) | collective-permute-done | bytes 327712 | tf_op jit(solution)/shard_map/ppermute | solution.py:280
  21.7 1.3 %collective-permute-done.4.refs_3_ = f32[640,128]{1,0:T(8,128)S(1)} collective-permute-done((f32[640,128]{1,0:T(8,128)S(1)}, f32[640,128]{1,0:T(8,128)S(1)}, u32[]{:S(2)}, u32[]{:S(2)}) %collective-permute-start.4) | collective-permute-done | bytes 327712 | tf_op jit(solution)/shard_map/ppermute | solution.py:281
  23.5 1.6 %collective-permute-start.2 = (f32[640,128]{1,0:T(8,128)S(1)}, f32[640,128]{1,0:T(8,128)S(1)}, u32[]{:S(2)}, u32[]{:S(2)}) collective-permute-start(f32[640,128]{1,0:T(8,128)S(1)} %collective-permute-done.1.refs_8_), channel_id=1, source_target_pairs={{0,8},{8,16},{16,24},{24,28},{28,20},{20,12},{12,4},{4,0},{1,9},{9... | collective-permute-start | bytes 983048 | tf_op jit(solution)/shard_map/ppermute | solution.py:280
  25.1 4.2 %mirrored_products.1 = (f32[320,128]{1,0:T(8,128)S(1)}, f32[320,128]{1,0:T(8,128)S(1)}, f32[320,128]{1,0:T(8,128)S(1)}, f32[320,128]{1,0:T(8,128)S(1)}, f32[320,...) custom-call(s32[1,1]{1,0:T(1,128)S(6)} %copy.8.live, ...), custom_call_target="tpu_custom_call" | custom-call | bytes 1048576 | tf_op jit(solution)/shard_map/mirrored_products/pallas_call | solution.py:197
  30.9 1.6 %collective-permute-start.10 = (f32[320,128]{1,0:T(8,128)S(1)}, f32[320,128]{1,0:T(8,128)S(1)}, u32[]{:S(2)}, u32[]{:S(2)}) collective-permute-start(f32[320,128]{1,0:T(8,128)S(1)} %get-tuple-element.111), channel_id=1, source_target_pairs={{8,0},{16,8},{24,16},{28,24},{20,28},{12,20},{4,12},{0,4},{9,1},{1... | collective-permute-start | bytes 491528 | tf_op jit(solution)/shard_map/ppermute | solution.py:305
  32.9 1.6 %collective-permute-start.13 = (f32[320,128]{1,0:T(8,128)S(1)}, f32[320,128]{1,0:T(8,128)S(1)}, u32[]{:S(2)}, u32[]{:S(2)}) collective-permute-start(f32[320,128]{1,0:T(8,128)S(1)} %get-tuple-element.116), channel_id=1, source_target_pairs={{0,8},{8,16},{16,24},{24,28},{28,20},{20,12},{12,4},{4,0},{1,9},{9... | collective-permute-start | bytes 491528 | tf_op jit(solution)/shard_map/ppermute | solution.py:305
  35.0 1.6 %collective-permute-start.17 = (f32[320,128]{1,0:T(8,128)S(1)}, f32[320,128]{1,0:T(8,128)S(1)}, u32[]{:S(2)}, u32[]{:S(2)}) collective-permute-start(f32[320,128]{1,0:T(8,128)S(1)} %slice.12), channel_id=1, source_target_pairs={{0,8},{8,16},{16,24},{24,28},{28,20},{20,12},{12,4},{4,0},{1,9},{9... | collective-permute-start | bytes 491528 | tf_op jit(solution)/shard_map/ppermute | solution.py:302
  37.9 1.5 %collective-permute-start.18 = (f32[320,128]{1,0:T(8,128)S(1)}, f32[320,128]{1,0:T(8,128)S(1)}, u32[]{:S(2)}, u32[]{:S(2)}) collective-permute-start(f32[320,128]{1,0:T(8,128)S(1)} %slice.13), channel_id=1, source_target_pairs={{8,0},{16,8},{24,16},{28,24},{20,28},{12,20},{4,12},{0,4},{9,1},{1... | collective-permute-start | bytes 491528 | tf_op jit(solution)/shard_map/ppermute | solution.py:302
  39.4 1.6 %collective-permute-start.12 = (f32[320,128]{1,0:T(8,128)S(1)}, f32[320,128]{1,0:T(8,128)S(1)}, u32[]{:S(2)}, u32[]{:S(2)}) collective-permute-start(f32[320,128]{1,0:T(8,128)S(1)} %add.34), channel_id=1, source_target_pairs={{8,0},{16,8},{24,16},{28,24},{20,28},{12,20},{4,12},{0,4},{9,1},{1... | collective-permute-start | bytes 491528 | tf_op jit(solution)/shard_map/ppermute | solution.py:305
  41.7 1.6 %collective-permute-start.16 = (f32[320,128]{1,0:T(8,128)S(1)}, f32[320,128]{1,0:T(8,128)S(1)}, u32[]{:S(2)}, u32[]{:S(2)}) collective-permute-start(f32[320,128]{1,0:T(8,128)S(1)} %add.36), channel_id=1, source_target_pairs={{8,0},{16,8},{24,16},{28,24},{20,28},{12,20},{4,12},{0,4},{9,1},{1... | collective-permute-start | bytes 491528 | tf_op jit(solution)/shard_map/ppermute | solution.py:305
  45.5 4.9 %forward_products.1 = (f32[1280,128]{1,0:T(8,128)S(1)}, f32[1280,128]{1,0:T(8,128)S(1)}) custom-call(s32[1,1]{1,0:T(1,128)S(6)} %copy.8.live, s32[1,640]{1,0:T(1,128)S(1)} %get-tuple-element.122.gidx, s32[1,640]{1,0:T(1,128)S(1)} %get-tuple-element.123.sidx, bf16[40960,128]{1,0:T(8,128)(2,1)S(1)} %split_tiles.1.refs_0_, f32[640,128]{1,0:T(8,128)S(1)} %pack.1.refs_1_, ...), custom_call_target="tpu_custom_call" | custom-call | bytes 1048576 | tf_op jit(solution)/shard_map/forward_products/pallas_call | solution.py:197
  50.7 3.5 %collective-permute-start.20 = (f32[320,128]{1,0:T(8,128)S(1)}, f32[320,128]{1,0:T(8,128)S(1)}, u32[]{:S(2)}, u32[]{:S(2)}) collective-permute-start(f32[320,128]{1,0:T(8,128)S(1)} %add.38), channel_id=1, source_target_pairs={{8,0},{16,8},{24,16},{28,24},{20,28},{12,20},{4,12},{0,4},{9,1},{1... | collective-permute-start | bytes 491528 | tf_op jit(solution)/shard_map/ppermute | solution.py:305
  54.6 2.1 %collective-permute-start.23 = (f32[320,128]{1,0:T(8,128)S(1)}, f32[320,128]{1,0:T(8,128)S(1)}, u32[]{:S(2)}, u32[]{:S(2)}) collective-permute-start(f32[320,128]{1,0:T(8,128)S(1)} %add.41), channel_id=1, source_target_pairs={{8,0},{16,8},{24,16},{28,24},{20,28},{12,20},{4,12},{0,4},{9,1},{1... | collective-permute-start | bytes 491528 | tf_op jit(solution)/shard_map/ppermute | solution.py:305
  56.7 2.0 %collective-permute-done.20 = f32[320,128]{1,0:T(8,128)S(1)} collective-permute-done((f32[320,128]{1,0:T(8,128)S(1)}, f32[320,128]{1,0:T(8,128)S(1)}, u32[]{:S(2)}, u32[]{:S(2)}) %collective-permute-start.20) | collective-permute-done | bytes 163872 | tf_op jit(solution)/shard_map/ppermute | solution.py:305
  58.7 2.2 %collective-permute-done.19 = f32[320,128]{1,0:T(8,128)S(1)} collective-permute-done((f32[320,128]{1,0:T(8,128)S(1)}, f32[320,128]{1,0:T(8,128)S(1)}, u32[]{:S(2)}, u32[]{:S(2)}) %collective-permute-start.19) | collective-permute-done | bytes 163872 | tf_op jit(solution)/shard_map/ppermute | solution.py:305
  61.3 1.8 %collective-permute-start.21 = (f32[320,128]{1,0:T(8,128)S(1)}, f32[320,128]{1,0:T(8,128)S(1)}, u32[]{:S(2)}, u32[]{:S(2)}) collective-permute-start(f32[320,128]{1,0:T(8,128)S(1)} %add.39), channel_id=1, source_target_pairs={{0,8},{8,16},{16,24},{24,28},{28,20},{20,12},{12,4},{4,0},{1,9},{9... | collective-permute-start | bytes 491528 | tf_op jit(solution)/shard_map/ppermute | solution.py:305
  63.1 1.7 %collective-permute-done.22.refs_4_ = f32[320,128]{1,0:T(8,128)S(1)} collective-permute-done((f32[320,128]{1,0:T(8,128)S(1)}, f32[320,128]{1,0:T(8,128)S(1)}, u32[]{:S(2)}, u32[]{:S(2)}) %collective-permute-start.22) | collective-permute-done | bytes 163872 | tf_op jit(solution)/shard_map/ppermute | solution.py:305
  64.8 1.5 %collective-permute-done.24.refs_5_ = f32[320,128]{1,0:T(8,128)S(1)} collective-permute-done((f32[320,128]{1,0:T(8,128)S(1)}, f32[320,128]{1,0:T(8,128)S(1)}, u32[]{:S(2)}, u32[]{:S(2)}) %collective-permute-start.24) | collective-permute-done | bytes 163872 | tf_op jit(solution)/shard_map/ppermute | solution.py:305
  66.3 1.3 %collective-permute-done.21.refs_1_ = f32[320,128]{1,0:T(8,128)S(1)} collective-permute-done((f32[320,128]{1,0:T(8,128)S(1)}, f32[320,128]{1,0:T(8,128)S(1)}, u32[]{:S(2)}, u32[]{:S(2)}) %collective-permute-start.21) | collective-permute-done | bytes 163872 | tf_op jit(solution)/shard_map/ppermute | solution.py:305
  (51 shorter events, 12.0 us)
Async XLA Ops:
  1.8 11.3 %collective-permute-start = (f32[640,128]{1,0:T(8,128)S(1)}, f32[640,128]{1,0:T(8,128)S(1)}, u32[]{:S(2)}, u32[]{:S(2)}) collective-permute-start(f32[640,128]{1,0:T(8,128)S(1)} %pack.1.refs_1_), channel_id=1, source_target_pairs={{0,8},{8,16},{16,24},{24,28},{28,20},{20,12},{12,4},{4,0},{1,9},{9... | collective-permute-start | bytes 983048 | tf_op jit(solution)/shard_map/ppermute | solution.py:280
  4.9 9.8 %collective-permute-start.3 = (f32[640,128]{1,0:T(8,128)S(1)}, f32[640,128]{1,0:T(8,128)S(1)}, u32[]{:S(2)}, u32[]{:S(2)}) collective-permute-start(f32[640,128]{1,0:T(8,128)S(1)} %pack.1.refs_1_), channel_id=1, source_target_pairs={{8,0},{16,8},{24,16},{28,24},{20,28},{12,20},{4,12},{0,4},{9,1},{1... | collective-permute-start | bytes 983048 | tf_op jit(solution)/shard_map/ppermute | solution.py:281
  4.9 14.5 %collective-permute-start.6 = (f32[640,128]{1,0:T(8,128)S(1)}, f32[640,128]{1,0:T(8,128)S(1)}, u32[]{:S(2)}, u32[]{:S(2)}) collective-permute-start(f32[640,128]{1,0:T(8,128)S(1)} %pack.1.refs_1_), channel_id=1, source_target_pairs={{0,2},{1,3},{2,0},{3,1},{4,6},{5,7},{6,4},{7,5},{8,10},{9,11},{10,... | collective-permute-start | bytes 983048 | tf_op jit(solution)/shard_map/ppermute | solution.py:283
  13.1 8.7 %collective-permute-start.1 = (f32[640,128]{1,0:T(8,128)S(1)}, f32[640,128]{1,0:T(8,128)S(1)}, u32[]{:S(2)}, u32[]{:S(2)}) collective-permute-start(f32[640,128]{1,0:T(8,128)S(1)} %collective-permute-done.refs_9_), channel_id=1, source_target_pairs={{0,8},{8,16},{16,24},{24,28},{28,20},{20,12},{12,4},{4,0},{1,9},{9... | collective-permute-start | bytes 983048 | tf_op jit(solution)/shard_map/ppermute | solution.py:280
  14.7 8.3 %collective-permute-start.4 = (f32[640,128]{1,0:T(8,128)S(1)}, f32[640,128]{1,0:T(8,128)S(1)}, u32[]{:S(2)}, u32[]{:S(2)}) collective-permute-start(f32[640,128]{1,0:T(8,128)S(1)} %collective-permute-done.3.refs_2_), channel_id=1, source_target_pairs={{8,0},{16,8},{24,16},{28,24},{20,28},{12,20},{4,12},{0,4},{9,1},{1... | collective-permute-start | bytes 983048 | tf_op jit(solution)/shard_map/ppermute | solution.py:281
  15.1 9.9 %collective-permute-start.7 = (f32[640,128]{1,0:T(8,128)S(1)}, f32[640,128]{1,0:T(8,128)S(1)}, u32[]{:S(2)}, u32[]{:S(2)}) collective-permute-start(f32[640,128]{1,0:T(8,128)S(1)} %pack.1.refs_1_), channel_id=1, source_target_pairs={{0,1},{1,0},{2,3},{3,2},{4,5},{5,4},{6,7},{7,6},{8,9},{9,8},{10,11... | collective-permute-start | bytes 983048 | tf_op jit(solution)/shard_map/ppermute | solution.py:271
  19.4 5.7 %collective-permute-start.8 = (f32[640,128]{1,0:T(8,128)S(1)}, f32[640,128]{1,0:T(8,128)S(1)}, u32[]{:S(2)}, u32[]{:S(2)}) collective-permute-start(f32[640,128]{1,0:T(8,128)S(1)} %collective-permute-done.6.refs_2_), channel_id=1, source_target_pairs={{0,1},{1,0},{2,3},{3,2},{4,5},{5,4},{6,7},{7,6},{8,9},{9,8},{10,11... | collective-permute-start | bytes 983048 | tf_op jit(solution)/shard_map/ppermute | solution.py:288
  23.0 7.4 %collective-permute-start.5 = (f32[640,128]{1,0:T(8,128)S(1)}, f32[640,128]{1,0:T(8,128)S(1)}, u32[]{:S(2)}, u32[]{:S(2)}) collective-permute-start(f32[640,128]{1,0:T(8,128)S(1)} %collective-permute-done.4.refs_3_), channel_id=1, source_target_pairs={{8,0},{16,8},{24,16},{28,24},{20,28},{12,20},{4,12},{0,4},{9,1},{1... | collective-permute-start | bytes 983048 | tf_op jit(solution)/shard_map/ppermute | solution.py:281
  23.5 7.4 %collective-permute-start.2 = (f32[640,128]{1,0:T(8,128)S(1)}, f32[640,128]{1,0:T(8,128)S(1)}, u32[]{:S(2)}, u32[]{:S(2)}) collective-permute-start(f32[640,128]{1,0:T(8,128)S(1)} %collective-permute-done.1.refs_8_), channel_id=1, source_target_pairs={{0,8},{8,16},{16,24},{24,28},{28,20},{20,12},{12,4},{4,0},{1,9},{9... | collective-permute-start | bytes 983048 | tf_op jit(solution)/shard_map/ppermute | solution.py:280
  30.9 7.0 %collective-permute-start.10 = (f32[320,128]{1,0:T(8,128)S(1)}, f32[320,128]{1,0:T(8,128)S(1)}, u32[]{:S(2)}, u32[]{:S(2)}) collective-permute-start(f32[320,128]{1,0:T(8,128)S(1)} %get-tuple-element.111), channel_id=1, source_target_pairs={{8,0},{16,8},{24,16},{28,24},{20,28},{12,20},{4,12},{0,4},{9,1},{1... | collective-permute-start | bytes 491528 | tf_op jit(solution)/shard_map/ppermute | solution.py:305
  32.5 6.9 %collective-permute-start.9 = (f32[320,128]{1,0:T(8,128)S(1)}, f32[320,128]{1,0:T(8,128)S(1)}, u32[]{:S(2)}, u32[]{:S(2)}) collective-permute-start(f32[320,128]{1,0:T(8,128)S(1)} %get-tuple-element.110), channel_id=1, source_target_pairs={{0,8},{8,16},{16,24},{24,28},{28,20},{20,12},{12,4},{4,0},{1,9},{9... | collective-permute-start | bytes 491528 | tf_op jit(solution)/shard_map/ppermute | solution.py:305
  32.9 8.6 %collective-permute-start.13 = (f32[320,128]{1,0:T(8,128)S(1)}, f32[320,128]{1,0:T(8,128)S(1)}, u32[]{:S(2)}, u32[]{:S(2)}) collective-permute-start(f32[320,128]{1,0:T(8,128)S(1)} %get-tuple-element.116), channel_id=1, source_target_pairs={{0,8},{8,16},{16,24},{24,28},{28,20},{20,12},{12,4},{4,0},{1,9},{9... | collective-permute-start | bytes 491528 | tf_op jit(solution)/shard_map/ppermute | solution.py:305
  34.5 7.1 %collective-permute-start.14 = (f32[320,128]{1,0:T(8,128)S(1)}, f32[320,128]{1,0:T(8,128)S(1)}, u32[]{:S(2)}, u32[]{:S(2)}) collective-permute-start(f32[320,128]{1,0:T(8,128)S(1)} %get-tuple-element.117), channel_id=1, source_target_pairs={{8,0},{16,8},{24,16},{28,24},{20,28},{12,20},{4,12},{0,4},{9,1},{1... | collective-permute-start | bytes 491528 | tf_op jit(solution)/shard_map/ppermute | solution.py:305
  35.0 10.1 %collective-permute-start.17 = (f32[320,128]{1,0:T(8,128)S(1)}, f32[320,128]{1,0:T(8,128)S(1)}, u32[]{:S(2)}, u32[]{:S(2)}) collective-permute-start(f32[320,128]{1,0:T(8,128)S(1)} %slice.12), channel_id=1, source_target_pairs={{0,8},{8,16},{16,24},{24,28},{28,20},{20,12},{12,4},{4,0},{1,9},{9... | collective-permute-start | bytes 491528 | tf_op jit(solution)/shard_map/ppermute | solution.py:302
  37.9 7.6 %collective-permute-start.18 = (f32[320,128]{1,0:T(8,128)S(1)}, f32[320,128]{1,0:T(8,128)S(1)}, u32[]{:S(2)}, u32[]{:S(2)}) collective-permute-start(f32[320,128]{1,0:T(8,128)S(1)} %slice.13), channel_id=1, source_target_pairs={{8,0},{16,8},{24,16},{28,24},{20,28},{12,20},{4,12},{0,4},{9,1},{1... | collective-permute-start | bytes 491528 | tf_op jit(solution)/shard_map/ppermute | solution.py:302
  39.4 11.1 %collective-permute-start.12 = (f32[320,128]{1,0:T(8,128)S(1)}, f32[320,128]{1,0:T(8,128)S(1)}, u32[]{:S(2)}, u32[]{:S(2)}) collective-permute-start(f32[320,128]{1,0:T(8,128)S(1)} %add.34), channel_id=1, source_target_pairs={{8,0},{16,8},{24,16},{28,24},{20,28},{12,20},{4,12},{0,4},{9,1},{1... | collective-permute-start | bytes 491528 | tf_op jit(solution)/shard_map/ppermute | solution.py:305
  41.7 8.8 %collective-permute-start.16 = (f32[320,128]{1,0:T(8,128)S(1)}, f32[320,128]{1,0:T(8,128)S(1)}, u32[]{:S(2)}, u32[]{:S(2)}) collective-permute-start(f32[320,128]{1,0:T(8,128)S(1)} %add.36), channel_id=1, source_target_pairs={{8,0},{16,8},{24,16},{28,24},{20,28},{12,20},{4,12},{0,4},{9,1},{1... | collective-permute-start | bytes 491528 | tf_op jit(solution)/shard_map/ppermute | solution.py:305
  43.2 7.2 %collective-permute-start.15 = (f32[320,128]{1,0:T(8,128)S(1)}, f32[320,128]{1,0:T(8,128)S(1)}, u32[]{:S(2)}, u32[]{:S(2)}) collective-permute-start(f32[320,128]{1,0:T(8,128)S(1)} %add.35), channel_id=1, source_target_pairs={{0,8},{8,16},{16,24},{24,28},{28,20},{20,12},{12,4},{4,0},{1,9},{9... | collective-permute-start | bytes 491528 | tf_op jit(solution)/shard_map/ppermute | solution.py:305
  50.7 8.0 %collective-permute-start.20 = (f32[320,128]{1,0:T(8,128)S(1)}, f32[320,128]{1,0:T(8,128)S(1)}, u32[]{:S(2)}, u32[]{:S(2)}) collective-permute-start(f32[320,128]{1,0:T(8,128)S(1)} %add.38), channel_id=1, source_target_pairs={{8,0},{16,8},{24,16},{28,24},{20,28},{12,20},{4,12},{0,4},{9,1},{1... | collective-permute-start | bytes 491528 | tf_op jit(solution)/shard_map/ppermute | solution.py:305
  54.2 6.7 %collective-permute-start.19 = (f32[320,128]{1,0:T(8,128)S(1)}, f32[320,128]{1,0:T(8,128)S(1)}, u32[]{:S(2)}, u32[]{:S(2)}) collective-permute-start(f32[320,128]{1,0:T(8,128)S(1)} %add.37), channel_id=1, source_target_pairs={{0,8},{8,16},{16,24},{24,28},{28,20},{20,12},{12,4},{4,0},{1,9},{9... | collective-permute-start | bytes 491528 | tf_op jit(solution)/shard_map/ppermute | solution.py:305
  54.5 13.2 %collective-permute-start.26 = (f32[640,128]{1,0:T(8,128)S(1)}, f32[640,128]{1,0:T(8,128)S(1)}, u32[]{:S(2)}, u32[]{:S(2)}) collective-permute-start(f32[640,128]{1,0:T(8,128)S(1)} %get-tuple-element.158), channel_id=1, source_target_pairs={{0,2},{1,3},{2,0},{3,1},{4,6},{5,7},{6,4},{7,5},{8,10},{9,11},{10,... | collective-permute-start | bytes 983048 | tf_op jit(solution)/shard_map/ppermute | solution.py:332
  54.6 8.5 %collective-permute-start.23 = (f32[320,128]{1,0:T(8,128)S(1)}, f32[320,128]{1,0:T(8,128)S(1)}, u32[]{:S(2)}, u32[]{:S(2)}) collective-permute-start(f32[320,128]{1,0:T(8,128)S(1)} %add.41), channel_id=1, source_target_pairs={{8,0},{16,8},{24,16},{28,24},{20,28},{12,20},{4,12},{0,4},{9,1},{1... | collective-permute-start | bytes 491528 | tf_op jit(solution)/shard_map/ppermute | solution.py:305
  56.6 8.2 %collective-permute-start.22 = (f32[320,128]{1,0:T(8,128)S(1)}, f32[320,128]{1,0:T(8,128)S(1)}, u32[]{:S(2)}, u32[]{:S(2)}) collective-permute-start(f32[320,128]{1,0:T(8,128)S(1)} %add.40), channel_id=1, source_target_pairs={{0,8},{8,16},{16,24},{24,28},{28,20},{20,12},{12,4},{4,0},{1,9},{9... | collective-permute-start | bytes 491528 | tf_op jit(solution)/shard_map/ppermute | solution.py:305
  61.3 6.3 %collective-permute-start.21 = (f32[320,128]{1,0:T(8,128)S(1)}, f32[320,128]{1,0:T(8,128)S(1)}, u32[]{:S(2)}, u32[]{:S(2)}) collective-permute-start(f32[320,128]{1,0:T(8,128)S(1)} %add.39), channel_id=1, source_target_pairs={{0,8},{8,16},{16,24},{24,28},{28,20},{20,12},{12,4},{4,0},{1,9},{9... | collective-permute-start | bytes 491528 | tf_op jit(solution)/shard_map/ppermute | solution.py:305
  (3 other events, 14.6 us)

commit v5 on v4

--- a/solution.py
+++ b/solution.py
@@ -131,14 +131,10 @@
     )(pltpu.with_memory_space_constraint(turned, pltpu.VMEM))
 
 
-def tile_kernel(forward, nsrc, group, live, gidx, sidx, *refs):
-    parts, refs = refs[0], refs[1:]
-    srcs, outs, pairs, acc = refs[:nsrc], refs[nsrc:-2], refs[-2], refs[-1]
-    first8 = first_half(SUB)
-    at = 0
+def widen(pairs, srcs, places):
     some = 4
     first = first_half(some * SUB)
-    for src in srcs:
+    for src, at in zip(srcs, places):
         n = src.shape[0] // SUB
 
         def pack(k, carry, src=src, at=at):
@@ -155,8 +151,26 @@
             return carry
 
         lax.fori_loop(0, n // some, pack, 0, unroll=n // some)
-        at += n
-    acc[...] = jnp.zeros_like(acc)
+
+
+def widen_kernel(places, *refs):
+    widen(refs[-1], refs[:-1], places)
+
+
+def widen_blocks(srcs, places, blocks):
+    return pl.pallas_call(
+        functools.partial(widen_kernel, places),
+        out_shape=pltpu.VMEM((blocks * PAIR, LANES), jnp.bfloat16),
+        in_specs=[VMEM] * len(srcs),
+        out_specs=VMEM,
+        compiler_params=pltpu.CompilerParams(vmem_limit_bytes=4 << 20),
+        cost_estimate=pl.CostEstimate(flops=0, bytes_accessed=1 << 20, transcendentals=0),
+        name="widen",
+    )(*srcs)
+
+
+def add_products(forward, group, begin, end, live, gidx, sidx, parts, pairs, acc):
+    first8 = first_half(SUB)
 
     def step(k, carry):
         for u in range(LANES // group):
@@ -184,7 +198,15 @@
                 acc[to, :] += z
         return carry
 
-    lax.fori_loop(0, (live[0, 0] + LANES - 1) // LANES, step, 0)
+    lax.fori_loop(begin, jnp.minimum((live[0, 0] + LANES - 1) // LANES, end), step, 0)
+
+
+def mirrored_kernel(nsrc, chunks, live, gidx, sidx, parts, *refs):
+    srcs, outs, pairs, acc = refs[:nsrc], refs[nsrc:-2], refs[-2], refs[-1]
+    places = [sum(s.shape[0] for s in srcs[:k]) // SUB for k in range(nsrc)]
+    widen(pairs, srcs, places)
+    acc[...] = jnp.zeros_like(acc)
+    add_products(False, 1, 0, chunks, live, gidx, sidx, parts, pairs, acc)
     at = 0
     for out in outs:
         n = out.shape[0]
@@ -192,21 +214,47 @@
         at += n
 
 
-def tile_products(forward, live, gidx, sidx, parts, srcs, out_blocks):
+def mirrored_products(live, gidx, sidx, parts, srcs, out_blocks):
     slots = gidx.shape[1]
     return pl.pallas_call(
-        functools.partial(tile_kernel, forward, len(srcs), 4 if forward else 1),
-        out_shape=tuple(jax.ShapeDtypeStruct((n * SUB, LANES), jnp.float32) for n in out_blocks),
+        functools.partial(mirrored_kernel, len(srcs), slots // LANES),
+        out_shape=tuple(pltpu.VMEM((n * SUB, LANES), jnp.float32) for n in out_blocks),
         in_specs=[SMEM] * 3 + [VMEM] * (1 + len(srcs)),
-        out_specs=tuple([VMEM] * len(out_blocks)),
+        out_specs=(VMEM,) * len(out_blocks),
         scratch_shapes=[
             pltpu.VMEM((sum(s.shape[0] for s in srcs) * PAIR // SUB, LANES), jnp.bfloat16),
             pltpu.VMEM(((sum(out_blocks) + 1) * SUB, LANES), jnp.float32),
         ],
-        compiler_params=pltpu.CompilerParams(vmem_limit_bytes=20 << 20),
+        compiler_params=pltpu.CompilerParams(vmem_limit_bytes=16 << 20),
         cost_estimate=pl.CostEstimate(flops=0, bytes_accessed=1 << 20, transcendentals=0),
-        name="forward_products" if forward else "mirrored_products",
+        name="mirrored_products",
     )(live, gidx, sidx, pltpu.with_memory_space_constraint(parts, pltpu.VMEM), *srcs)
+
+
+def forward_kernel(nsrc, places, begin, end, live, gidx, sidx, parts, *refs):
+    srcs, acc, pairs = refs[:nsrc], refs[-2], refs[-1]
+    widen(pairs, srcs, places)
+    if begin == 0:
+        acc[...] = jnp.zeros_like(acc)
+    add_products(True, 4, begin, end, live, gidx, sidx, parts, pairs, acc)
+
+
+def forward_products(live, gidx, sidx, parts, srcs, places, out_blocks, begin, end, pairs, acc=()):
+    begun = acc + (pairs,)
+    at = 4 + len(srcs)
+    return pl.pallas_call(
+        functools.partial(forward_kernel, len(srcs), places, begin, end),
+        out_shape=(
+            pltpu.VMEM(((out_blocks + 1) * SUB, LANES), jnp.float32),
+            pltpu.VMEM(pairs.shape, jnp.bfloat16),
+        ),
+        in_specs=[SMEM] * 3 + [VMEM] * (1 + len(srcs) + len(begun)),
+        out_specs=(VMEM,) * 2,
+        input_output_aliases={at + k: 2 - len(begun) + k for k in range(len(begun))},
+        compiler_params=pltpu.CompilerParams(vmem_limit_bytes=8 << 20),
+        cost_estimate=pl.CostEstimate(flops=0, bytes_accessed=1 << 20, transcendentals=0),
+        name="forward_products",
+    )(live, gidx, sidx, pltpu.with_memory_space_constraint(parts, pltpu.VMEM), *srcs, *begun)
 
 
 def finish_kernel(blocks, nterm, *refs):
@@ -296,37 +344,43 @@
         held.append(lax.ppermute(held[-1], "col", up))
         near_core.append(lax.ppermute(held[-1], "col", core))
     near_rows = [held[0]] + held[:0:-1] + [near_core[0]] + near_core[:0:-1]
-    col_parts = tile_products(False, live_counts, grows, scols, parts, near_rows, [blocks // 2] * (2 * nrow))
-    left, right, col_parts = hold((left, right, col_parts))
-    near_cols[half + 1], near_cols[half - 1] = left, right
-    near_cols[half:half + 1] = [lax.ppermute(left[:mid], "row", cw), lax.ppermute(right[mid:], "row", ccw)]
+    chunks = slots // LANES
+    col_sums = mirrored_products(live_counts, grows, scols, parts, near_rows, [blocks // 2] * (2 * nrow))
 
     def send(pair):
         return lax.ppermute(pair[0], "row", cw), lax.ppermute(pair[1], "row", ccw)
 
     def mine(k, first):
-        return col_parts[2 * k + 1 - first], col_parts[2 * ((nrow - k) % nrow) + first]
+        return col_sums[2 * k + 1 - first], col_sums[2 * ((nrow - k) % nrow) + first]
 
     def add(pair, more):
         return pair[0] + more[0], pair[1] + more[1]
 
+    left, right, col_sums = hold((left, right, col_sums))
+    near_cols[half + 1], near_cols[half - 1] = left, right
+    ends = lax.ppermute(left[:mid], "row", cw), lax.ppermute(right[mid:], "row", ccw)
+    there = [k for k in range(nrow) if k != half]
+    pairs = widen_blocks([near_cols[k] for k in there], [k * blocks for k in there], nrow * blocks)
     far = send(mine(half, 1))
-    near = send(mine(half - 1, 0))
+    near, unused = hold((mine(half - 1, 0), pairs))
+    near = send(near)
     for k in range(half - 1, 0, -1):
-        far = hold(far)
         more = add(far, mine(k, 1))
         far = send(more)
         near, unused = hold((near, more))
         if k > 1:
             near = send(add(near, mine(k - 1, 0)))
         if k == half - 1:
-            near_cols = hold((near_cols, more))[0]
-            own, other = tile_products(True, live_counts, gcols, srows, parts, near_cols, [major * blocks] * 2)
-            far, near, own, other = hold((far, near, own, other))
-
+            ends, unused = hold((ends, more))
+            row_sums, pairs = forward_products(
+                live_counts, gcols, srows, parts, ends, [half * blocks, half * blocks + blocks // 2], ncol * blocks, 0,
+                chunks, pairs,
+            )
+            far, near, row_sums = hold((far, near, row_sums))
+    own, other = row_sums[:major * rows_each], row_sums[major * rows_each:2 * major * rows_each]
     own = own + lax.ppermute(other, "col", core)
     part = own[(major - 1) * rows_each:] if major > 1 else None
-    halves = [(col_parts[0], far[0], near[1]), (col_parts[1], near[0], far[1])]
+    halves = [(col_sums[0], far[0], near[1]), (col_sums[1], near[0], far[1])]
     terms = [own[:rows_each]]
     for k in range(major - 1, 0, -1):
         got = lax.ppermute(part, "col", up)

time: 68.6 us -> 66.9 us (0.975)
  waiting for transfers between devices: 16.7 us -> 13.5 us
  starting transfers between devices: 29 us -> 30.5 us
    ppermute x14, waiting for transfers between devices: 10.8 us -> 8.43 us  [send(): return (lax.ppermute(pair[0], 'row', cw), lax.ppermute(pair[1], 'row', ccw))]
    ppermute x1, starting transfers between devices: 0.07 us -> 1.12 us  [body(): got = lax.ppermute(part, 'col', up)]
    ppermute x1, waiting for transfers between devices: 1.25 us -> 0.31 us  [body(): lax.ppermute(left[:mid], 'row', cw)]
    pallas_call x2 -> x3, Pallas kernels: 9.13 us -> 9.02 us  [the longest x1 4.16 us: mirrored_products(): pl.pallas_call(functools.partial(mirrored_kernel, len(srcs), slots // LAN...]
  transfers between devices with their start and end apart: 27 -> 27, of which waited for: 14 -> 13; matrix products, arithmetic and copies ran while one was open for 1% -> 1% of each run, Pallas kernels for 28% -> 28%
where the time goes in v5:
time: 66.9 us; the launch traced here: 66.7 us
  starting transfers between devices  30.5 us (46%)
  Pallas kernels  20.9 us (31%)
  waiting for transfers between devices  13.5 us (20%)
  between operations  1.46 us (2%)
    ppermute x14, starting transfers between devices, send(): return (lax.ppermute(pair[0], 'row', cw), lax.ppermute(pair[1], 'row', ccw))  16.3 us
    ppermute x14, waiting for transfers between devices, send(): return (lax.ppermute(pair[0], 'row', cw), lax.ppermute(pair[1], 'row', ccw))  8.43 us
    ppermute x3, starting transfers between devices, body(): left = lax.ppermute(left, 'row', cw)  6.28 us
    pallas_call x1, Pallas kernels, turn_tiles(): pl.pallas_call(turn_kernel, out_shape=pltpu.VMEM((slots * PITCH, LANES),...  4.82 us
    pallas_call x1, Pallas kernels, split_tiles(): pl.pallas_call(split_kernel, out_shape=pltpu.VMEM((slots * BLK, LANES), j...  4.25 us
    pallas_call x1, Pallas kernels, mirrored_products(): pl.pallas_call(functools.partial(mirrored_kernel, len(srcs), slots // LAN...  4.16 us
    pallas_call x1, Pallas kernels, forward_products(): pl.pallas_call(functools.partial(forward_kernel, len(srcs), places, begin...  3.98 us
    ppermute x3, waiting for transfers between devices, body(): right = lax.ppermute(right, 'row', ccw)  2.51 us
  transfers between devices with their start and end apart: 27, of which 13 were waited for; matrix products, arithmetic and copies ran while one was open for 1% of the time, Pallas kernels for 28%

profile of v5, /device:TPU:0, one launch (start us, length us, event | category | flops | bytes accessed | tf_op | source)
XLA Modules:
  0.0 66.7 jit_solution(5805566052210543269)
XLA Ops:
  1.8 3.1 %collective-permute-start = (f32[640,128]{1,0:T(8,128)S(1)}, f32[640,128]{1,0:T(8,128)S(1)}, u32[]{:S(2)}, u32[]{:S(2)}) collective-permute-start(f32[640,128]{1,0:T(8,128)S(1)} %pack.1.refs_0_), channel_id=1, source_target_pairs={{0,8},{8,16},{16,24},{24,28},{28,20},{20,12},{12,4},{4,0},{1,9},{9... | collective-permute-start | bytes 983048 | tf_op jit(solution)/shard_map/ppermute | solution.py:328
  4.9 2.0 %collective-permute-start.6 = (f32[640,128]{1,0:T(8,128)S(1)}, f32[640,128]{1,0:T(8,128)S(1)}, u32[]{:S(2)}, u32[]{:S(2)}) collective-permute-start(f32[640,128]{1,0:T(8,128)S(1)} %pack.1.refs_0_), channel_id=1, source_target_pairs={{0,2},{1,3},{2,0},{3,1},{4,6},{5,7},{6,4},{7,5},{8,10},{9,11},{10,... | collective-permute-start | bytes 983048 | tf_op jit(solution)/shard_map/ppermute | solution.py:331
  8.2 4.8 %turn_tiles.1.turned = f32[25600,128]{1,0:T(8,128)S(1)} custom-call(f32[4096,640]{1,0:T(8,128)} %bitcast.7), custom_call_target="tpu_custom_call" | custom-call | bytes 1048576 | tf_op jit(solution)/shard_map/turn_tiles/pallas_call | solution.py:92
  13.1 1.6 %collective-permute-start.1 = (f32[640,128]{1,0:T(8,128)S(1)}, f32[640,128]{1,0:T(8,128)S(1)}, u32[]{:S(2)}, u32[]{:S(2)}) collective-permute-start(f32[640,128]{1,0:T(8,128)S(1)} %collective-permute-done.refs_6_), channel_id=1, source_target_pairs={{0,8},{8,16},{16,24},{24,28},{28,20},{20,12},{12,4},{4,0},{1,9},{9... | collective-permute-start | bytes 983048 | tf_op jit(solution)/shard_map/ppermute | solution.py:328
  15.1 4.2 %split_tiles.1.parts = bf16[40960,128]{1,0:T(8,128)(2,1)S(1)} custom-call(f32[25600,128]{1,0:T(8,128)S(1)} %turn_tiles.1.turned), custom_call_target="tpu_custom_call" | custom-call | bytes 1048576 | tf_op jit(solution)/shard_map/split_tiles/pallas_call | solution.py:123
  20.0 1.7 %collective-permute-done.1.refs_5_ = f32[640,128]{1,0:T(8,128)S(1)} collective-permute-done((f32[640,128]{1,0:T(8,128)S(1)}, f32[640,128]{1,0:T(8,128)S(1)}, u32[]{:S(2)}, u32[]{:S(2)}) %collective-permute-start.1) | collective-permute-done | bytes 327712 | tf_op jit(solution)/shard_map/ppermute | solution.py:328
  21.7 1.3 %collective-permute-done.4.refs_2_ = f32[640,128]{1,0:T(8,128)S(1)} collective-permute-done((f32[640,128]{1,0:T(8,128)S(1)}, f32[640,128]{1,0:T(8,128)S(1)}, u32[]{:S(2)}, u32[]{:S(2)}) %collective-permute-start.4) | collective-permute-done | bytes 327712 | tf_op jit(solution)/shard_map/ppermute | solution.py:329
  23.5 1.6 %collective-permute-start.2 = (f32[640,128]{1,0:T(8,128)S(1)}, f32[640,128]{1,0:T(8,128)S(1)}, u32[]{:S(2)}, u32[]{:S(2)}) collective-permute-start(f32[640,128]{1,0:T(8,128)S(1)} %collective-permute-done.1.refs_5_), channel_id=1, source_target_pairs={{0,8},{8,16},{16,24},{24,28},{28,20},{20,12},{12,4},{4,0},{1,9},{9... | collective-permute-start | bytes 983048 | tf_op jit(solution)/shard_map/ppermute | solution.py:328
  25.1 4.2 %mirrored_products.1 = (f32[320,128]{1,0:T(8,128)S(1)}, f32[320,128]{1,0:T(8,128)S(1)}, f32[320,128]{1,0:T(8,128)S(1)}, f32[320,128]{1,0:T(8,128)S(1)}, f32[320,...) custom-call(s32[1,1]{1,0:T(1,128)S(6)} %copy.10.live, ...), custom_call_target="tpu_custom_call" | custom-call | bytes 1048576 | tf_op jit(solution)/shard_map/mirrored_products/pallas_call | solution.py:219
  29.2 1.2 %collective-permute-done.5.refs_3_ = f32[640,128]{1,0:T(8,128)S(1)} collective-permute-done((f32[640,128]{1,0:T(8,128)S(1)}, f32[640,128]{1,0:T(8,128)S(1)}, u32[]{:S(2)}, u32[]{:S(2)}) %collective-permute-start.5) | collective-permute-done | bytes 327712 | tf_op jit(solution)/shard_map/ppermute | solution.py:329
  30.9 1.6 %collective-permute-start.11 = (f32[320,128]{1,0:T(8,128)S(1)}, f32[320,128]{1,0:T(8,128)S(1)}, u32[]{:S(2)}, u32[]{:S(2)}) collective-permute-start(f32[320,128]{1,0:T(8,128)S(1)} %get-tuple-element.99), channel_id=1, source_target_pairs={{8,0},{16,8},{24,16},{28,24},{20,28},{12,20},{4,12},{0,4},{9,1},{1... | collective-permute-start | bytes 491528 | tf_op jit(solution)/shard_map/ppermute | solution.py:351
  33.8 1.6 %collective-permute-start.13 = (f32[320,128]{1,0:T(8,128)S(1)}, f32[320,128]{1,0:T(8,128)S(1)}, u32[]{:S(2)}, u32[]{:S(2)}) collective-permute-start(f32[320,128]{1,0:T(8,128)S(1)} %get-tuple-element.105), channel_id=1, source_target_pairs={{0,8},{8,16},{16,24},{24,28},{28,20},{20,12},{12,4},{4,0},{1,9},{9... | collective-permute-start | bytes 491528 | tf_op jit(solution)/shard_map/ppermute | solution.py:351
  35.9 1.6 %collective-permute-start.17 = (f32[320,128]{1,0:T(8,128)S(1)}, f32[320,128]{1,0:T(8,128)S(1)}, u32[]{:S(2)}, u32[]{:S(2)}) collective-permute-start(f32[320,128]{1,0:T(8,128)S(1)} %slice.18), channel_id=1, source_target_pairs={{0,8},{8,16},{16,24},{24,28},{28,20},{20,12},{12,4},{4,0},{1,9},{9... | collective-permute-start | bytes 491528 | tf_op jit(solution)/shard_map/ppermute | solution.py:361
  37.9 1.7 %collective-permute-start.18 = (f32[320,128]{1,0:T(8,128)S(1)}, f32[320,128]{1,0:T(8,128)S(1)}, u32[]{:S(2)}, u32[]{:S(2)}) collective-permute-start(f32[320,128]{1,0:T(8,128)S(1)} %slice.19), channel_id=1, source_target_pairs={{8,0},{16,8},{24,16},{28,24},{20,28},{12,20},{4,12},{0,4},{9,1},{1... | collective-permute-start | bytes 491528 | tf_op jit(solution)/shard_map/ppermute | solution.py:361
  39.6 1.6 %collective-permute-start.12 = (f32[320,128]{1,0:T(8,128)S(1)}, f32[320,128]{1,0:T(8,128)S(1)}, u32[]{:S(2)}, u32[]{:S(2)}) collective-permute-start(f32[320,128]{1,0:T(8,128)S(1)} %add.34), channel_id=1, source_target_pairs={{8,0},{16,8},{24,16},{28,24},{20,28},{12,20},{4,12},{0,4},{9,1},{1... | collective-permute-start | bytes 491528 | tf_op jit(solution)/shard_map/ppermute | solution.py:351
  43.2 1.5 %collective-permute-start.15 = (f32[320,128]{1,0:T(8,128)S(1)}, f32[320,128]{1,0:T(8,128)S(1)}, u32[]{:S(2)}, u32[]{:S(2)}) collective-permute-start(f32[320,128]{1,0:T(8,128)S(1)} %add.35), channel_id=1, source_target_pairs={{0,8},{8,16},{16,24},{24,28},{28,20},{20,12},{12,4},{4,0},{1,9},{9... | collective-permute-start | bytes 491528 | tf_op jit(solution)/shard_map/ppermute | solution.py:351
  45.1 1.4 %collective-permute-start.10 = (f32[320,128]{1,0:T(8,128)S(1)}, f32[320,128]{1,0:T(8,128)S(1)}, u32[]{:S(2)}, u32[]{:S(2)}) collective-permute-start(f32[320,128]{1,0:T(8,128)S(1)} %add.33), channel_id=1, source_target_pairs={{0,8},{8,16},{16,24},{24,28},{28,20},{20,12},{12,4},{4,0},{1,9},{9... | collective-permute-start | bytes 491528 | tf_op jit(solution)/shard_map/ppermute | solution.py:351
  46.5 4.0 %forward_products.1 = (f32[2568,128]{1,0:T(8,128)S(1)}, bf16[20480,128]{1,0:T(8,128)(2,1)S(1)}) custom-call(s32[1,1]{1,0:T(1,128)S(6)} %copy.10.live, s32[1,640]{1,0:T(1,128)S(1)} %get-tuple-element.111.gidx, s32[1,640]{1,0:T(1,128)S(1)} %get-tuple-element.112.sidx, bf16[40960,128]{1,0:T(8,128)(2,1)S(1)} %split_tiles.1.parts, ...), custom_call_target="tpu_custom_call", output_to_operand_aliasing={{1}: (6, {})} | custom-call | bytes 1048576 | tf_op jit(solution)/shard_map/forward_products/pallas_call | solution.py:245
  50.7 1.7 %collective-permute-start.23 = (f32[320,128]{1,0:T(8,128)S(1)}, f32[320,128]{1,0:T(8,128)S(1)}, u32[]{:S(2)}, u32[]{:S(2)}) collective-permute-start(f32[320,128]{1,0:T(8,128)S(1)} %add.39), channel_id=1, source_target_pairs={{8,0},{16,8},{24,16},{28,24},{20,28},{12,20},{4,12},{0,4},{9,1},{1... | collective-permute-start | bytes 491528 | tf_op jit(solution)/shard_map/ppermute | solution.py:351
  54.7 1.2 %collective-permute-start.22 = (f32[320,128]{1,0:T(8,128)S(1)}, f32[320,128]{1,0:T(8,128)S(1)}, u32[]{:S(2)}, u32[]{:S(2)}) collective-permute-start(f32[320,128]{1,0:T(8,128)S(1)} %add.41), channel_id=1, source_target_pairs={{8,0},{16,8},{24,16},{28,24},{20,28},{12,20},{4,12},{0,4},{9,1},{1... | collective-permute-start | bytes 491528 | tf_op jit(solution)/shard_map/ppermute | solution.py:351
  56.9 1.5 %collective-permute-done.23 = f32[320,128]{1,0:T(8,128)S(1)} collective-permute-done((f32[320,128]{1,0:T(8,128)S(1)}, f32[320,128]{1,0:T(8,128)S(1)}, u32[]{:S(2)}, u32[]{:S(2)}) %collective-permute-start.23) | collective-permute-done | bytes 163872 | tf_op jit(solution)/shard_map/ppermute | solution.py:351
  60.6 1.3 %collective-permute-done.22.refs_2_ = f32[320,128]{1,0:T(8,128)S(1)} collective-permute-done((f32[320,128]{1,0:T(8,128)S(1)}, f32[320,128]{1,0:T(8,128)S(1)}, u32[]{:S(2)}, u32[]{:S(2)}) %collective-permute-start.22) | collective-permute-done | bytes 163872 | tf_op jit(solution)/shard_map/ppermute | solution.py:351
  61.9 1.2 %collective-permute-done.21.refs_4_ = f32[320,128]{1,0:T(8,128)S(1)} collective-permute-done((f32[320,128]{1,0:T(8,128)S(1)}, f32[320,128]{1,0:T(8,128)S(1)}, u32[]{:S(2)}, u32[]{:S(2)}) %collective-permute-start.21) | collective-permute-done | bytes 163872 | tf_op jit(solution)/shard_map/ppermute | solution.py:351
  63.1 2.1 %collective-permute-done.24.refs_5_ = f32[320,128]{1,0:T(8,128)S(1)} collective-permute-done((f32[320,128]{1,0:T(8,128)S(1)}, f32[320,128]{1,0:T(8,128)S(1)}, u32[]{:S(2)}, u32[]{:S(2)}) %collective-permute-start.24) | collective-permute-done | bytes 163872 | tf_op jit(solution)/shard_map/ppermute | solution.py:351
  (53 shorter events, 15.4 us)
Async XLA Ops:
  1.8 11.3 %collective-permute-start = (f32[640,128]{1,0:T(8,128)S(1)}, f32[640,128]{1,0:T(8,128)S(1)}, u32[]{:S(2)}, u32[]{:S(2)}) collective-permute-start(f32[640,128]{1,0:T(8,128)S(1)} %pack.1.refs_0_), channel_id=1, source_target_pairs={{0,8},{8,16},{16,24},{24,28},{28,20},{20,12},{12,4},{4,0},{1,9},{9... | collective-permute-start | bytes 983048 | tf_op jit(solution)/shard_map/ppermute | solution.py:328
  4.9 9.8 %collective-permute-start.3 = (f32[640,128]{1,0:T(8,128)S(1)}, f32[640,128]{1,0:T(8,128)S(1)}, u32[]{:S(2)}, u32[]{:S(2)}) collective-permute-start(f32[640,128]{1,0:T(8,128)S(1)} %pack.1.refs_0_), channel_id=1, source_target_pairs={{8,0},{16,8},{24,16},{28,24},{20,28},{12,20},{4,12},{0,4},{9,1},{1... | collective-permute-start | bytes 983048 | tf_op jit(solution)/shard_map/ppermute | solution.py:329
  4.9 14.5 %collective-permute-start.6 = (f32[640,128]{1,0:T(8,128)S(1)}, f32[640,128]{1,0:T(8,128)S(1)}, u32[]{:S(2)}, u32[]{:S(2)}) collective-permute-start(f32[640,128]{1,0:T(8,128)S(1)} %pack.1.refs_0_), channel_id=1, source_target_pairs={{0,2},{1,3},{2,0},{3,1},{4,6},{5,7},{6,4},{7,5},{8,10},{9,11},{10,... | collective-permute-start | bytes 983048 | tf_op jit(solution)/shard_map/ppermute | solution.py:331
  13.1 8.7 %collective-permute-start.1 = (f32[640,128]{1,0:T(8,128)S(1)}, f32[640,128]{1,0:T(8,128)S(1)}, u32[]{:S(2)}, u32[]{:S(2)}) collective-permute-start(f32[640,128]{1,0:T(8,128)S(1)} %collective-permute-done.refs_6_), channel_id=1, source_target_pairs={{0,8},{8,16},{16,24},{24,28},{28,20},{20,12},{12,4},{4,0},{1,9},{9... | collective-permute-start | bytes 983048 | tf_op jit(solution)/shard_map/ppermute | solution.py:328
  14.7 8.3 %collective-permute-start.4 = (f32[640,128]{1,0:T(8,128)S(1)}, f32[640,128]{1,0:T(8,128)S(1)}, u32[]{:S(2)}, u32[]{:S(2)}) collective-permute-start(f32[640,128]{1,0:T(8,128)S(1)} %collective-permute-done.3.refs_1_), channel_id=1, source_target_pairs={{8,0},{16,8},{24,16},{28,24},{20,28},{12,20},{4,12},{0,4},{9,1},{1... | collective-permute-start | bytes 983048 | tf_op jit(solution)/shard_map/ppermute | solution.py:329
  15.1 9.9 %collective-permute-start.7 = (f32[640,128]{1,0:T(8,128)S(1)}, f32[640,128]{1,0:T(8,128)S(1)}, u32[]{:S(2)}, u32[]{:S(2)}) collective-permute-start(f32[640,128]{1,0:T(8,128)S(1)} %pack.1.refs_0_), channel_id=1, source_target_pairs={{0,1},{1,0},{2,3},{3,2},{4,5},{5,4},{6,7},{7,6},{8,9},{9,8},{10,11... | collective-permute-start | bytes 983048 | tf_op jit(solution)/shard_map/ppermute | solution.py:319
  23.0 7.4 %collective-permute-start.5 = (f32[640,128]{1,0:T(8,128)S(1)}, f32[640,128]{1,0:T(8,128)S(1)}, u32[]{:S(2)}, u32[]{:S(2)}) collective-permute-start(f32[640,128]{1,0:T(8,128)S(1)} %collective-permute-done.4.refs_2_), channel_id=1, source_target_pairs={{8,0},{16,8},{24,16},{28,24},{20,28},{12,20},{4,12},{0,4},{9,1},{1... | collective-permute-start | bytes 983048 | tf_op jit(solution)/shard_map/ppermute | solution.py:329
  23.5 7.4 %collective-permute-start.2 = (f32[640,128]{1,0:T(8,128)S(1)}, f32[640,128]{1,0:T(8,128)S(1)}, u32[]{:S(2)}, u32[]{:S(2)}) collective-permute-start(f32[640,128]{1,0:T(8,128)S(1)} %collective-permute-done.1.refs_5_), channel_id=1, source_target_pairs={{0,8},{8,16},{16,24},{24,28},{28,20},{20,12},{12,4},{4,0},{1,9},{9... | collective-permute-start | bytes 983048 | tf_op jit(solution)/shard_map/ppermute | solution.py:328
  30.9 7.1 %collective-permute-start.11 = (f32[320,128]{1,0:T(8,128)S(1)}, f32[320,128]{1,0:T(8,128)S(1)}, u32[]{:S(2)}, u32[]{:S(2)}) collective-permute-start(f32[320,128]{1,0:T(8,128)S(1)} %get-tuple-element.99), channel_id=1, source_target_pairs={{8,0},{16,8},{24,16},{28,24},{20,28},{12,20},{4,12},{0,4},{9,1},{1... | collective-permute-start | bytes 491528 | tf_op jit(solution)/shard_map/ppermute | solution.py:351
  32.5 7.2 %collective-permute-start.9 = (f32[320,128]{1,0:T(8,128)S(1)}, f32[320,128]{1,0:T(8,128)S(1)}, u32[]{:S(2)}, u32[]{:S(2)}) collective-permute-start(f32[320,128]{1,0:T(8,128)S(1)} %get-tuple-element.97), channel_id=1, source_target_pairs={{0,8},{8,16},{16,24},{24,28},{28,20},{20,12},{12,4},{4,0},{1,9},{9... | collective-permute-start | bytes 491528 | tf_op jit(solution)/shard_map/ppermute | solution.py:351
  33.8 7.8 %collective-permute-start.13 = (f32[320,128]{1,0:T(8,128)S(1)}, f32[320,128]{1,0:T(8,128)S(1)}, u32[]{:S(2)}, u32[]{:S(2)}) collective-permute-start(f32[320,128]{1,0:T(8,128)S(1)} %get-tuple-element.105), channel_id=1, source_target_pairs={{0,8},{8,16},{16,24},{24,28},{28,20},{20,12},{12,4},{4,0},{1,9},{9... | collective-permute-start | bytes 491528 | tf_op jit(solution)/shard_map/ppermute | solution.py:351
  35.4 7.1 %collective-permute-start.14 = (f32[320,128]{1,0:T(8,128)S(1)}, f32[320,128]{1,0:T(8,128)S(1)}, u32[]{:S(2)}, u32[]{:S(2)}) collective-permute-start(f32[320,128]{1,0:T(8,128)S(1)} %get-tuple-element.106), channel_id=1, source_target_pairs={{8,0},{16,8},{24,16},{28,24},{20,28},{12,20},{4,12},{0,4},{9,1},{1... | collective-permute-start | bytes 491528 | tf_op jit(solution)/shard_map/ppermute | solution.py:351
  35.9 9.2 %collective-permute-start.17 = (f32[320,128]{1,0:T(8,128)S(1)}, f32[320,128]{1,0:T(8,128)S(1)}, u32[]{:S(2)}, u32[]{:S(2)}) collective-permute-start(f32[320,128]{1,0:T(8,128)S(1)} %slice.18), channel_id=1, source_target_pairs={{0,8},{8,16},{16,24},{24,28},{28,20},{20,12},{12,4},{4,0},{1,9},{9... | collective-permute-start | bytes 491528 | tf_op jit(solution)/shard_map/ppermute | solution.py:361
  37.9 8.6 %collective-permute-start.18 = (f32[320,128]{1,0:T(8,128)S(1)}, f32[320,128]{1,0:T(8,128)S(1)}, u32[]{:S(2)}, u32[]{:S(2)}) collective-permute-start(f32[320,128]{1,0:T(8,128)S(1)} %slice.19), channel_id=1, source_target_pairs={{8,0},{16,8},{24,16},{28,24},{20,28},{12,20},{4,12},{0,4},{9,1},{1... | collective-permute-start | bytes 491528 | tf_op jit(solution)/shard_map/ppermute | solution.py:361
  39.6 10.9 %collective-permute-start.12 = (f32[320,128]{1,0:T(8,128)S(1)}, f32[320,128]{1,0:T(8,128)S(1)}, u32[]{:S(2)}, u32[]{:S(2)}) collective-permute-start(f32[320,128]{1,0:T(8,128)S(1)} %add.34), channel_id=1, source_target_pairs={{8,0},{16,8},{24,16},{28,24},{20,28},{12,20},{4,12},{0,4},{9,1},{1... | collective-permute-start | bytes 491528 | tf_op jit(solution)/shard_map/ppermute | solution.py:351
  42.6 7.9 %collective-permute-start.16 = (f32[320,128]{1,0:T(8,128)S(1)}, f32[320,128]{1,0:T(8,128)S(1)}, u32[]{:S(2)}, u32[]{:S(2)}) collective-permute-start(f32[320,128]{1,0:T(8,128)S(1)} %add.36), channel_id=1, source_target_pairs={{8,0},{16,8},{24,16},{28,24},{20,28},{12,20},{4,12},{0,4},{9,1},{1... | collective-permute-start | bytes 491528 | tf_op jit(solution)/shard_map/ppermute | solution.py:351
  43.2 7.3 %collective-permute-start.15 = (f32[320,128]{1,0:T(8,128)S(1)}, f32[320,128]{1,0:T(8,128)S(1)}, u32[]{:S(2)}, u32[]{:S(2)}) collective-permute-start(f32[320,128]{1,0:T(8,128)S(1)} %add.35), channel_id=1, source_target_pairs={{0,8},{8,16},{16,24},{24,28},{28,20},{20,12},{12,4},{4,0},{1,9},{9... | collective-permute-start | bytes 491528 | tf_op jit(solution)/shard_map/ppermute | solution.py:351
  50.7 7.7 %collective-permute-start.23 = (f32[320,128]{1,0:T(8,128)S(1)}, f32[320,128]{1,0:T(8,128)S(1)}, u32[]{:S(2)}, u32[]{:S(2)}) collective-permute-start(f32[320,128]{1,0:T(8,128)S(1)} %add.39), channel_id=1, source_target_pairs={{8,0},{16,8},{24,16},{28,24},{20,28},{12,20},{4,12},{0,4},{9,1},{1... | collective-permute-start | bytes 491528 | tf_op jit(solution)/shard_map/ppermute | solution.py:351
  52.4 7.1 %collective-permute-start.19 = (f32[320,128]{1,0:T(8,128)S(1)}, f32[320,128]{1,0:T(8,128)S(1)}, u32[]{:S(2)}, u32[]{:S(2)}) collective-permute-start(f32[320,128]{1,0:T(8,128)S(1)} %add.37), channel_id=1, source_target_pairs={{0,8},{8,16},{16,24},{24,28},{28,20},{20,12},{12,4},{4,0},{1,9},{9... | collective-permute-start | bytes 491528 | tf_op jit(solution)/shard_map/ppermute | solution.py:351
  53.6 12.2 %collective-permute-start.26 = (f32[640,128]{1,0:T(8,128)S(1)}, f32[640,128]{1,0:T(8,128)S(1)}, u32[]{:S(2)}, u32[]{:S(2)}) collective-permute-start(f32[640,128]{1,0:T(8,128)S(1)} %get-tuple-element.132), channel_id=1, source_target_pairs={{0,2},{1,3},{2,0},{3,1},{4,6},{5,7},{6,4},{7,5},{8,10},{9,11},{10,... | collective-permute-start | bytes 983048 | tf_op jit(solution)/shard_map/ppermute | solution.py:386
  54.7 7.2 %collective-permute-start.22 = (f32[320,128]{1,0:T(8,128)S(1)}, f32[320,128]{1,0:T(8,128)S(1)}, u32[]{:S(2)}, u32[]{:S(2)}) collective-permute-start(f32[320,128]{1,0:T(8,128)S(1)} %add.41), channel_id=1, source_target_pairs={{8,0},{16,8},{24,16},{28,24},{20,28},{12,20},{4,12},{0,4},{9,1},{1... | collective-permute-start | bytes 491528 | tf_op jit(solution)/shard_map/ppermute | solution.py:351
  55.9 7.2 %collective-permute-start.21 = (f32[320,128]{1,0:T(8,128)S(1)}, f32[320,128]{1,0:T(8,128)S(1)}, u32[]{:S(2)}, u32[]{:S(2)}) collective-permute-start(f32[320,128]{1,0:T(8,128)S(1)} %add.40), channel_id=1, source_target_pairs={{0,8},{8,16},{16,24},{24,28},{28,20},{20,12},{12,4},{4,0},{1,9},{9... | collective-permute-start | bytes 491528 | tf_op jit(solution)/shard_map/ppermute | solution.py:351
  58.4 6.8 %collective-permute-start.24 = (f32[320,128]{1,0:T(8,128)S(1)}, f32[320,128]{1,0:T(8,128)S(1)}, u32[]{:S(2)}, u32[]{:S(2)}) collective-permute-start(f32[320,128]{1,0:T(8,128)S(1)} %add.42), channel_id=1, source_target_pairs={{8,0},{16,8},{24,16},{28,24},{20,28},{12,20},{4,12},{0,4},{9,1},{1... | collective-permute-start | bytes 491528 | tf_op jit(solution)/shard_map/ppermute | solution.py:351
  59.4 6.3 %collective-permute-start.20 = (f32[320,128]{1,0:T(8,128)S(1)}, f32[320,128]{1,0:T(8,128)S(1)}, u32[]{:S(2)}, u32[]{:S(2)}) collective-permute-start(f32[320,128]{1,0:T(8,128)S(1)} %add.38), channel_id=1, source_target_pairs={{0,8},{8,16},{16,24},{24,28},{28,20},{20,12},{12,4},{4,0},{1,9},{9... | collective-permute-start | bytes 491528 | tf_op jit(solution)/shard_map/ppermute | solution.py:351
  (3 other events, 13.9 us)

commit v6 on v5

--- a/solution.py
+++ b/solution.py
@@ -115,7 +115,7 @@
         parts[pl.ds(pl.multiple_of(s * BLK, BLK), BLK), :] = both
         return carry
 
-    lax.fori_loop(0, turned.shape[0] // PITCH, split, 0, unroll=32)
+    lax.fori_loop(0, turned.shape[0] // PITCH, split, 0, unroll=turned.shape[0] // PITCH // 4)
 
 
 def split_tiles(turned):
@@ -169,12 +169,12 @@
     )(*srcs)
 
 
-def add_products(forward, group, begin, end, live, gidx, sidx, parts, pairs, acc):
+def add_products(forward, group, size, live, gidx, sidx, parts, pairs, acc):
     first8 = first_half(SUB)
 
     def step(k, carry):
-        for u in range(LANES // group):
-            s = k * LANES + u * group
+        for u in range(size // group):
+            s = k * size + u * group
             x = jnp.concatenate(
                 [pairs[pl.ds(pl.multiple_of(gidx[0, s + t] * PAIR, PAIR), PAIR), :] for t in range(group)], axis=0
             )
@@ -198,15 +198,15 @@
                 acc[to, :] += z
         return carry
 
-    lax.fori_loop(begin, jnp.minimum((live[0, 0] + LANES - 1) // LANES, end), step, 0)
-
-
-def mirrored_kernel(nsrc, chunks, live, gidx, sidx, parts, *refs):
+    lax.fori_loop(0, (live[0, 0] + size - 1) // size, step, 0)
+
+
+def mirrored_kernel(nsrc, size, live, gidx, sidx, parts, *refs):
     srcs, outs, pairs, acc = refs[:nsrc], refs[nsrc:-2], refs[-2], refs[-1]
     places = [sum(s.shape[0] for s in srcs[:k]) // SUB for k in range(nsrc)]
     widen(pairs, srcs, places)
     acc[...] = jnp.zeros_like(acc)
-    add_products(False, 1, 0, chunks, live, gidx, sidx, parts, pairs, acc)
+    add_products(False, 1, size, live, gidx, sidx, parts, pairs, acc)
     at = 0
     for out in outs:
         n = out.shape[0]
@@ -217,7 +217,7 @@
 def mirrored_products(live, gidx, sidx, parts, srcs, out_blocks):
     slots = gidx.shape[1]
     return pl.pallas_call(
-        functools.partial(mirrored_kernel, len(srcs), slots // LANES),
+        functools.partial(mirrored_kernel, len(srcs), slots // 2),
         out_shape=tuple(pltpu.VMEM((n * SUB, LANES), jnp.float32) for n in out_blocks),
         in_specs=[SMEM] * 3 + [VMEM] * (1 + len(srcs)),
         out_specs=(VMEM,) * len(out_blocks),
@@ -231,30 +231,28 @@
     )(live, gidx, sidx, pltpu.with_memory_space_constraint(parts, pltpu.VMEM), *srcs)
 
 
-def forward_kernel(nsrc, places, begin, end, live, gidx, sidx, parts, *refs):
+def forward_kernel(nsrc, places, size, live, gidx, sidx, parts, *refs):
     srcs, acc, pairs = refs[:nsrc], refs[-2], refs[-1]
     widen(pairs, srcs, places)
-    if begin == 0:
-        acc[...] = jnp.zeros_like(acc)
-    add_products(True, 4, begin, end, live, gidx, sidx, parts, pairs, acc)
-
-
-def forward_products(live, gidx, sidx, parts, srcs, places, out_blocks, begin, end, pairs, acc=()):
-    begun = acc + (pairs,)
-    at = 4 + len(srcs)
-    return pl.pallas_call(
-        functools.partial(forward_kernel, len(srcs), places, begin, end),
+    acc[...] = jnp.zeros_like(acc)
+    add_products(True, 4, size, live, gidx, sidx, parts, pairs, acc)
+
+
+def forward_products(live, gidx, sidx, parts, srcs, places, out_blocks, pairs):
+    slots = gidx.shape[1]
+    return pl.pallas_call(
+        functools.partial(forward_kernel, len(srcs), places, slots // 2),
         out_shape=(
             pltpu.VMEM(((out_blocks + 1) * SUB, LANES), jnp.float32),
             pltpu.VMEM(pairs.shape, jnp.bfloat16),
         ),
-        in_specs=[SMEM] * 3 + [VMEM] * (1 + len(srcs) + len(begun)),
+        in_specs=[SMEM] * 3 + [VMEM] * (2 + len(srcs)),
         out_specs=(VMEM,) * 2,
-        input_output_aliases={at + k: 2 - len(begun) + k for k in range(len(begun))},
+        input_output_aliases={4 + len(srcs): 1},
         compiler_params=pltpu.CompilerParams(vmem_limit_bytes=8 << 20),
         cost_estimate=pl.CostEstimate(flops=0, bytes_accessed=1 << 20, transcendentals=0),
         name="forward_products",
-    )(live, gidx, sidx, pltpu.with_memory_space_constraint(parts, pltpu.VMEM), *srcs, *begun)
+    )(live, gidx, sidx, pltpu.with_memory_space_constraint(parts, pltpu.VMEM), *srcs, pairs)
 
 
 def finish_kernel(blocks, nterm, *refs):
@@ -344,7 +342,6 @@
         held.append(lax.ppermute(held[-1], "col", up))
         near_core.append(lax.ppermute(held[-1], "col", core))
     near_rows = [held[0]] + held[:0:-1] + [near_core[0]] + near_core[:0:-1]
-    chunks = slots // LANES
     col_sums = mirrored_products(live_counts, grows, scols, parts, near_rows, [blocks // 2] * (2 * nrow))
 
     def send(pair):
@@ -372,9 +369,8 @@
             near = send(add(near, mine(k - 1, 0)))
         if k == half - 1:
             ends, unused = hold((ends, more))
-            row_sums, pairs = forward_products(
-                live_counts, gcols, srows, parts, ends, [half * blocks, half * blocks + blocks // 2], ncol * blocks, 0,
-                chunks, pairs,
+            row_sums, unused = forward_products(
+                live_counts, gcols, srows, parts, ends, [half * blocks, half * blocks + blocks // 2], ncol * blocks, pairs
             )
             far, near, row_sums = hold((far, near, row_sums))
     own, other = row_sums[:major * rows_each], row_sums[major * rows_each:2 * major * rows_each]

time: 66.9 us -> 66.8 us (level)
  waiting for transfers between devices: 13.5 us -> 16.1 us
  Pallas kernels: 20.9 us -> 18.4 us
    pallas_call x2, Pallas kernels: 8.13 us -> 6.58 us  [the longest x1 3.46 us: mirrored_products(): pl.pallas_call(functools.partial(mirrored_kernel, len(srcs), slots // 2),...]
    ppermute x14, waiting for transfers between devices: 8.43 us -> 9.72 us  [send(): return (lax.ppermute(pair[0], 'row', cw), lax.ppermute(pair[1], 'row', ccw))]
    ppermute x3, waiting for transfers between devices: 2.51 us -> 3.67 us  [body(): right = lax.ppermute(right, 'row', ccw)]
    pallas_call x1, Pallas kernels: 4.25 us -> 3.3 us  [split_tiles(): pl.pallas_call(split_kernel, out_shape=pltpu.VMEM((slots * BLK, LANES), j...]
    ppermute x1, starting transfers between devices: 1.12 us -> 0.29 us  [body(): got = lax.ppermute(part, 'col', up)]
  transfers between devices with their start and end apart: 27 -> 27, of which waited for: 13 -> 11; matrix products, arithmetic and copies ran while one was open for 1% -> 1% of each run, Pallas kernels for 28% -> 25%
where the time goes in v6:
time: 66.8 us; the launch traced here: 66.5 us
  starting transfers between devices  30.1 us (45%)
  Pallas kernels  18.4 us (28%)
  waiting for transfers between devices  16.1 us (24%)
  between operations  1.46 us (2%)
    ppermute x14, starting transfers between devices, send(): return (lax.ppermute(pair[0], 'row', cw), lax.ppermute(pair[1], 'row', ccw))  16.8 us
    ppermute x14, waiting for transfers between devices, send(): return (lax.ppermute(pair[0], 'row', cw), lax.ppermute(pair[1], 'row', ccw))  9.72 us
    ppermute x3, starting transfers between devices, body(): left = lax.ppermute(left, 'row', cw)  6.28 us
    pallas_call x1, Pallas kernels, turn_tiles(): pl.pallas_call(turn_kernel, out_shape=pltpu.VMEM((slots * PITCH, LANES),...  4.82 us
    ppermute x3, waiting for transfers between devices, body(): right = lax.ppermute(right, 'row', ccw)  3.67 us
    pallas_call x1, Pallas kernels, mirrored_products(): pl.pallas_call(functools.partial(mirrored_kernel, len(srcs), slots // 2),...  3.46 us
    pallas_call x1, Pallas kernels, split_tiles(): pl.pallas_call(split_kernel, out_shape=pltpu.VMEM((slots * BLK, LANES), j...  3.3 us
    pallas_call x1, Pallas kernels, forward_products(): pl.pallas_call(functools.partial(forward_kernel, len(srcs), places, slots...  3.12 us
  transfers between devices with their start and end apart: 27, of which 11 were waited for; matrix products, arithmetic and copies ran while one was open for 1% of the time, Pallas kernels for 25%

profile of v6, /device:TPU:0, one launch (start us, length us, event | category | flops | bytes accessed | tf_op | source)
XLA Modules:
  0.0 66.5 jit_solution(17979353098447607189)
XLA Ops:
  1.8 3.1 %collective-permute-start = (f32[640,128]{1,0:T(8,128)S(1)}, f32[640,128]{1,0:T(8,128)S(1)}, u32[]{:S(2)}, u32[]{:S(2)}) collective-permute-start(f32[640,128]{1,0:T(8,128)S(1)} %pack.1.refs_0_), channel_id=1, source_target_pairs={{0,8},{8,16},{16,24},{24,28},{28,20},{20,12},{12,4},{4,0},{1,9},{9... | collective-permute-start | bytes 983048 | tf_op jit(solution)/shard_map/ppermute | solution.py:326
  4.9 2.0 %collective-permute-start.6 = (f32[640,128]{1,0:T(8,128)S(1)}, f32[640,128]{1,0:T(8,128)S(1)}, u32[]{:S(2)}, u32[]{:S(2)}) collective-permute-start(f32[640,128]{1,0:T(8,128)S(1)} %pack.1.refs_0_), channel_id=1, source_target_pairs={{0,2},{1,3},{2,0},{3,1},{4,6},{5,7},{6,4},{7,5},{8,10},{9,11},{10,... | collective-permute-start | bytes 983048 | tf_op jit(solution)/shard_map/ppermute | solution.py:329
  8.2 4.8 %turn_tiles.1.turned = f32[25600,128]{1,0:T(8,128)S(1)} custom-call(f32[4096,640]{1,0:T(8,128)} %bitcast.7), custom_call_target="tpu_custom_call" | custom-call | bytes 1048576 | tf_op jit(solution)/shard_map/turn_tiles/pallas_call | solution.py:92
  13.1 1.6 %collective-permute-start.1 = (f32[640,128]{1,0:T(8,128)S(1)}, f32[640,128]{1,0:T(8,128)S(1)}, u32[]{:S(2)}, u32[]{:S(2)}) collective-permute-start(f32[640,128]{1,0:T(8,128)S(1)} %collective-permute-done.refs_6_), channel_id=1, source_target_pairs={{0,8},{8,16},{16,24},{24,28},{28,20},{20,12},{12,4},{4,0},{1,9},{9... | collective-permute-start | bytes 983048 | tf_op jit(solution)/shard_map/ppermute | solution.py:326
  15.1 3.3 %split_tiles.1.parts = bf16[40960,128]{1,0:T(8,128)(2,1)S(1)} custom-call(f32[25600,128]{1,0:T(8,128)S(1)} %turn_tiles.1.turned), custom_call_target="tpu_custom_call" | custom-call | bytes 1048576 | tf_op jit(solution)/shard_map/split_tiles/pallas_call | solution.py:123
  19.0 2.7 %collective-permute-done.1.refs_5_ = f32[640,128]{1,0:T(8,128)S(1)} collective-permute-done((f32[640,128]{1,0:T(8,128)S(1)}, f32[640,128]{1,0:T(8,128)S(1)}, u32[]{:S(2)}, u32[]{:S(2)}) %collective-permute-start.1) | collective-permute-done | bytes 327712 | tf_op jit(solution)/shard_map/ppermute | solution.py:326
  23.5 1.6 %collective-permute-start.2 = (f32[640,128]{1,0:T(8,128)S(1)}, f32[640,128]{1,0:T(8,128)S(1)}, u32[]{:S(2)}, u32[]{:S(2)}) collective-permute-start(f32[640,128]{1,0:T(8,128)S(1)} %collective-permute-done.1.refs_5_), channel_id=1, source_target_pairs={{0,8},{8,16},{16,24},{24,28},{28,20},{20,12},{12,4},{4,0},{1,9},{9... | collective-permute-start | bytes 983048 | tf_op jit(solution)/shard_map/ppermute | solution.py:326
  25.1 3.5 %mirrored_products.1 = (f32[320,128]{1,0:T(8,128)S(1)}, f32[320,128]{1,0:T(8,128)S(1)}, f32[320,128]{1,0:T(8,128)S(1)}, f32[320,128]{1,0:T(8,128)S(1)}, f32[320,...) custom-call(s32[1,1]{1,0:T(1,128)S(6)} %copy.10.live, ...), custom_call_target="tpu_custom_call" | custom-call | bytes 1048576 | tf_op jit(solution)/shard_map/mirrored_products/pallas_call | solution.py:219
  28.5 2.4 %collective-permute-done.5.refs_3_ = f32[640,128]{1,0:T(8,128)S(1)} collective-permute-done((f32[640,128]{1,0:T(8,128)S(1)}, f32[640,128]{1,0:T(8,128)S(1)}, u32[]{:S(2)}, u32[]{:S(2)}) %collective-permute-start.5) | collective-permute-done | bytes 327712 | tf_op jit(solution)/shard_map/ppermute | solution.py:327
  33.8 1.8 %collective-permute-start.13 = (f32[320,128]{1,0:T(8,128)S(1)}, f32[320,128]{1,0:T(8,128)S(1)}, u32[]{:S(2)}, u32[]{:S(2)}) collective-permute-start(f32[320,128]{1,0:T(8,128)S(1)} %get-tuple-element.105), channel_id=1, source_target_pairs={{0,8},{8,16},{16,24},{24,28},{28,20},{20,12},{12,4},{4,0},{1,9},{9... | collective-permute-start | bytes 491528 | tf_op jit(solution)/shard_map/ppermute | solution.py:348
  35.9 1.8 %collective-permute-start.17 = (f32[320,128]{1,0:T(8,128)S(1)}, f32[320,128]{1,0:T(8,128)S(1)}, u32[]{:S(2)}, u32[]{:S(2)}) collective-permute-start(f32[320,128]{1,0:T(8,128)S(1)} %slice.18), channel_id=1, source_target_pairs={{0,8},{8,16},{16,24},{24,28},{28,20},{20,12},{12,4},{4,0},{1,9},{9... | collective-permute-start | bytes 491528 | tf_op jit(solution)/shard_map/ppermute | solution.py:358
  37.9 1.4 %collective-permute-start.18 = (f32[320,128]{1,0:T(8,128)S(1)}, f32[320,128]{1,0:T(8,128)S(1)}, u32[]{:S(2)}, u32[]{:S(2)}) collective-permute-start(f32[320,128]{1,0:T(8,128)S(1)} %slice.19), channel_id=1, source_target_pairs={{8,0},{16,8},{24,16},{28,24},{20,28},{12,20},{4,12},{0,4},{9,1},{1... | collective-permute-start | bytes 491528 | tf_op jit(solution)/shard_map/ppermute | solution.py:358
  39.4 1.6 %collective-permute-start.12 = (f32[320,128]{1,0:T(8,128)S(1)}, f32[320,128]{1,0:T(8,128)S(1)}, u32[]{:S(2)}, u32[]{:S(2)}) collective-permute-start(f32[320,128]{1,0:T(8,128)S(1)} %add.34), channel_id=1, source_target_pairs={{8,0},{16,8},{24,16},{28,24},{20,28},{12,20},{4,12},{0,4},{9,1},{1... | collective-permute-start | bytes 491528 | tf_op jit(solution)/shard_map/ppermute | solution.py:348
  41.0 1.7 %collective-permute-done.14 = f32[320,128]{1,0:T(8,128)S(1)} collective-permute-done((f32[320,128]{1,0:T(8,128)S(1)}, f32[320,128]{1,0:T(8,128)S(1)}, u32[]{:S(2)}, u32[]{:S(2)}) %collective-permute-start.14) | collective-permute-done | bytes 163872 | tf_op jit(solution)/shard_map/ppermute | solution.py:348
  43.1 1.8 %collective-permute-start.15 = (f32[320,128]{1,0:T(8,128)S(1)}, f32[320,128]{1,0:T(8,128)S(1)}, u32[]{:S(2)}, u32[]{:S(2)}) collective-permute-start(f32[320,128]{1,0:T(8,128)S(1)} %add.35), channel_id=1, source_target_pairs={{0,8},{8,16},{16,24},{24,28},{28,20},{20,12},{12,4},{4,0},{1,9},{9... | collective-permute-start | bytes 491528 | tf_op jit(solution)/shard_map/ppermute | solution.py:348
  44.9 1.4 %collective-permute-start.10 = (f32[320,128]{1,0:T(8,128)S(1)}, f32[320,128]{1,0:T(8,128)S(1)}, u32[]{:S(2)}, u32[]{:S(2)}) collective-permute-start(f32[320,128]{1,0:T(8,128)S(1)} %add.33), channel_id=1, source_target_pairs={{0,8},{8,16},{16,24},{24,28},{28,20},{20,12},{12,4},{4,0},{1,9},{9... | collective-permute-start | bytes 491528 | tf_op jit(solution)/shard_map/ppermute | solution.py:348
  46.3 3.1 %forward_products.1 = (f32[2568,128]{1,0:T(8,128)S(1)}, bf16[20480,128]{1,0:T(8,128)(2,1)S(1)}) custom-call(s32[1,1]{1,0:T(1,128)S(6)} %copy.10.live, s32[1,640]{1,0:T(1,128)S(1)} %get-tuple-element.111.gidx, s32[1,640]{1,0:T(1,128)S(1)} %get-tuple-element.112.sidx, bf16[40960,128]{1,0:T(8,128)(2,1)S(1)} %split_tiles.1.parts, ...), custom_call_target="tpu_custom_call", output_to_operand_aliasing={{1}: (6, {})} | custom-call | bytes 1048576 | tf_op jit(solution)/shard_map/forward_products/pallas_call | solution.py:243
  50.4 1.6 %collective-permute-start.23 = (f32[320,128]{1,0:T(8,128)S(1)}, f32[320,128]{1,0:T(8,128)S(1)}, u32[]{:S(2)}, u32[]{:S(2)}) collective-permute-start(f32[320,128]{1,0:T(8,128)S(1)} %add.39), channel_id=1, source_target_pairs={{8,0},{16,8},{24,16},{28,24},{20,28},{12,20},{4,12},{0,4},{9,1},{1... | collective-permute-start | bytes 491528 | tf_op jit(solution)/shard_map/ppermute | solution.py:348
  52.0 1.8 %collective-permute-start.19 = (f32[320,128]{1,0:T(8,128)S(1)}, f32[320,128]{1,0:T(8,128)S(1)}, u32[]{:S(2)}, u32[]{:S(2)}) collective-permute-start(f32[320,128]{1,0:T(8,128)S(1)} %add.37), channel_id=1, source_target_pairs={{0,8},{8,16},{16,24},{24,28},{28,20},{20,12},{12,4},{4,0},{1,9},{9... | collective-permute-start | bytes 491528 | tf_op jit(solution)/shard_map/ppermute | solution.py:348
  54.2 2.1 %collective-permute-start.22 = (f32[320,128]{1,0:T(8,128)S(1)}, f32[320,128]{1,0:T(8,128)S(1)}, u32[]{:S(2)}, u32[]{:S(2)}) collective-permute-start(f32[320,128]{1,0:T(8,128)S(1)} %add.41), channel_id=1, source_target_pairs={{8,0},{16,8},{24,16},{28,24},{20,28},{12,20},{4,12},{0,4},{9,1},{1... | collective-permute-start | bytes 491528 | tf_op jit(solution)/shard_map/ppermute | solution.py:348
  56.4 2.3 %collective-permute-done.23 = f32[320,128]{1,0:T(8,128)S(1)} collective-permute-done((f32[320,128]{1,0:T(8,128)S(1)}, f32[320,128]{1,0:T(8,128)S(1)}, u32[]{:S(2)}, u32[]{:S(2)}) %collective-permute-start.23) | collective-permute-done | bytes 163872 | tf_op jit(solution)/shard_map/ppermute | solution.py:348
  58.8 2.1 %collective-permute-start.20 = (f32[320,128]{1,0:T(8,128)S(1)}, f32[320,128]{1,0:T(8,128)S(1)}, u32[]{:S(2)}, u32[]{:S(2)}) collective-permute-start(f32[320,128]{1,0:T(8,128)S(1)} %add.38), channel_id=1, source_target_pairs={{0,8},{8,16},{16,24},{24,28},{28,20},{20,12},{12,4},{4,0},{1,9},{9... | collective-permute-start | bytes 491528 | tf_op jit(solution)/shard_map/ppermute | solution.py:348
  60.9 1.3 %collective-permute-done.22.refs_2_ = f32[320,128]{1,0:T(8,128)S(1)} collective-permute-done((f32[320,128]{1,0:T(8,128)S(1)}, f32[320,128]{1,0:T(8,128)S(1)}, u32[]{:S(2)}, u32[]{:S(2)}) %collective-permute-start.22) | collective-permute-done | bytes 163872 | tf_op jit(solution)/shard_map/ppermute | solution.py:348
  62.6 2.9 %collective-permute-done.24.refs_5_ = f32[320,128]{1,0:T(8,128)S(1)} collective-permute-done((f32[320,128]{1,0:T(8,128)S(1)}, f32[320,128]{1,0:T(8,128)S(1)}, u32[]{:S(2)}, u32[]{:S(2)}) %collective-permute-start.24) | collective-permute-done | bytes 163872 | tf_op jit(solution)/shard_map/ppermute | solution.py:348
  (53 shorter events, 11.4 us)
Async XLA Ops:
  1.8 11.3 %collective-permute-start = (f32[640,128]{1,0:T(8,128)S(1)}, f32[640,128]{1,0:T(8,128)S(1)}, u32[]{:S(2)}, u32[]{:S(2)}) collective-permute-start(f32[640,128]{1,0:T(8,128)S(1)} %pack.1.refs_0_), channel_id=1, source_target_pairs={{0,8},{8,16},{16,24},{24,28},{28,20},{20,12},{12,4},{4,0},{1,9},{9... | collective-permute-start | bytes 983048 | tf_op jit(solution)/shard_map/ppermute | solution.py:326
  4.9 9.8 %collective-permute-start.3 = (f32[640,128]{1,0:T(8,128)S(1)}, f32[640,128]{1,0:T(8,128)S(1)}, u32[]{:S(2)}, u32[]{:S(2)}) collective-permute-start(f32[640,128]{1,0:T(8,128)S(1)} %pack.1.refs_0_), channel_id=1, source_target_pairs={{8,0},{16,8},{24,16},{28,24},{20,28},{12,20},{4,12},{0,4},{9,1},{1... | collective-permute-start | bytes 983048 | tf_op jit(solution)/shard_map/ppermute | solution.py:327
  4.9 13.6 %collective-permute-start.6 = (f32[640,128]{1,0:T(8,128)S(1)}, f32[640,128]{1,0:T(8,128)S(1)}, u32[]{:S(2)}, u32[]{:S(2)}) collective-permute-start(f32[640,128]{1,0:T(8,128)S(1)} %pack.1.refs_0_), channel_id=1, source_target_pairs={{0,2},{1,3},{2,0},{3,1},{4,6},{5,7},{6,4},{7,5},{8,10},{9,11},{10,... | collective-permute-start | bytes 983048 | tf_op jit(solution)/shard_map/ppermute | solution.py:329
  13.1 8.7 %collective-permute-start.1 = (f32[640,128]{1,0:T(8,128)S(1)}, f32[640,128]{1,0:T(8,128)S(1)}, u32[]{:S(2)}, u32[]{:S(2)}) collective-permute-start(f32[640,128]{1,0:T(8,128)S(1)} %collective-permute-done.refs_6_), channel_id=1, source_target_pairs={{0,8},{8,16},{16,24},{24,28},{28,20},{20,12},{12,4},{4,0},{1,9},{9... | collective-permute-start | bytes 983048 | tf_op jit(solution)/shard_map/ppermute | solution.py:326
  14.7 8.3 %collective-permute-start.4 = (f32[640,128]{1,0:T(8,128)S(1)}, f32[640,128]{1,0:T(8,128)S(1)}, u32[]{:S(2)}, u32[]{:S(2)}) collective-permute-start(f32[640,128]{1,0:T(8,128)S(1)} %collective-permute-done.3.refs_1_), channel_id=1, source_target_pairs={{8,0},{16,8},{24,16},{28,24},{20,28},{12,20},{4,12},{0,4},{9,1},{1... | collective-permute-start | bytes 983048 | tf_op jit(solution)/shard_map/ppermute | solution.py:327
  15.1 9.9 %collective-permute-start.7 = (f32[640,128]{1,0:T(8,128)S(1)}, f32[640,128]{1,0:T(8,128)S(1)}, u32[]{:S(2)}, u32[]{:S(2)}) collective-permute-start(f32[640,128]{1,0:T(8,128)S(1)} %pack.1.refs_0_), channel_id=1, source_target_pairs={{0,1},{1,0},{2,3},{3,2},{4,5},{5,4},{6,7},{7,6},{8,9},{9,8},{10,11... | collective-permute-start | bytes 983048 | tf_op jit(solution)/shard_map/ppermute | solution.py:317
  18.5 6.6 %collective-permute-start.8 = (f32[640,128]{1,0:T(8,128)S(1)}, f32[640,128]{1,0:T(8,128)S(1)}, u32[]{:S(2)}, u32[]{:S(2)}) collective-permute-start(f32[640,128]{1,0:T(8,128)S(1)} %collective-permute-done.6.refs_1_), channel_id=1, source_target_pairs={{0,1},{1,0},{2,3},{3,2},{4,5},{5,4},{6,7},{7,6},{8,9},{9,8},{10,11... | collective-permute-start | bytes 983048 | tf_op jit(solution)/shard_map/ppermute | solution.py:334
  23.0 7.9 %collective-permute-start.5 = (f32[640,128]{1,0:T(8,128)S(1)}, f32[640,128]{1,0:T(8,128)S(1)}, u32[]{:S(2)}, u32[]{:S(2)}) collective-permute-start(f32[640,128]{1,0:T(8,128)S(1)} %collective-permute-done.4.refs_2_), channel_id=1, source_target_pairs={{8,0},{16,8},{24,16},{28,24},{20,28},{12,20},{4,12},{0,4},{9,1},{1... | collective-permute-start | bytes 983048 | tf_op jit(solution)/shard_map/ppermute | solution.py:327
  23.5 7.4 %collective-permute-start.2 = (f32[640,128]{1,0:T(8,128)S(1)}, f32[640,128]{1,0:T(8,128)S(1)}, u32[]{:S(2)}, u32[]{:S(2)}) collective-permute-start(f32[640,128]{1,0:T(8,128)S(1)} %collective-permute-done.1.refs_5_), channel_id=1, source_target_pairs={{0,8},{8,16},{16,24},{24,28},{28,20},{20,12},{12,4},{4,0},{1,9},{9... | collective-permute-start | bytes 983048 | tf_op jit(solution)/shard_map/ppermute | solution.py:326
  30.9 7.0 %collective-permute-start.11 = (f32[320,128]{1,0:T(8,128)S(1)}, f32[320,128]{1,0:T(8,128)S(1)}, u32[]{:S(2)}, u32[]{:S(2)}) collective-permute-start(f32[320,128]{1,0:T(8,128)S(1)} %get-tuple-element.99), channel_id=1, source_target_pairs={{8,0},{16,8},{24,16},{28,24},{20,28},{12,20},{4,12},{0,4},{9,1},{1... | collective-permute-start | bytes 491528 | tf_op jit(solution)/shard_map/ppermute | solution.py:348
  32.2 7.2 %collective-permute-start.9 = (f32[320,128]{1,0:T(8,128)S(1)}, f32[320,128]{1,0:T(8,128)S(1)}, u32[]{:S(2)}, u32[]{:S(2)}) collective-permute-start(f32[320,128]{1,0:T(8,128)S(1)} %get-tuple-element.97), channel_id=1, source_target_pairs={{0,8},{8,16},{16,24},{24,28},{28,20},{20,12},{12,4},{4,0},{1,9},{9... | collective-permute-start | bytes 491528 | tf_op jit(solution)/shard_map/ppermute | solution.py:348
  33.8 7.2 %collective-permute-start.13 = (f32[320,128]{1,0:T(8,128)S(1)}, f32[320,128]{1,0:T(8,128)S(1)}, u32[]{:S(2)}, u32[]{:S(2)}) collective-permute-start(f32[320,128]{1,0:T(8,128)S(1)} %get-tuple-element.105), channel_id=1, source_target_pairs={{0,8},{8,16},{16,24},{24,28},{28,20},{20,12},{12,4},{4,0},{1,9},{9... | collective-permute-start | bytes 491528 | tf_op jit(solution)/shard_map/ppermute | solution.py:348
  35.6 7.1 %collective-permute-start.14 = (f32[320,128]{1,0:T(8,128)S(1)}, f32[320,128]{1,0:T(8,128)S(1)}, u32[]{:S(2)}, u32[]{:S(2)}) collective-permute-start(f32[320,128]{1,0:T(8,128)S(1)} %get-tuple-element.106), channel_id=1, source_target_pairs={{8,0},{16,8},{24,16},{28,24},{20,28},{12,20},{4,12},{0,4},{9,1},{1... | collective-permute-start | bytes 491528 | tf_op jit(solution)/shard_map/ppermute | solution.py:348
  35.9 9.0 %collective-permute-start.17 = (f32[320,128]{1,0:T(8,128)S(1)}, f32[320,128]{1,0:T(8,128)S(1)}, u32[]{:S(2)}, u32[]{:S(2)}) collective-permute-start(f32[320,128]{1,0:T(8,128)S(1)} %slice.18), channel_id=1, source_target_pairs={{0,8},{8,16},{16,24},{24,28},{28,20},{20,12},{12,4},{4,0},{1,9},{9... | collective-permute-start | bytes 491528 | tf_op jit(solution)/shard_map/ppermute | solution.py:358
  37.9 8.4 %collective-permute-start.18 = (f32[320,128]{1,0:T(8,128)S(1)}, f32[320,128]{1,0:T(8,128)S(1)}, u32[]{:S(2)}, u32[]{:S(2)}) collective-permute-start(f32[320,128]{1,0:T(8,128)S(1)} %slice.19), channel_id=1, source_target_pairs={{8,0},{16,8},{24,16},{28,24},{20,28},{12,20},{4,12},{0,4},{9,1},{1... | collective-permute-start | bytes 491528 | tf_op jit(solution)/shard_map/ppermute | solution.py:358
  39.4 10.2 %collective-permute-start.12 = (f32[320,128]{1,0:T(8,128)S(1)}, f32[320,128]{1,0:T(8,128)S(1)}, u32[]{:S(2)}, u32[]{:S(2)}) collective-permute-start(f32[320,128]{1,0:T(8,128)S(1)} %add.34), channel_id=1, source_target_pairs={{8,0},{16,8},{24,16},{28,24},{20,28},{12,20},{4,12},{0,4},{9,1},{1... | collective-permute-start | bytes 491528 | tf_op jit(solution)/shard_map/ppermute | solution.py:348
  42.8 6.8 %collective-permute-start.16 = (f32[320,128]{1,0:T(8,128)S(1)}, f32[320,128]{1,0:T(8,128)S(1)}, u32[]{:S(2)}, u32[]{:S(2)}) collective-permute-start(f32[320,128]{1,0:T(8,128)S(1)} %add.36), channel_id=1, source_target_pairs={{8,0},{16,8},{24,16},{28,24},{20,28},{12,20},{4,12},{0,4},{9,1},{1... | collective-permute-start | bytes 491528 | tf_op jit(solution)/shard_map/ppermute | solution.py:348
  43.1 6.4 %collective-permute-start.15 = (f32[320,128]{1,0:T(8,128)S(1)}, f32[320,128]{1,0:T(8,128)S(1)}, u32[]{:S(2)}, u32[]{:S(2)}) collective-permute-start(f32[320,128]{1,0:T(8,128)S(1)} %add.35), channel_id=1, source_target_pairs={{0,8},{8,16},{16,24},{24,28},{28,20},{20,12},{12,4},{4,0},{1,9},{9... | collective-permute-start | bytes 491528 | tf_op jit(solution)/shard_map/ppermute | solution.py:348
  50.4 8.3 %collective-permute-start.23 = (f32[320,128]{1,0:T(8,128)S(1)}, f32[320,128]{1,0:T(8,128)S(1)}, u32[]{:S(2)}, u32[]{:S(2)}) collective-permute-start(f32[320,128]{1,0:T(8,128)S(1)} %add.39), channel_id=1, source_target_pairs={{8,0},{16,8},{24,16},{28,24},{20,28},{12,20},{4,12},{0,4},{9,1},{1... | collective-permute-start | bytes 491528 | tf_op jit(solution)/shard_map/ppermute | solution.py:348
  52.0 6.8 %collective-permute-start.19 = (f32[320,128]{1,0:T(8,128)S(1)}, f32[320,128]{1,0:T(8,128)S(1)}, u32[]{:S(2)}, u32[]{:S(2)}) collective-permute-start(f32[320,128]{1,0:T(8,128)S(1)} %add.37), channel_id=1, source_target_pairs={{0,8},{8,16},{16,24},{24,28},{28,20},{20,12},{12,4},{4,0},{1,9},{9... | collective-permute-start | bytes 491528 | tf_op jit(solution)/shard_map/ppermute | solution.py:348
  53.9 11.6 %collective-permute-start.26 = (f32[640,128]{1,0:T(8,128)S(1)}, f32[640,128]{1,0:T(8,128)S(1)}, u32[]{:S(2)}, u32[]{:S(2)}) collective-permute-start(f32[640,128]{1,0:T(8,128)S(1)} %get-tuple-element.132), channel_id=1, source_target_pairs={{0,2},{1,3},{2,0},{3,1},{4,6},{5,7},{6,4},{7,5},{8,10},{9,11},{10,... | collective-permute-start | bytes 983048 | tf_op jit(solution)/shard_map/ppermute | solution.py:382
  54.2 8.0 %collective-permute-start.22 = (f32[320,128]{1,0:T(8,128)S(1)}, f32[320,128]{1,0:T(8,128)S(1)}, u32[]{:S(2)}, u32[]{:S(2)}) collective-permute-start(f32[320,128]{1,0:T(8,128)S(1)} %add.41), channel_id=1, source_target_pairs={{8,0},{16,8},{24,16},{28,24},{20,28},{12,20},{4,12},{0,4},{9,1},{1... | collective-permute-start | bytes 491528 | tf_op jit(solution)/shard_map/ppermute | solution.py:348
  58.7 6.8 %collective-permute-start.24 = (f32[320,128]{1,0:T(8,128)S(1)}, f32[320,128]{1,0:T(8,128)S(1)}, u32[]{:S(2)}, u32[]{:S(2)}) collective-permute-start(f32[320,128]{1,0:T(8,128)S(1)} %add.42), channel_id=1, source_target_pairs={{8,0},{16,8},{24,16},{28,24},{20,28},{12,20},{4,12},{0,4},{9,1},{1... | collective-permute-start | bytes 491528 | tf_op jit(solution)/shard_map/ppermute | solution.py:348
  58.8 6.7 %collective-permute-start.20 = (f32[320,128]{1,0:T(8,128)S(1)}, f32[320,128]{1,0:T(8,128)S(1)}, u32[]{:S(2)}, u32[]{:S(2)}) collective-permute-start(f32[320,128]{1,0:T(8,128)S(1)} %add.38), channel_id=1, source_target_pairs={{0,8},{8,16},{16,24},{24,28},{28,20},{20,12},{12,4},{4,0},{1,9},{9... | collective-permute-start | bytes 491528 | tf_op jit(solution)/shard_map/ppermute | solution.py:348
  (3 other events, 15.1 us)

commit v7 on v6

--- a/solution.py
+++ b/solution.py
@@ -256,7 +256,7 @@
 
 
 def finish_kernel(blocks, nterm, *refs):
-    halves, terms, h_it, h_res = (refs[:3], refs[3:6]), refs[6:6 + nterm], refs[6 + nterm], refs[7 + nterm]
+    halves, terms, h_it, h_res = (refs[:2], refs[2:4]), refs[4:4 + nterm], refs[4 + nterm], refs[5 + nterm]
     lane = lax.broadcasted_iota(jnp.int32, (SUB, LANES), 1)
 
     def total(k):
@@ -376,7 +376,9 @@
     own, other = row_sums[:major * rows_each], row_sums[major * rows_each:2 * major * rows_each]
     own = own + lax.ppermute(other, "col", core)
     part = own[(major - 1) * rows_each:] if major > 1 else None
-    halves = [(col_sums[0], far[0], near[1]), (col_sums[1], near[0], far[1])]
+    far = add(far, (col_sums[0], col_sums[1]))
+    near, far = hold((near, far))
+    halves = [(far[0], near[1]), (near[0], far[1])]
     terms = [own[:rows_each]]
     for k in range(major - 1, 0, -1):
         got = lax.ppermute(part, "col", up)
@@ -388,7 +390,7 @@
     return pl.pallas_call(
         functools.partial(finish_kernel, blocks, len(terms)),
         out_shape=(out_shape, out_shape),
-        in_specs=[VMEM] * (6 + len(terms)),
+        in_specs=[VMEM] * (4 + len(terms)),
         out_specs=(VMEM, VMEM),
         compiler_params=pltpu.CompilerParams(vmem_limit_bytes=4 << 20),
         name="unpack",

time: 66.8 us -> 66.7 us (level)
  Pallas kernels: 18.4 us -> 22.9 us
  waiting for transfers between devices: 16.1 us -> 12 us
    pallas_call x1, Pallas kernels: 3.12 us -> 5.55 us  [forward_products(): pl.pallas_call(functools.partial(forward_kernel, len(srcs), places, slots...]
    ppermute x3, waiting for transfers between devices: 3.67 us -> 1.31 us  [body(): right = lax.ppermute(right, 'row', ccw)]
    pallas_call x1, Pallas kernels: 3.46 us -> 5.59 us  [mirrored_products(): pl.pallas_call(functools.partial(mirrored_kernel, len(srcs), slots // 2),...]
    ppermute x14, waiting for transfers between devices: 9.72 us -> 8.02 us  [send(): return (lax.ppermute(pair[0], 'row', cw), lax.ppermute(pair[1], 'row', ccw))]
    ppermute x14, starting transfers between devices: 16.8 us -> 16.1 us  [send(): return (lax.ppermute(pair[0], 'row', cw), lax.ppermute(pair[1], 'row', ccw))]
  transfers between devices with their start and end apart: 27 -> 27, of which waited for: 11 -> 9; matrix products, arithmetic and copies ran while one was open for 1% -> 1% of each run, Pallas kernels for 25% -> 31%
where the time goes in v7:
time: 66.7 us; the launch traced here: 66.8 us
  starting transfers between devices  29.9 us (45%)
  Pallas kernels  22.9 us (34%)
  waiting for transfers between devices  12 us (18%)
  between operations  1.5 us (2%)
    ppermute x14, starting transfers between devices, send(): return (lax.ppermute(pair[0], 'row', cw), lax.ppermute(pair[1], 'row', ccw))  16.1 us
    ppermute x14, waiting for transfers between devices, send(): return (lax.ppermute(pair[0], 'row', cw), lax.ppermute(pair[1], 'row', ccw))  8.02 us
    ppermute x3, starting transfers between devices, body(): left = lax.ppermute(left, 'row', cw)  6.28 us
    pallas_call x1, Pallas kernels, mirrored_products(): pl.pallas_call(functools.partial(mirrored_kernel, len(srcs), slots // 2),...  5.59 us
    pallas_call x1, Pallas kernels, forward_products(): pl.pallas_call(functools.partial(forward_kernel, len(srcs), places, slots...  5.55 us
    pallas_call x1, Pallas kernels, turn_tiles(): pl.pallas_call(turn_kernel, out_shape=pltpu.VMEM((slots * PITCH, LANES),...  4.82 us
    pallas_call x1, Pallas kernels, split_tiles(): pl.pallas_call(split_kernel, out_shape=pltpu.VMEM((slots * BLK, LANES), j...  3.3 us
    ppermute x3, waiting for transfers between devices, body(): left = lax.ppermute(left, 'row', cw)  2.7 us
  transfers between devices with their start and end apart: 27, of which 9 were waited for; matrix products, arithmetic and copies ran while one was open for 1% of the time, Pallas kernels for 31%

profile of v7, /device:TPU:0, one launch (start us, length us, event | category | flops | bytes accessed | tf_op | source)
XLA Modules:
  0.0 66.8 jit_solution(1022660247703655100)
XLA Ops:
  1.8 3.1 %collective-permute-start = (f32[640,128]{1,0:T(8,128)S(1)}, f32[640,128]{1,0:T(8,128)S(1)}, u32[]{:S(2)}, u32[]{:S(2)}) collective-permute-start(f32[640,128]{1,0:T(8,128)S(1)} %pack.1.refs_0_), channel_id=1, source_target_pairs={{0,8},{8,16},{16,24},{24,28},{28,20},{20,12},{12,4},{4,0},{1,9},{9... | collective-permute-start | bytes 983048 | tf_op jit(solution)/shard_map/ppermute | solution.py:326
  4.9 2.0 %collective-permute-start.6 = (f32[640,128]{1,0:T(8,128)S(1)}, f32[640,128]{1,0:T(8,128)S(1)}, u32[]{:S(2)}, u32[]{:S(2)}) collective-permute-start(f32[640,128]{1,0:T(8,128)S(1)} %pack.1.refs_0_), channel_id=1, source_target_pairs={{0,2},{1,3},{2,0},{3,1},{4,6},{5,7},{6,4},{7,5},{8,10},{9,11},{10,... | collective-permute-start | bytes 983048 | tf_op jit(solution)/shard_map/ppermute | solution.py:329
  8.2 4.8 %turn_tiles.1.turned = f32[25600,128]{1,0:T(8,128)S(1)} custom-call(f32[4096,640]{1,0:T(8,128)} %bitcast.7), custom_call_target="tpu_custom_call" | custom-call | bytes 1048576 | tf_op jit(solution)/shard_map/turn_tiles/pallas_call | solution.py:92
  13.1 1.6 %collective-permute-start.1 = (f32[640,128]{1,0:T(8,128)S(1)}, f32[640,128]{1,0:T(8,128)S(1)}, u32[]{:S(2)}, u32[]{:S(2)}) collective-permute-start(f32[640,128]{1,0:T(8,128)S(1)} %collective-permute-done.refs_6_), channel_id=1, source_target_pairs={{0,8},{8,16},{16,24},{24,28},{28,20},{20,12},{12,4},{4,0},{1,9},{9... | collective-permute-start | bytes 983048 | tf_op jit(solution)/shard_map/ppermute | solution.py:326
  15.1 3.3 %split_tiles.1.parts = bf16[40960,128]{1,0:T(8,128)(2,1)S(1)} custom-call(f32[25600,128]{1,0:T(8,128)S(1)} %turn_tiles.1.turned), custom_call_target="tpu_custom_call" | custom-call | bytes 1048576 | tf_op jit(solution)/shard_map/split_tiles/pallas_call | solution.py:123
  19.0 2.7 %collective-permute-done.1.refs_5_ = f32[640,128]{1,0:T(8,128)S(1)} collective-permute-done((f32[640,128]{1,0:T(8,128)S(1)}, f32[640,128]{1,0:T(8,128)S(1)}, u32[]{:S(2)}, u32[]{:S(2)}) %collective-permute-start.1) | collective-permute-done | bytes 327712 | tf_op jit(solution)/shard_map/ppermute | solution.py:326
  21.7 1.3 %collective-permute-done.4.refs_2_ = f32[640,128]{1,0:T(8,128)S(1)} collective-permute-done((f32[640,128]{1,0:T(8,128)S(1)}, f32[640,128]{1,0:T(8,128)S(1)}, u32[]{:S(2)}, u32[]{:S(2)}) %collective-permute-start.4) | collective-permute-done | bytes 327712 | tf_op jit(solution)/shard_map/ppermute | solution.py:327
  23.5 1.6 %collective-permute-start.2 = (f32[640,128]{1,0:T(8,128)S(1)}, f32[640,128]{1,0:T(8,128)S(1)}, u32[]{:S(2)}, u32[]{:S(2)}) collective-permute-start(f32[640,128]{1,0:T(8,128)S(1)} %collective-permute-done.1.refs_5_), channel_id=1, source_target_pairs={{0,8},{8,16},{16,24},{24,28},{28,20},{20,12},{12,4},{4,0},{1,9},{9... | collective-permute-start | bytes 983048 | tf_op jit(solution)/shard_map/ppermute | solution.py:326
  25.1 5.6 %mirrored_products.1 = (f32[320,128]{1,0:T(8,128)S(1)}, f32[320,128]{1,0:T(8,128)S(1)}, f32[320,128]{1,0:T(8,128)S(1)}, f32[320,128]{1,0:T(8,128)S(1)}, f32[320,...) custom-call(s32[1,1]{1,0:T(1,128)S(6)} %copy.10.live, ...), custom_call_target="tpu_custom_call" | custom-call | bytes 1048576 | tf_op jit(solution)/shard_map/mirrored_products/pallas_call | solution.py:219
  30.7 1.5 %collective-permute-start.11 = (f32[320,128]{1,0:T(8,128)S(1)}, f32[320,128]{1,0:T(8,128)S(1)}, u32[]{:S(2)}, u32[]{:S(2)}) collective-permute-start(f32[320,128]{1,0:T(8,128)S(1)} %get-tuple-element.102), channel_id=1, source_target_pairs={{8,0},{16,8},{24,16},{28,24},{20,28},{12,20},{4,12},{0,4},{9,1},{1... | collective-permute-start | bytes 491528 | tf_op jit(solution)/shard_map/ppermute | solution.py:348
  33.6 1.6 %collective-permute-start.13 = (f32[320,128]{1,0:T(8,128)S(1)}, f32[320,128]{1,0:T(8,128)S(1)}, u32[]{:S(2)}, u32[]{:S(2)}) collective-permute-start(f32[320,128]{1,0:T(8,128)S(1)} %get-tuple-element.108), channel_id=1, source_target_pairs={{0,8},{8,16},{16,24},{24,28},{28,20},{20,12},{12,4},{4,0},{1,9},{9... | collective-permute-start | bytes 491528 | tf_op jit(solution)/shard_map/ppermute | solution.py:348
  35.7 1.6 %collective-permute-start.17 = (f32[320,128]{1,0:T(8,128)S(1)}, f32[320,128]{1,0:T(8,128)S(1)}, u32[]{:S(2)}, u32[]{:S(2)}) collective-permute-start(f32[320,128]{1,0:T(8,128)S(1)} %slice.18), channel_id=1, source_target_pairs={{0,8},{8,16},{16,24},{24,28},{28,20},{20,12},{12,4},{4,0},{1,9},{9... | collective-permute-start | bytes 491528 | tf_op jit(solution)/shard_map/ppermute | solution.py:358
  37.8 1.5 %collective-permute-start.18 = (f32[320,128]{1,0:T(8,128)S(1)}, f32[320,128]{1,0:T(8,128)S(1)}, u32[]{:S(2)}, u32[]{:S(2)}) collective-permute-start(f32[320,128]{1,0:T(8,128)S(1)} %slice.19), channel_id=1, source_target_pairs={{8,0},{16,8},{24,16},{28,24},{20,28},{12,20},{4,12},{0,4},{9,1},{1... | collective-permute-start | bytes 491528 | tf_op jit(solution)/shard_map/ppermute | solution.py:358
  39.3 1.7 %collective-permute-start.12 = (f32[320,128]{1,0:T(8,128)S(1)}, f32[320,128]{1,0:T(8,128)S(1)}, u32[]{:S(2)}, u32[]{:S(2)}) collective-permute-start(f32[320,128]{1,0:T(8,128)S(1)} %add.40), channel_id=1, source_target_pairs={{8,0},{16,8},{24,16},{28,24},{20,28},{12,20},{4,12},{0,4},{9,1},{1... | collective-permute-start | bytes 491528 | tf_op jit(solution)/shard_map/ppermute | solution.py:348
  41.0 1.3 %collective-permute-done.14 = f32[320,128]{1,0:T(8,128)S(1)} collective-permute-done((f32[320,128]{1,0:T(8,128)S(1)}, f32[320,128]{1,0:T(8,128)S(1)}, u32[]{:S(2)}, u32[]{:S(2)}) %collective-permute-start.14) | collective-permute-done | bytes 163872 | tf_op jit(solution)/shard_map/ppermute | solution.py:348
  42.9 1.6 %collective-permute-start.15 = (f32[320,128]{1,0:T(8,128)S(1)}, f32[320,128]{1,0:T(8,128)S(1)}, u32[]{:S(2)}, u32[]{:S(2)}) collective-permute-start(f32[320,128]{1,0:T(8,128)S(1)} %add.41), channel_id=1, source_target_pairs={{0,8},{8,16},{16,24},{24,28},{28,20},{20,12},{12,4},{4,0},{1,9},{9... | collective-permute-start | bytes 491528 | tf_op jit(solution)/shard_map/ppermute | solution.py:348
  44.6 1.8 %collective-permute-start.10 = (f32[320,128]{1,0:T(8,128)S(1)}, f32[320,128]{1,0:T(8,128)S(1)}, u32[]{:S(2)}, u32[]{:S(2)}) collective-permute-start(f32[320,128]{1,0:T(8,128)S(1)} %add.39), channel_id=1, source_target_pairs={{0,8},{8,16},{16,24},{24,28},{28,20},{20,12},{12,4},{4,0},{1,9},{9... | collective-permute-start | bytes 491528 | tf_op jit(solution)/shard_map/ppermute | solution.py:348
  46.3 5.5 %forward_products.1 = (f32[2568,128]{1,0:T(8,128)S(1)}, bf16[20480,128]{1,0:T(8,128)(2,1)S(1)}) custom-call(s32[1,1]{1,0:T(1,128)S(6)} %copy.10.live, s32[1,640]{1,0:T(1,128)S(1)} %get-tuple-element.114.gidx, s32[1,640]{1,0:T(1,128)S(1)} %get-tuple-element.115.sidx, bf16[40960,128]{1,0:T(8,128)(2,1)S(1)} %split_tiles.1.parts, ...), custom_call_target="tpu_custom_call", output_to_operand_aliasing={{1}: (6, {})} | custom-call | bytes 1048576 | tf_op jit(solution)/shard_map/forward_products/pallas_call | solution.py:243
  52.2 2.1 %collective-permute-start.21 = (f32[320,128]{1,0:T(8,128)S(1)}, f32[320,128]{1,0:T(8,128)S(1)}, u32[]{:S(2)}, u32[]{:S(2)}) collective-permute-start(f32[320,128]{1,0:T(8,128)S(1)} %add.43), channel_id=1, source_target_pairs={{0,8},{8,16},{16,24},{24,28},{28,20},{20,12},{12,4},{4,0},{1,9},{9... | collective-permute-start | bytes 491528 | tf_op jit(solution)/shard_map/ppermute | solution.py:348
  56.0 1.4 %collective-permute-start.19 = (f32[320,128]{1,0:T(8,128)S(1)}, f32[320,128]{1,0:T(8,128)S(1)}, u32[]{:S(2)}, u32[]{:S(2)}) collective-permute-start(f32[320,128]{1,0:T(8,128)S(1)} %add.45), channel_id=1, source_target_pairs={{0,8},{8,16},{16,24},{24,28},{28,20},{20,12},{12,4},{4,0},{1,9},{9... | collective-permute-start | bytes 491528 | tf_op jit(solution)/shard_map/ppermute | solution.py:348
  57.4 1.7 %collective-permute-done.22 = f32[320,128]{1,0:T(8,128)S(1)} collective-permute-done((f32[320,128]{1,0:T(8,128)S(1)}, f32[320,128]{1,0:T(8,128)S(1)}, u32[]{:S(2)}, u32[]{:S(2)}) %collective-permute-start.22) | collective-permute-done | bytes 163872 | tf_op jit(solution)/shard_map/ppermute | solution.py:348
  59.3 2.0 %collective-permute-start.23 = (f32[320,128]{1,0:T(8,128)S(1)}, f32[320,128]{1,0:T(8,128)S(1)}, u32[]{:S(2)}, u32[]{:S(2)}) collective-permute-start(f32[320,128]{1,0:T(8,128)S(1)} %add.47), channel_id=1, source_target_pairs={{0,8},{8,16},{16,24},{24,28},{28,20},{20,12},{12,4},{4,0},{1,9},{9... | collective-permute-start | bytes 491528 | tf_op jit(solution)/shard_map/ppermute | solution.py:348
  61.3 1.3 %collective-permute-done.20.refs_1_ = f32[320,128]{1,0:T(8,128)S(1)} collective-permute-done((f32[320,128]{1,0:T(8,128)S(1)}, f32[320,128]{1,0:T(8,128)S(1)}, u32[]{:S(2)}, u32[]{:S(2)}) %collective-permute-start.20) | collective-permute-done | bytes 163872 | tf_op jit(solution)/shard_map/ppermute | solution.py:348
  63.2 2.5 %collective-permute-done.24 = f32[320,128]{1,0:T(8,128)S(1)} collective-permute-done((f32[320,128]{1,0:T(8,128)S(1)}, f32[320,128]{1,0:T(8,128)S(1)}, u32[]{:S(2)}, u32[]{:S(2)}) %collective-permute-start.24) | collective-permute-done | bytes 163872 | tf_op jit(solution)/shard_map/ppermute | solution.py:348
  (55 shorter events, 10.1 us)
Async XLA Ops:
  1.8 11.3 %collective-permute-start = (f32[640,128]{1,0:T(8,128)S(1)}, f32[640,128]{1,0:T(8,128)S(1)}, u32[]{:S(2)}, u32[]{:S(2)}) collective-permute-start(f32[640,128]{1,0:T(8,128)S(1)} %pack.1.refs_0_), channel_id=1, source_target_pairs={{0,8},{8,16},{16,24},{24,28},{28,20},{20,12},{12,4},{4,0},{1,9},{9... | collective-permute-start | bytes 983048 | tf_op jit(solution)/shard_map/ppermute | solution.py:326
  4.9 9.8 %collective-permute-start.3 = (f32[640,128]{1,0:T(8,128)S(1)}, f32[640,128]{1,0:T(8,128)S(1)}, u32[]{:S(2)}, u32[]{:S(2)}) collective-permute-start(f32[640,128]{1,0:T(8,128)S(1)} %pack.1.refs_0_), channel_id=1, source_target_pairs={{8,0},{16,8},{24,16},{28,24},{20,28},{12,20},{4,12},{0,4},{9,1},{1... | collective-permute-start | bytes 983048 | tf_op jit(solution)/shard_map/ppermute | solution.py:327
  4.9 13.6 %collective-permute-start.6 = (f32[640,128]{1,0:T(8,128)S(1)}, f32[640,128]{1,0:T(8,128)S(1)}, u32[]{:S(2)}, u32[]{:S(2)}) collective-permute-start(f32[640,128]{1,0:T(8,128)S(1)} %pack.1.refs_0_), channel_id=1, source_target_pairs={{0,2},{1,3},{2,0},{3,1},{4,6},{5,7},{6,4},{7,5},{8,10},{9,11},{10,... | collective-permute-start | bytes 983048 | tf_op jit(solution)/shard_map/ppermute | solution.py:329
  13.1 8.7 %collective-permute-start.1 = (f32[640,128]{1,0:T(8,128)S(1)}, f32[640,128]{1,0:T(8,128)S(1)}, u32[]{:S(2)}, u32[]{:S(2)}) collective-permute-start(f32[640,128]{1,0:T(8,128)S(1)} %collective-permute-done.refs_6_), channel_id=1, source_target_pairs={{0,8},{8,16},{16,24},{24,28},{28,20},{20,12},{12,4},{4,0},{1,9},{9... | collective-permute-start | bytes 983048 | tf_op jit(solution)/shard_map/ppermute | solution.py:326
  14.7 8.3 %collective-permute-start.4 = (f32[640,128]{1,0:T(8,128)S(1)}, f32[640,128]{1,0:T(8,128)S(1)}, u32[]{:S(2)}, u32[]{:S(2)}) collective-permute-start(f32[640,128]{1,0:T(8,128)S(1)} %collective-permute-done.3.refs_1_), channel_id=1, source_target_pairs={{8,0},{16,8},{24,16},{28,24},{20,28},{12,20},{4,12},{0,4},{9,1},{1... | collective-permute-start | bytes 983048 | tf_op jit(solution)/shard_map/ppermute | solution.py:327
  15.1 9.9 %collective-permute-start.7 = (f32[640,128]{1,0:T(8,128)S(1)}, f32[640,128]{1,0:T(8,128)S(1)}, u32[]{:S(2)}, u32[]{:S(2)}) collective-permute-start(f32[640,128]{1,0:T(8,128)S(1)} %pack.1.refs_0_), channel_id=1, source_target_pairs={{0,1},{1,0},{2,3},{3,2},{4,5},{5,4},{6,7},{7,6},{8,9},{9,8},{10,11... | collective-permute-start | bytes 983048 | tf_op jit(solution)/shard_map/ppermute | solution.py:317
  18.5 6.6 %collective-permute-start.8 = (f32[640,128]{1,0:T(8,128)S(1)}, f32[640,128]{1,0:T(8,128)S(1)}, u32[]{:S(2)}, u32[]{:S(2)}) collective-permute-start(f32[640,128]{1,0:T(8,128)S(1)} %collective-permute-done.6.refs_1_), channel_id=1, source_target_pairs={{0,1},{1,0},{2,3},{3,2},{4,5},{5,4},{6,7},{7,6},{8,9},{9,8},{10,11... | collective-permute-start | bytes 983048 | tf_op jit(solution)/shard_map/ppermute | solution.py:334
  23.0 7.6 %collective-permute-start.5 = (f32[640,128]{1,0:T(8,128)S(1)}, f32[640,128]{1,0:T(8,128)S(1)}, u32[]{:S(2)}, u32[]{:S(2)}) collective-permute-start(f32[640,128]{1,0:T(8,128)S(1)} %collective-permute-done.4.refs_2_), channel_id=1, source_target_pairs={{8,0},{16,8},{24,16},{28,24},{20,28},{12,20},{4,12},{0,4},{9,1},{1... | collective-permute-start | bytes 983048 | tf_op jit(solution)/shard_map/ppermute | solution.py:327
  23.5 7.2 %collective-permute-start.2 = (f32[640,128]{1,0:T(8,128)S(1)}, f32[640,128]{1,0:T(8,128)S(1)}, u32[]{:S(2)}, u32[]{:S(2)}) collective-permute-start(f32[640,128]{1,0:T(8,128)S(1)} %collective-permute-done.1.refs_5_), channel_id=1, source_target_pairs={{0,8},{8,16},{16,24},{24,28},{28,20},{20,12},{12,4},{4,0},{1,9},{9... | collective-permute-start | bytes 983048 | tf_op jit(solution)/shard_map/ppermute | solution.py:326
  30.7 7.1 %collective-permute-start.11 = (f32[320,128]{1,0:T(8,128)S(1)}, f32[320,128]{1,0:T(8,128)S(1)}, u32[]{:S(2)}, u32[]{:S(2)}) collective-permute-start(f32[320,128]{1,0:T(8,128)S(1)} %get-tuple-element.102), channel_id=1, source_target_pairs={{8,0},{16,8},{24,16},{28,24},{20,28},{12,20},{4,12},{0,4},{9,1},{1... | collective-permute-start | bytes 491528 | tf_op jit(solution)/shard_map/ppermute | solution.py:348
  32.2 7.1 %collective-permute-start.9 = (f32[320,128]{1,0:T(8,128)S(1)}, f32[320,128]{1,0:T(8,128)S(1)}, u32[]{:S(2)}, u32[]{:S(2)}) collective-permute-start(f32[320,128]{1,0:T(8,128)S(1)} %get-tuple-element.100), channel_id=1, source_target_pairs={{0,8},{8,16},{16,24},{24,28},{28,20},{20,12},{12,4},{4,0},{1,9},{9... | collective-permute-start | bytes 491528 | tf_op jit(solution)/shard_map/ppermute | solution.py:348
  33.6 7.4 %collective-permute-start.13 = (f32[320,128]{1,0:T(8,128)S(1)}, f32[320,128]{1,0:T(8,128)S(1)}, u32[]{:S(2)}, u32[]{:S(2)}) collective-permute-start(f32[320,128]{1,0:T(8,128)S(1)} %get-tuple-element.108), channel_id=1, source_target_pairs={{0,8},{8,16},{16,24},{24,28},{28,20},{20,12},{12,4},{4,0},{1,9},{9... | collective-permute-start | bytes 491528 | tf_op jit(solution)/shard_map/ppermute | solution.py:348
  35.2 7.1 %collective-permute-start.14 = (f32[320,128]{1,0:T(8,128)S(1)}, f32[320,128]{1,0:T(8,128)S(1)}, u32[]{:S(2)}, u32[]{:S(2)}) collective-permute-start(f32[320,128]{1,0:T(8,128)S(1)} %get-tuple-element.109), channel_id=1, source_target_pairs={{8,0},{16,8},{24,16},{28,24},{20,28},{12,20},{4,12},{0,4},{9,1},{1... | collective-permute-start | bytes 491528 | tf_op jit(solution)/shard_map/ppermute | solution.py:348
  35.7 8.8 %collective-permute-start.17 = (f32[320,128]{1,0:T(8,128)S(1)}, f32[320,128]{1,0:T(8,128)S(1)}, u32[]{:S(2)}, u32[]{:S(2)}) collective-permute-start(f32[320,128]{1,0:T(8,128)S(1)} %slice.18), channel_id=1, source_target_pairs={{0,8},{8,16},{16,24},{24,28},{28,20},{20,12},{12,4},{4,0},{1,9},{9... | collective-permute-start | bytes 491528 | tf_op jit(solution)/shard_map/ppermute | solution.py:358
  37.8 8.5 %collective-permute-start.18 = (f32[320,128]{1,0:T(8,128)S(1)}, f32[320,128]{1,0:T(8,128)S(1)}, u32[]{:S(2)}, u32[]{:S(2)}) collective-permute-start(f32[320,128]{1,0:T(8,128)S(1)} %slice.19), channel_id=1, source_target_pairs={{8,0},{16,8},{24,16},{28,24},{20,28},{12,20},{4,12},{0,4},{9,1},{1... | collective-permute-start | bytes 491528 | tf_op jit(solution)/shard_map/ppermute | solution.py:358
  39.3 12.6 %collective-permute-start.12 = (f32[320,128]{1,0:T(8,128)S(1)}, f32[320,128]{1,0:T(8,128)S(1)}, u32[]{:S(2)}, u32[]{:S(2)}) collective-permute-start(f32[320,128]{1,0:T(8,128)S(1)} %add.40), channel_id=1, source_target_pairs={{8,0},{16,8},{24,16},{28,24},{20,28},{12,20},{4,12},{0,4},{9,1},{1... | collective-permute-start | bytes 491528 | tf_op jit(solution)/shard_map/ppermute | solution.py:348
  42.4 9.5 %collective-permute-start.16 = (f32[320,128]{1,0:T(8,128)S(1)}, f32[320,128]{1,0:T(8,128)S(1)}, u32[]{:S(2)}, u32[]{:S(2)}) collective-permute-start(f32[320,128]{1,0:T(8,128)S(1)} %add.42), channel_id=1, source_target_pairs={{8,0},{16,8},{24,16},{28,24},{20,28},{12,20},{4,12},{0,4},{9,1},{1... | collective-permute-start | bytes 491528 | tf_op jit(solution)/shard_map/ppermute | solution.py:348
  42.9 9.0 %collective-permute-start.15 = (f32[320,128]{1,0:T(8,128)S(1)}, f32[320,128]{1,0:T(8,128)S(1)}, u32[]{:S(2)}, u32[]{:S(2)}) collective-permute-start(f32[320,128]{1,0:T(8,128)S(1)} %add.41), channel_id=1, source_target_pairs={{0,8},{8,16},{16,24},{24,28},{28,20},{20,12},{12,4},{4,0},{1,9},{9... | collective-permute-start | bytes 491528 | tf_op jit(solution)/shard_map/ppermute | solution.py:348
  44.6 7.4 %collective-permute-start.10 = (f32[320,128]{1,0:T(8,128)S(1)}, f32[320,128]{1,0:T(8,128)S(1)}, u32[]{:S(2)}, u32[]{:S(2)}) collective-permute-start(f32[320,128]{1,0:T(8,128)S(1)} %add.39), channel_id=1, source_target_pairs={{0,8},{8,16},{16,24},{24,28},{28,20},{20,12},{12,4},{4,0},{1,9},{9... | collective-permute-start | bytes 491528 | tf_op jit(solution)/shard_map/ppermute | solution.py:348
  52.1 7.0 %collective-permute-start.22 = (f32[320,128]{1,0:T(8,128)S(1)}, f32[320,128]{1,0:T(8,128)S(1)}, u32[]{:S(2)}, u32[]{:S(2)}) collective-permute-start(f32[320,128]{1,0:T(8,128)S(1)} %add.44), channel_id=1, source_target_pairs={{8,0},{16,8},{24,16},{28,24},{20,28},{12,20},{4,12},{0,4},{9,1},{1... | collective-permute-start | bytes 491528 | tf_op jit(solution)/shard_map/ppermute | solution.py:348
  52.2 7.1 %collective-permute-start.21 = (f32[320,128]{1,0:T(8,128)S(1)}, f32[320,128]{1,0:T(8,128)S(1)}, u32[]{:S(2)}, u32[]{:S(2)}) collective-permute-start(f32[320,128]{1,0:T(8,128)S(1)} %add.43), channel_id=1, source_target_pairs={{0,8},{8,16},{16,24},{24,28},{28,20},{20,12},{12,4},{4,0},{1,9},{9... | collective-permute-start | bytes 491528 | tf_op jit(solution)/shard_map/ppermute | solution.py:348
  54.4 11.5 %collective-permute-start.26 = (f32[640,128]{1,0:T(8,128)S(1)}, f32[640,128]{1,0:T(8,128)S(1)}, u32[]{:S(2)}, u32[]{:S(2)}) collective-permute-start(f32[640,128]{1,0:T(8,128)S(1)} %get-tuple-element.140), channel_id=1, source_target_pairs={{0,2},{1,3},{2,0},{3,1},{4,6},{5,7},{6,4},{7,5},{8,10},{9,11},{10,... | collective-permute-start | bytes 983048 | tf_op jit(solution)/shard_map/ppermute | solution.py:384
  55.2 7.4 %collective-permute-start.20 = (f32[320,128]{1,0:T(8,128)S(1)}, f32[320,128]{1,0:T(8,128)S(1)}, u32[]{:S(2)}, u32[]{:S(2)}) collective-permute-start(f32[320,128]{1,0:T(8,128)S(1)} %add.46), channel_id=1, source_target_pairs={{8,0},{16,8},{24,16},{28,24},{20,28},{12,20},{4,12},{0,4},{9,1},{1... | collective-permute-start | bytes 491528 | tf_op jit(solution)/shard_map/ppermute | solution.py:348
  56.0 7.2 %collective-permute-start.19 = (f32[320,128]{1,0:T(8,128)S(1)}, f32[320,128]{1,0:T(8,128)S(1)}, u32[]{:S(2)}, u32[]{:S(2)}) collective-permute-start(f32[320,128]{1,0:T(8,128)S(1)} %add.45), channel_id=1, source_target_pairs={{0,8},{8,16},{16,24},{24,28},{28,20},{20,12},{12,4},{4,0},{1,9},{9... | collective-permute-start | bytes 491528 | tf_op jit(solution)/shard_map/ppermute | solution.py:348
  (3 other events, 15.4 us)
